TPU v7x, 128 devices: a whole 4x4x4 slice. The times are simulated.
128 devices in a mesh: section: 8 (over z, y_lo), fsdp: 16 (over y_hi, x, core).
Axes of the slice: x: 4, y: 4 (y_hi: 2, y_lo: 2; y = y_hi * 2 + y_lo), z: 4, core: 2. Of those that a mesh axis runs over, the one named last changes fastest.
Arguments:
- activations: bfloat16 [8, 512, 5120], P('section', 'fsdp'), may hold values from -0.625 to 0.625
- gate_preact: bfloat16 [8, 512, 14336], P('section', None, 'fsdp'), may hold values from -6 to 6
- hidden_grad: bfloat16 [8, 512, 14336], P('section', None, 'fsdp'), may hold values from -6 to 6
- up_weight: bfloat16 [8, 5120, 14336], P('section', None, 'fsdp'), may hold values from -0.046875 to 0.046875
- resid_grad: bfloat16 [8, 512, 5120], P('section', 'fsdp'), may hold values from -6 to 6
- feedback: float32 [8, 512, 5120], P('section', 'fsdp'), may hold values from -4 to 4
- start_basis: float32 [8, 5120, 64], P('section'), may hold values from -6 to 6
Outputs:
- up_grad: bfloat16 [8, 5120, 14336], P('section', None, 'fsdp')
- new_feedback: float32 [8, 512, 5120], P('section', 'fsdp')
- received: float32 [8, 512, 5120], P('section', 'fsdp')
All inputs are finite; a program needn't handle non-finite values.
Results may differ from a plain program's by a relative error of at most 0.005.
Values may be sent and summed in bfloat16 or wider, within the bound.
No kernel may reach another device: no remote copies, remote signals or barrier semaphores. Data moves between devices by JAX's collectives and lax.ppermute only.
A program may use at most 128 MiB of HBM per device.

v0:
```python
import jax
import jax.numpy as jnp
from jax import lax
from jax.sharding import PartitionSpec as P


def shifted(value, axis, steps):
    count = lax.axis_size(axis)
    leading, last = (max(0, -steps), min(count, count - steps))
    return lax.ppermute(value, axis, [(source, source + steps) for source in range(leading, last)])


def on_device(activations, gate_preact, hidden_grad, up_weight, resid_grad, feedback, start_basis):
    highest = lax.Precision.HIGHEST
    own_acts = activations[0]
    weight_local = up_weight[0]
    unit_grad = (
        hidden_grad[0].astype(jnp.float32) * jax.nn.silu(gate_preact[0].astype(jnp.float32))
    ).astype(jnp.bfloat16)
    input_grad = lax.psum_scatter(
        lax.dot_general(
            unit_grad, weight_local, (((1,), (1,)), ((), ())), preferred_element_type=jnp.float32
        ),
        "fsdp",
        scatter_dimension=0,
        tiled=True,
    )
    all_acts = lax.all_gather(own_acts, "fsdp", axis=0, tiled=True)
    weight_grad = lax.dot_general(
        all_acts, unit_grad, (((0,), (0,)), ((), ())), preferred_element_type=jnp.float32
    ).astype(jnp.bfloat16)
    merged = resid_grad[0].astype(jnp.float32) + feedback[0] + input_grad
    raw_left = jnp.dot(merged, start_basis[0], precision=highest)
    gram_local = jnp.dot(raw_left.T, raw_left, precision=highest)
    gram_total = lax.psum(gram_local, "fsdp")
    lower_factor = jnp.linalg.cholesky(gram_total)
    left_factor = lax.linalg.triangular_solve(
        lower_factor, raw_left, left_side=False, lower=True, transpose_a=True
    )
    right_factor = lax.psum(jnp.dot(merged.T, left_factor, precision=highest), "fsdp")
    approximation = jnp.dot(left_factor, right_factor.T, precision=highest)
    new_feedback = merged - approximation
    left_next, right_next = shifted((left_factor, right_factor), "section", -1)
    received = jnp.dot(left_next, right_next.T, precision=highest)
    return (weight_grad[None], new_feedback[None], received[None])


def solution(mesh):
    return jax.shard_map(
        on_device,
        mesh=mesh,
        in_specs=(
            P("section", "fsdp", None),
            P("section", None, "fsdp"),
            P("section", None, "fsdp"),
            P("section", None, "fsdp"),
            P("section", "fsdp", None),
            P("section", "fsdp", None),
            P("section", None, None),
        ),
        out_specs=(
            P("section", None, "fsdp"),
            P("section", "fsdp", None),
            P("section", "fsdp", None),
        ),
        check_vma=False,
    )
```

profile of v0, /device:TPU:96, one launch (start us, length us, event | category | flops | bytes accessed | tf_op | source)
XLA Modules:
  0.0 460.3 jit_solution(9795890983480770064)
XLA Ops:
  7.2 0.0 copy-start
  7.2 0.0 reduce-scatter.2.cloned.1.call-start
  7.2 11.2 %fusion = f32[512,5120]{1,0:T(8,128)} fusion(bf16[1,5120,896]{2,1,0:T(8,128)(2,1)} %param.10, bf16[1,512,896]{2,1,0:T(8,128)(2,1)} %param.9, bf16[1,512,896]{2,1,0:T(8,128)(2,1)} %param.8), kind=kOutput, calls=%fused_computation | convolution fusion | flops 4701290496 | bytes 21495808 | tf_op jit(solution)/shard_map/dot_general | solution.py:21
  18.5 0.0 copy-start.2
  18.5 0.0 copy-start.3
  18.5 0.0 reduce-scatter.2.cloned.1.call-update
  18.5 0.0 all-reduce.2.cloned.1.call-start
  18.6 113.5 %reduce-scatter.2.cloned.1.call-done = f32[32,5120]{1,0:T(8,128)} async-done(((f32[512,5120]{1,0:T(8,128)}), f32[32,5120]{1,0:T(8,128)}) %reduce-scatter.2.cloned.1.call-update) | async-done | bytes 655376 | tf_op jit(solution)/shard_map/reduce_scatter | solution.py:20
  132.0 0.0 copy-done.2
  132.0 0.0 copy-done.3
  132.0 1.2 bitcast_add_fusion
  133.2 0.0 copy-done
  133.2 1.2 fusion.15
  134.4 0.2 fusion.27
  134.6 65.2 %psum.14 = f32[64,64]{0,1:T(8,128)S(1)} all-reduce(f32[64,64]{0,1:T(8,128)S(1)} %fusion.27), channel_id=1, replica_groups=mesh['section'=8,'fsdp'=16] {'fsdp'}, use_global_device_ids=true, to_apply=%region_1.2 | all-reduce | flops 4096 | bytes 32768 | tf_op jit(solution)/shard_map/psum | solution.py:35
  199.8 0.1 copy.11
  199.9 5.8 %cholesky.16 = f32[64,64]{1,0:T(8,128)S(1)} custom-call(f32[64,64]{1,0:T(8,128)S(1)} %fusion.24), custom_call_target="Cholesky" | custom-call | tf_op jit(solution)/shard_map/jit(cholesky)/cholesky | solution.py:36
  205.8 0.6 compare_reduce_fusion
  206.4 0.7 fusion.21
  207.1 4.9 %custom-call.6 = f32[1,64,64]{1,2,0:T(8,128)S(1)} custom-call(f32[1,64,64]{2,1,0:T(8,128)S(1)} %fusion.21), custom_call_target="InvertDiagBlocksLowerTriangular" | custom-call | tf_op jit(solution)/shard_map/triangular_solve | solution.py:37
  212.0 0.0 copy-start.4
  212.0 0.1 fusion.22
  212.2 2.3 fusion.28
  214.4 0.0 all-reduce.2.cloned.1.call-update
  214.5 0.0 all-gather.3.cloned.1.call-start
  214.5 0.7 all-gather.3.cloned.1.call-update
  215.2 139.7 %all-reduce.2.cloned.1.call-done = f32[5120,64]{0,1:T(8,128)} async-done(((f32[5120,64]{0,1:T(8,128)}), f32[5120,64]{0,1:T(8,128)}) %all-reduce.2.cloned.1.call-update) | async-done | bytes 1310736 | tf_op jit(solution)/shard_map/psum | solution.py:40
  354.9 3.3 collective-permute-start.1
  358.2 62.8 %all-gather.3.cloned.1.call-done = bf16[1,512,5120]{2,1,0:T(8,128)(2,1)} async-done(((bf16[1,32,5120]{2,1,0:T(8,128)(2,1)}), bf16[1,512,5120]{2,1,0:T(8,128)(2,1)}) %all-gather.3.cloned.1.call-update) | async-done | bytes 5242896 | tf_op jit(solution)/shard_map/all_gather | solution.py:28
  421.0 0.0 copy-done.4
  421.0 11.4 %convert_bitcast_fusion = bf16[1,5120,896]{1,2,0:T(8,128)(2,1)} fusion(bf16[1,512,5120]{2,1,0:T(8,128)(2,1)} %all-gather.3.cloned.1.call-done, bf16[1,512,896]{2,1,0:T(8,128)(2,1)S(1)} %copy-done.4, bf16[1,512,896]{2,1,0:T(8,128)(2,1)} %param.8), kind=kOutput, calls=%fused_computation.2 | convolution fusion | flops 4705878016 | bytes 16252928 | tf_op jit(solution)/shard_map/dot_general | solution.py:29
  432.4 0.0 copy-start.1
  432.4 12.8 %copy.12 = bf16[1,5120,896]{2,1,0:T(8,128)(2,1)} copy(bf16[1,5120,896]{1,2,0:T(8,128)(2,1)} %convert_bitcast_fusion) | data formatting | bytes 18350080
  445.2 2.7 collective-permute-start
  447.9 0.0 copy-done.1
  447.9 1.6 fusion.2
  449.5 1.3 collective-permute-done
  450.8 0.0 collective-permute-done.1
  450.8 2.9 convolution_bitcast_fusion
  (2 shorter events, 0.0 us)
Async XLA Ops:
  7.2 126.0 %copy-start = (f32[1,5120,64]{1,2,0:T(8,128)S(1)}, f32[1,5120,64]{1,2,0:T(8,128)}, u32[]{:S(2)}) copy-start(f32[1,5120,64]{1,2,0:T(8,128)} %param.13) | copy-start | bytes 3932164
  7.2 124.9 %reduce-scatter.2.cloned.1.call-start = ((), (), s32[]{:S(2)}) async-start(), calls=%async_computation.1 | async-start | bytes 11141120 | tf_op jit(solution)/shard_map/reduce_scatter | solution.py:20
  18.5 113.6 %copy-start.2 = (f32[1,32,5120]{2,1,0:T(8,128)S(1)}, f32[1,32,5120]{2,1,0:T(8,128)}, u32[]{:S(2)}) copy-start(f32[1,32,5120]{2,1,0:T(8,128)} %param.12) | copy-start | bytes 1966084
  18.5 113.6 %copy-start.3 = (bf16[1,32,5120]{2,1,0:T(8,128)(2,1)S(1)}, bf16[1,32,5120]{2,1,0:T(8,128)(2,1)}, u32[]{:S(2)}) copy-start(bf16[1,32,5120]{2,1,0:T(8,128)(2,1)} %param.11) | copy-start | bytes 983044
  18.5 336.4 %all-reduce.2.cloned.1.call-start = ((), (), s32[]{:S(2)}) async-start(), calls=%async_computation.2 | async-start | bytes 2621440 | tf_op jit(solution)/shard_map/psum | solution.py:40
  212.0 209.0 %copy-start.4 = (bf16[1,512,896]{2,1,0:T(8,128)(2,1)S(1)}, bf16[1,512,896]{2,1,0:T(8,128)(2,1)}, u32[]{:S(2)}) copy-start(bf16[1,512,896]{2,1,0:T(8,128)(2,1)} %param.9) | copy-start | bytes 2752516
  214.5 206.5 %all-gather.3.cloned.1.call-start = ((), (), s32[]{:S(2)}) async-start(), calls=%async_computation.3 | async-start | bytes 5570560 | tf_op jit(solution)/shard_map/all_gather | solution.py:28
  354.9 95.9 %collective-permute-start.1 = (f32[5120,64]{0,1:T(8,128)}, f32[5120,64]{0,1:T(8,128)}, u32[]{:S(2)}, u32[]{:S(2)}) collective-permute-start(f32[5120,64]{0,1:T(8,128)} %all-reduce.2.cloned.1.call-done), channel_id=1, source_target_pairs={{16,0},{32,16},{48,32},{64,48},{80,64},{96,80},{112,96},{17,1},{33... | collective-permute-start | bytes 3932168 | tf_op jit(solution)/shard_map/ppermute | solution.py:10
  432.4 15.5 %copy-start.1 = (f32[5120,64]{0,1:T(8,128)S(1)}, f32[5120,64]{0,1:T(8,128)}, u32[]{:S(2)}) copy-start(f32[5120,64]{0,1:T(8,128)} %all-reduce.2.cloned.1.call-done) | copy-start | bytes 3932164
  445.2 5.6 %collective-permute-start = (f32[32,64]{1,0:T(8,128)S(1)}, f32[32,64]{1,0:T(8,128)S(1)}, u32[]{:S(2)}, u32[]{:S(2)}) collective-permute-start(f32[32,64]{1,0:T(8,128)S(1)} %fusion.22), channel_id=1, source_target_pairs={{16,0},{32,16},{48,32},{64,48},{80,64},{96,80},{112,96},{17,1},{33... | collective-permute-start | bytes 24584 | tf_op jit(solution)/shard_map/ppermute | solution.py:10
Sparse Core Ops, SparseCore 0:
  18.6 113.3 reduce-scatter.1
  214.6 140.2 all-reduce.1
  357.6 63.3 all-gather.2
where the time goes:
time: 462 us; the launch traced here: 460 us
  waiting for transfers between devices  318 us (69%)
  blocking collectives  65.2 us (14%)
  matrix products  30.9 us (7%)
  between operations  13.8 us (3%)
  other arithmetic  13.2 us (3%)
  local copies, waits for them, and re-layouts  12.9 us (3%)
  starting transfers between devices  6.06 us (1%)
    psum x1, waiting for transfers between devices, on_device(): lax.psum(jnp.dot(merged.T, left_factor, precision=highest), 'fsdp')  140 us
    reduce_scatter x1, waiting for transfers between devices, on_device(): lax.psum_scatter(lax.dot_general(unit_grad, weight_local, (((1,), (1,)),...  113 us
    psum x1, blocking collectives, on_device(): gram_total = lax.psum(gram_local, 'fsdp')  65.2 us
    all_gather x1, waiting for transfers between devices, on_device(): all_acts = lax.all_gather(own_acts, 'fsdp', axis=0, tiled=True)  62.8 us
    unnamed x11, local copies, waits for them, and re-layouts  12.8 us
    dot_general x1, matrix products, on_device(): lax.dot_general(all_acts, unit_grad, (((0,), (0,)), ((), ())), preferred_...  11.4 us
    dot_general x1, matrix products, on_device(): lax.dot_general(unit_grad, weight_local, (((1,), (1,)), ((), ())), prefer...  11.2 us
  transfers between devices with their start and end apart: 5, of which 4 were waited for; matrix products, arithmetic and copies ran while one was open for 6% of the time, Pallas kernels for 0%

commit v1 on v0

v1 whole, which is shorter than its diff:
```python
import jax
import jax.numpy as jnp
from jax import lax
from jax.experimental import pallas as pl
from jax.experimental.pallas import tpu as pltpu
from jax.sharding import PartitionSpec as P

D = 5120
F = 896
R = 64
T = 512
TILE = 640
STEPS = D // TILE
BF = jnp.bfloat16
F32 = jnp.float32
VMEM_LIMIT = 50 * 1024 * 1024


def params():
    return pltpu.CompilerParams(vmem_limit_bytes=VMEM_LIMIT)


def place():
    index = lax.axis_index("fsdp")
    y, x, core = index // 8, (index // 2) % 4, index % 2
    return index, y, x, core


def xor_x(x, mask):
    return x + mask - 2 * (x & mask)


def pieces(value, count):
    out = []
    for _ in range(count):
        part = value.astype(BF)
        out.append(part)
        value = value - part.astype(F32)
    return out


def nn(a, b):
    return lax.dot_general(a, b, (((1,), (0,)), ((), ())), preferred_element_type=F32)


def nt(a, b):
    return lax.dot_general(a, b, (((1,), (1,)), ((), ())), preferred_element_type=F32)


def tn(a, b):
    return lax.dot_general(a, b, (((0,), (0,)), ((), ())), preferred_element_type=F32)


def row_blocks(y, x, core):
    out = []
    for c in (1 - core, core):
        first, second = 1 + 2 * c, 3 - 2 * c
        for xx in (xor_x(x, 2), xor_x(x, first), xor_x(x, second), x):
            for yy in (1 - y, y):
                out.append(yy * 8 + xx * 2 + c)
    return out


def unit_kernel(gate, hidden, weight, basis, resid, feedback, unit, ordered, raw_t, wb, rb):
    step = pl.program_id(0)

    @pl.when(step == 0)
    def _():
        wb[...] = jnp.zeros_like(wb)
        rb[...] = jnp.zeros_like(rb)

    split = jnp.concatenate(pieces(basis[...], 3), axis=1)
    wb[...] += tn(split, weight[...])
    rows = jnp.concatenate(pieces(resid[...].astype(F32) + feedback[...], 3), axis=0)
    rb[...] += tn(split, rows.T)
    g = gate[...].astype(F32)
    unit[pl.ds(step * 64, 64), :] = (hidden[...].astype(F32) * (g / (1.0 + jnp.exp(-g)))).astype(BF)

    @pl.when(step == STEPS - 1)
    def _():
        index, y, x, core = place()
        for place_to, block in enumerate(row_blocks(y, x, core)):
            ordered[pl.ds(place_to * 32, 32), :] = unit[pl.ds(pl.multiple_of(block * 32, 32), 32), :]
        total = wb[0:R, :] + wb[R : 2 * R, :] + wb[2 * R : 3 * R, :]
        raw3 = nt(jnp.concatenate(pieces(total, 3), axis=0), unit[...])
        raw = raw3[0:R] + raw3[R : 2 * R] + raw3[2 * R : 3 * R]
        own = rb[0:R] + rb[R : 2 * R] + rb[2 * R : 3 * R]
        own = own[:, 0:32] + own[:, 32:64] + own[:, 64:96]
        spot = lax.broadcasted_iota(jnp.int32, (32, T), 1) - index * 32
        select = (spot == lax.broadcasted_iota(jnp.int32, (32, T), 0)).astype(BF)
        placed = nn(jnp.concatenate(pieces(own, 3), axis=0), select)
        raw_t[...] = raw + placed[0:R] + placed[R : 2 * R] + placed[2 * R : 3 * R]


def unit_call(gate, hidden, weight, basis, resid, feedback):
    return pl.pallas_call(
        unit_kernel,
        grid=(STEPS,),
        in_specs=[
            pl.BlockSpec((64, F), lambda i: (i, 0)),
            pl.BlockSpec((64, F), lambda i: (i, 0)),
            pl.BlockSpec((TILE, F), lambda i: (i, 0)),
            pl.BlockSpec((TILE, R), lambda i: (i, 0)),
            pl.BlockSpec((32, TILE), lambda i: (0, i)),
            pl.BlockSpec((32, TILE), lambda i: (0, i)),
        ],
        out_specs=[
            pl.BlockSpec((T, F), lambda i: (0, 0)),
            pl.BlockSpec((T, F), lambda i: (0, 0)),
            pl.BlockSpec((R, T), lambda i: (0, 0)),
        ],
        out_shape=[
            jax.ShapeDtypeStruct((T, F), BF),
            jax.ShapeDtypeStruct((T, F), BF),
            jax.ShapeDtypeStruct((R, T), F32),
        ],
        scratch_shapes=[pltpu.VMEM((3 * R, F), F32), pltpu.VMEM((3 * R, 96), F32)],
        compiler_params=params(),
        cost_estimate=pl.CostEstimate(flops=2 * D * F * 192, bytes_accessed=15_000_000, transcendentals=T * F),
        name="unit_and_raw",
    )(gate, hidden, weight, basis, resid, feedback)


def partial_kernel(unit, weight, first, second):
    product = nt(unit[...], weight[...])
    first[...] = product[0:128].astype(first.dtype)
    second[...] = product[128:256].astype(second.dtype)


def partial_call(ordered, half, weight, dtype, name):
    return pl.pallas_call(
        partial_kernel,
        grid=(STEPS,),
        in_specs=[
            pl.BlockSpec((256, F), lambda i: (half, 0)),
            pl.BlockSpec((TILE, F), lambda i: (i, 0)),
        ],
        out_specs=[pl.BlockSpec((128, TILE), lambda i: (0, i))] * 2,
        out_shape=[jax.ShapeDtypeStruct((128, D), dtype)] * 2,
        compiler_params=params(),
        cost_estimate=pl.CostEstimate(flops=2 * 256 * F * D, bytes_accessed=13_000_000, transcendentals=0),
        name=name,
    )(ordered, weight)


def eliminated(gram):
    rows = lax.broadcasted_iota(jnp.int32, (R, 2 * R), 0)
    lanes = lax.broadcasted_iota(jnp.int32, (R, 2 * R), 1)
    work = jnp.concatenate([gram, jnp.zeros((R, R), F32)], axis=1)
    work = jnp.where(lanes == rows + R, 1.0, work)
    scales = []
    for j in range(R):
        column = work[:, j : j + 1]
        pivot = column[j : j + 1, :]
        row = work[j : j + 1, :]
        scales.append(row * lax.rsqrt(pivot))
        work = work - jnp.where(rows[:, 0:1] > j, column, 0.0) * (row / pivot)
    return jnp.concatenate(scales, axis=0)[:, R:]


def exact(op, a, b):
    a1, a2, a3 = pieces(a, 3)
    b1, b2, b3 = pieces(b, 3)
    low = op(a1, b3) + op(a2, b2) + op(a3, b1)
    return op(a1, b1) + (op(a1, b2) + op(a2, b1) + low)


def factor_kernel(raw_a, raw_b, unit, weight, resid, feedback, own_out, other_out, left, z, left_t):
    step = pl.program_id(0)
    index, y, x, core = place()

    @pl.when(step == 0)
    def _():
        raw = raw_a[...] + raw_b[...]
        gram = exact(nt, raw, raw)
        inverse = eliminated(gram)
        basis = exact(nn, inverse, raw)
        parts = jnp.concatenate(pieces(basis, 3), axis=0)
        z3 = nn(parts, unit[...])
        z[...] = jnp.concatenate(pieces(z3[0:R] + z3[R : 2 * R] + z3[2 * R : 3 * R], 2), axis=0)
        spot = lax.broadcasted_iota(jnp.int32, (32, T), 1) - index * 32
        select = (spot == lax.broadcasted_iota(jnp.int32, (32, T), 0)).astype(BF)
        own3 = nt(select, parts)
        left[...] = own3[:, 0:R] + own3[:, R : 2 * R] + own3[:, 2 * R : 3 * R]
        own_t = nt(parts, select)
        left_t[...] = own_t[0:R] + own_t[R : 2 * R] + own_t[2 * R : 3 * R]

    both = nt(z[...], weight[...])
    value = both[0:R] + both[R : 2 * R]
    l1, l2 = pieces(left_t[...], 2)
    r1, r2 = pieces(resid[...].astype(F32) + feedback[...], 2)
    value = value + (nn(l1, r1) + (nn(l1, r2) + nn(l2, r1)))
    half = step // 4
    chunk = step % 4
    for c in (0, 1):
        first = 1 + 2 * c
        apart = xor_x(chunk, x)
        spot = jnp.where(apart == 0, 3, jnp.where(apart == 2, 0, jnp.where(apart == first, 1, 2)))

        @pl.when((half == c) & (core == c))
        def _():
            own_out[spot] = value

        @pl.when((half == c) & (core != c))
        def _():
            other_out[spot] = value.astype(BF)


def factor_call(raw_a, raw_b, unit, weight, resid, feedback):
    return pl.pallas_call(
        factor_kernel,
        grid=(STEPS,),
        in_specs=[
            pl.BlockSpec((R, T), lambda i: (0, 0)),
            pl.BlockSpec((R, T), lambda i: (0, 0)),
            pl.BlockSpec((T, F), lambda i: (0, 0)),
            pl.BlockSpec((TILE, F), lambda i: (i, 0)),
            pl.BlockSpec((32, TILE), lambda i: (0, i)),
            pl.BlockSpec((32, TILE), lambda i: (0, i)),
        ],
        out_specs=[
            pl.BlockSpec((4, R, TILE), lambda i: (0, 0, 0)),
            pl.BlockSpec((4, R, TILE), lambda i: (0, 0, 0)),
            pl.BlockSpec((32, R), lambda i: (0, 0)),
        ],
        out_shape=[
            jax.ShapeDtypeStruct((4, R, TILE), F32),
            jax.ShapeDtypeStruct((4, R, TILE), BF),
            jax.ShapeDtypeStruct((32, R), F32),
        ],
        scratch_shapes=[pltpu.VMEM((2 * R, F), BF), pltpu.VMEM((R, 32), F32)],
        compiler_params=params(),
        cost_estimate=pl.CostEstimate(flops=2 * D * F * 192, bytes_accessed=12_000_000, transcendentals=0),
        name="factor",
    )(raw_a, raw_b, unit, weight, resid, feedback)


def grad_kernel(*refs):
    unit, out = refs[8], refs[9]
    tokens = jnp.concatenate([ref[...] for ref in refs[:8]], axis=0)
    out[...] = tn(tokens, unit[...]).astype(BF)


def grad_call(pairs, ordered):
    return pl.pallas_call(
        grad_kernel,
        grid=(STEPS,),
        in_specs=[pl.BlockSpec((64, TILE), lambda i: (0, i))] * 8 + [pl.BlockSpec((T, F), lambda i: (0, 0))],
        out_specs=pl.BlockSpec((TILE, F), lambda i: (i, 0)),
        out_shape=jax.ShapeDtypeStruct((D, F), BF),
        compiler_params=params(),
        cost_estimate=pl.CostEstimate(flops=2 * D * F * T, bytes_accessed=16_000_000, transcendentals=0),
        name="weight_grad",
    )(*pairs, ordered)


def final_kernel(*refs):
    chunks, (left, left_next, resid, feedback, mine, partner, out, received) = refs[:8], refs[8:]
    _, _, x, core = place()
    l3 = jnp.concatenate(pieces(left[...], 2), axis=0)
    n3 = jnp.concatenate(pieces(left_next[...], 2), axis=0)
    for h in (0, 1):
        c = core if h == 0 else 1 - core
        first, second = 1 + 2 * c, 3 - 2 * c
        for k, xx in enumerate((xor_x(x, 2), xor_x(x, first), xor_x(x, second), x)):
            columns = pl.ds(pl.multiple_of((c * 4 + xx) * TILE, 128), TILE)
            chunk = chunks[h * 4 + k]
            here = nn(l3, chunk[0])
            there = nn(n3, chunk[1])
            merged = resid[:, columns].astype(F32) + feedback[:, columns]
            merged = merged + (mine[:, columns] + partner[:, columns].astype(F32))
            out[:, columns] = merged - (here[0:32] + here[32:64])
            received[:, columns] = there[0:32] + there[32:64]


def final_call(chunks, left, left_next, resid, feedback, mine, partner):
    vmem = pl.BlockSpec(memory_space=pltpu.VMEM)
    return pl.pallas_call(
        final_kernel,
        in_specs=[vmem] * 14,
        out_specs=[vmem, vmem],
        out_shape=[jax.ShapeDtypeStruct((32, D), F32)] * 2,
        compiler_params=params(),
        cost_estimate=pl.CostEstimate(flops=2 * 4 * 32 * R * D, bytes_accessed=5_000_000, transcendentals=0),
        name="feedback_and_received",
    )(*chunks, left, left_next, resid, feedback, mine, partner)


def sent(value, move):
    pairs = []
    for index in range(16):
        y, x, core = move(index // 8, (index // 2) % 4, index % 2)
        pairs.append((index, y * 8 + x * 2 + core))
    return lax.ppermute(value, "fsdp", pairs)


def to_core(value):
    return sent(value, lambda y, x, c: (y, x, 1 - c))


def to_first(value):
    return sent(value, lambda y, x, c: (y, x ^ (1 + 2 * c), c))


def to_second(value):
    return sent(value, lambda y, x, c: (y, x ^ (3 - 2 * c), c))


def to_y(value):
    return sent(value, lambda y, x, c: (1 - y, x, c))


def to_previous(value):
    return lax.ppermute(value, "section", [(s, s - 1) for s in range(1, 8)])


def on_device(activations, gate_preact, hidden_grad, up_weight, resid_grad, feedback, start_basis):
    acts, weight, resid, fb = activations[0], up_weight[0], resid_grad[0], feedback[0]

    pair = jnp.concatenate([to_y(acts), acts], axis=0)
    unit, ordered, raw = unit_call(gate_preact[0], hidden_grad[0], weight, start_basis[0], resid, fb)
    pair_first = to_first(pair)
    pair_second, pair_both = to_second(pair), to_second(pair_first)
    own_pairs = [pair_both, pair_first, pair_second, pair]
    other_pairs = [to_core(value) for value in own_pairs]

    raw = raw + to_core(raw)
    raw = raw + to_first(raw)
    raw = raw + to_second(raw)
    raw_far = to_y(raw)

    other_a, other_b = partial_call(ordered, 0, weight, BF, "input_grad_other")
    own_a, own_b = partial_call(ordered, 1, weight, F32, "input_grad_own")
    come_a, come_b = to_core(other_a), to_core(other_b)
    come_first = to_first((own_a + come_a.astype(F32)).astype(BF))
    kept = own_b + come_b.astype(F32) + come_first.astype(F32)
    come_second = to_second(kept[0:64].astype(BF))
    kept = kept[64:128] + come_second.astype(F32)
    mine, partner = kept[32:64], to_y(kept[0:32].astype(BF))

    own, other, left = factor_call(raw, raw_far, unit, weight, resid, fb)
    left_next = to_previous(left)
    come = to_core(other)
    come_first = to_first((own[0:2] + come[0:2].astype(F32)).astype(BF))
    kept = own[2:4] + come[2:4].astype(F32) + come_first.astype(F32)
    come_second = to_second(kept[0].astype(BF))
    half_sum = (kept[1] + come_second.astype(F32)).astype(BF)
    right = (half_sum.astype(F32) + to_y(half_sum).astype(F32)).astype(BF)
    both = jnp.stack([right, to_previous(right)])
    both_first = to_first(both)
    both_second, both_far = to_second(both), to_second(both_first)
    own_chunks = [both_far, both_first, both_second, both]
    chunks = own_chunks + [to_core(value) for value in own_chunks]

    weight_grad = grad_call(other_pairs + own_pairs, ordered)
    new_feedback, received = final_call(chunks, left, left_next, resid, fb, mine, partner)
    return (weight_grad[None], new_feedback[None], received[None])


def solution(mesh):
    return jax.shard_map(
        on_device,
        mesh=mesh,
        in_specs=(
            P("section", "fsdp", None),
            P("section", None, "fsdp"),
            P("section", None, "fsdp"),
            P("section", None, "fsdp"),
            P("section", "fsdp", None),
            P("section", "fsdp", None),
            P("section", None, None),
        ),
        out_specs=(
            P("section", None, "fsdp"),
            P("section", "fsdp", None),
            P("section", "fsdp", None),
        ),
        check_vma=False,
    )
```

time: 462 us -> 159 us (0.34)
  waiting for transfers between devices: 318 us -> 62 us
  blocking collectives: 65.2 us -> 0 us
  Pallas kernels: 0 us -> 55.2 us
  matrix products: 30.9 us -> 0 us
  starting transfers between devices: 6.06 us -> 33.8 us
  between operations: 13.8 us -> 0.93 us
  other arithmetic: 13.2 us -> 1.09 us
  local copies, waits for them, and re-layouts: 12.9 us -> 3.32 us
    psum x1 -> x0, waiting for transfers between devices: 140 us -> none  [on_device(): lax.psum(jnp.dot(merged.T, left_factor, precision=highest), 'fsdp')]
    reduce_scatter x1 -> x0, waiting for transfers between devices: 113 us -> none  [on_device(): lax.psum_scatter(lax.dot_general(unit_grad, weight_local, (((1,), (1,)),...]
    psum x1 -> x0, blocking collectives: 65.2 us -> none  [on_device(): gram_total = lax.psum(gram_local, 'fsdp')]
    all_gather x1 -> x0, waiting for transfers between devices: 62.8 us -> none  [on_device(): all_acts = lax.all_gather(own_acts, 'fsdp', axis=0, tiled=True)]
    ppermute x2 -> x30, waiting for transfers between devices: 1.33 us -> 62 us  [the longest x28 55.8 us: sent(): return lax.ppermute(value, 'fsdp', pairs)]
    pallas_call x0 -> x6, Pallas kernels: none -> 55.2 us  [the longest x2 18.3 us: partial_call(): pl.pallas_call(partial_kernel, grid=(STEPS,), in_specs=[pl.BlockSpec((256...]
    dot_general x7 -> x0, matrix products: 30.8 us -> none  [the longest x1 11.4 us: on_device(): lax.dot_general(all_acts, unit_grad, (((0,), (0,)), ((), ())), preferred_...]
    ppermute x2 -> x30, starting transfers between devices: 5.94 us -> 33.8 us  [the longest x28 28 us: sent(): return lax.ppermute(value, 'fsdp', pairs)]
  transfers between devices with their start and end apart: 5 -> 30, of which waited for: 4 -> 12; matrix products, arithmetic and copies ran while one was open for 6% -> 1% of each run, Pallas kernels for 0% -> 22%
where the time goes in v1:
time: 159 us; the launch traced here: 156 us
  waiting for transfers between devices  62 us (39%)
  Pallas kernels  55.2 us (35%)
  starting transfers between devices  33.8 us (21%)
  local copies, waits for them, and re-layouts  3.32 us (2%)
    ppermute x28, waiting for transfers between devices, sent(): return lax.ppermute(value, 'fsdp', pairs)  55.8 us
    ppermute x28, starting transfers between devices, sent(): return lax.ppermute(value, 'fsdp', pairs)  28 us
    pallas_call x2, Pallas kernels, partial_call(): pl.pallas_call(partial_kernel, grid=(STEPS,), in_specs=[pl.BlockSpec((256...  18.3 us
    pallas_call x1, Pallas kernels, factor_call(): pl.pallas_call(factor_kernel, grid=(STEPS,), in_specs=[pl.BlockSpec((R, T...  14.5 us
    pallas_call x1, Pallas kernels, grad_call(): pl.pallas_call(grad_kernel, grid=(STEPS,), in_specs=[pl.BlockSpec((64, TI...  10.5 us
    pallas_call x1, Pallas kernels, unit_call(): pl.pallas_call(unit_kernel, grid=(STEPS,), in_specs=[pl.BlockSpec((64, F)...  10.3 us
    ppermute x2, waiting for transfers between devices, to_previous(): return lax.ppermute(value, 'section', [(s, s - 1) for s in range(1, 8)])  6.18 us
    ppermute x2, starting transfers between devices, to_previous(): return lax.ppermute(value, 'section', [(s, s - 1) for s in range(1, 8)])  5.73 us
  transfers between devices with their start and end apart: 30, of which 12 were waited for; matrix products, arithmetic and copies ran while one was open for 1% of the time, Pallas kernels for 22%

profile of v1, /device:TPU:96, one launch (start us, length us, event | category | flops | bytes accessed | tf_op | source)
XLA Modules:
  0.0 156.3 jit_solution(7331598867318868168)
XLA Ops:
  0.7 3.1 %copy.10 = f32[1,5120,64]{2,1,0:T(8,128)} copy(f32[1,5120,64]{1,2,0:T(8,128)} %param.13) | data formatting | bytes 2621440 | tf_op args[6]
  3.8 10.3 %unit_and_raw.1 = (bf16[512,896]{1,0:T(8,128)(2,1)S(1)}, bf16[512,896]{1,0:T(8,128)(2,1)S(1)}, f32[64,512]{1,0:T(8,128)S(1)}) custom-call(bf16[512,896]{1,0:T(8,128)(2,1)S(1)} %bitcast.26, bf16[512,896]{1,0:T(8,128)(2,1)} %bitcast.32, bf16[5120,896]{1,0:T(8,128)(2,1)} %bitcast.27, f32[5120,64]{1,0:T(8,128)} %bitcast.31, bf16[32,5120]{1,0:T(8,128)(2,1)S(1)} %bitcast.23, ...), custom_call_target="tpu_custom_call" | custom-call | flops 1761607680 | bytes 15000000 | tf_op jit(solution)/shard_map/unit_and_raw/pallas_call | solution.py:96
  14.1 8.8 %input_grad_other.1 = (bf16[128,5120]{1,0:T(8,128)(2,1)S(1)}, bf16[128,5120]{1,0:T(8,128)(2,1)S(1)}) custom-call(bf16[512,896]{1,0:T(8,128)(2,1)S(1)} %get-tuple-element.15.refs_8_.unit, bf16[5120,896]{1,0:T(8,128)(2,1)} %bitcast.28), custom_call_target="tpu_custom_call" | custom-call | flops 2348810240 | bytes 13000000 | tf_op jit(solution)/shard_map/input_grad_other/pallas_call | solution.py:131
  22.9 0.1 collective-permute-start.26
  23.0 0.5 collective-permute-start.8
  23.5 2.7 %collective-permute-done.8 = f32[64,512]{1,0:T(8,128)S(1)} collective-permute-done((f32[64,512]{1,0:T(8,128)S(1)}, f32[64,512]{1,0:T(8,128)S(1)}, u32[]{:S(2)}, u32[]{:S(2)}) %collective-permute-start.8) | collective-permute-done | bytes 131104 | tf_op jit(solution)/shard_map/ppermute | solution.py:294
  26.2 1.6 %collective-permute-start.9 = (f32[64,512]{1,0:T(8,128)S(1)}, f32[64,512]{1,0:T(8,128)S(1)}, u32[]{:S(2)}, u32[]{:S(2)}) collective-permute-start(f32[64,512]{1,0:T(8,128)S(1)} %add.36), channel_id=1, source_target_pairs={{0,2},{1,7},{2,0},{3,5},{4,6},{5,3},{6,4},{7,1},{8,10},{9,15},{10,... | collective-permute-start | bytes 393224 | tf_op jit(solution)/shard_map/ppermute | solution.py:294
  27.8 3.5 %collective-permute-done.9 = f32[64,512]{1,0:T(8,128)S(1)} collective-permute-done((f32[64,512]{1,0:T(8,128)S(1)}, f32[64,512]{1,0:T(8,128)S(1)}, u32[]{:S(2)}, u32[]{:S(2)}) %collective-permute-start.9) | collective-permute-done | bytes 131104 | tf_op jit(solution)/shard_map/ppermute | solution.py:294
  31.3 2.8 %collective-permute-start.10 = (f32[64,512]{1,0:T(8,128)S(1)}, f32[64,512]{1,0:T(8,128)S(1)}, u32[]{:S(2)}, u32[]{:S(2)}) collective-permute-start(f32[64,512]{1,0:T(8,128)S(1)} %add.37), channel_id=1, source_target_pairs={{0,6},{1,3},{2,4},{3,1},{4,2},{5,7},{6,0},{7,5},{8,14},{9,11},{10,... | collective-permute-start | bytes 393224 | tf_op jit(solution)/shard_map/ppermute | solution.py:294
  34.1 3.4 %collective-permute-done.10 = f32[64,512]{1,0:T(8,128)S(1)} collective-permute-done((f32[64,512]{1,0:T(8,128)S(1)}, f32[64,512]{1,0:T(8,128)S(1)}, u32[]{:S(2)}, u32[]{:S(2)}) %collective-permute-start.10) | collective-permute-done | bytes 131104 | tf_op jit(solution)/shard_map/ppermute | solution.py:294
  37.6 3.3 %collective-permute-start.11 = (f32[64,512]{1,0:T(8,128)S(1)}, f32[64,512]{1,0:T(8,128)S(1)}, u32[]{:S(2)}, u32[]{:S(2)}) collective-permute-start(f32[64,512]{1,0:T(8,128)S(1)} %add.38.raw_a), channel_id=1, source_target_pairs={{0,8},{1,9},{2,10},{3,11},{4,12},{5,13},{6,14},{7,15},{8,0},{9,1},... | collective-permute-start | bytes 393224 | tf_op jit(solution)/shard_map/ppermute | solution.py:294
  40.8 3.3 %collective-permute-done.11.raw_b = f32[64,512]{1,0:T(8,128)S(1)} collective-permute-done((f32[64,512]{1,0:T(8,128)S(1)}, f32[64,512]{1,0:T(8,128)S(1)}, u32[]{:S(2)}, u32[]{:S(2)}) %collective-permute-start.11) | collective-permute-done | bytes 131104 | tf_op jit(solution)/shard_map/ppermute | solution.py:294
  44.1 14.5 %factor.1 = (f32[4,64,640]{2,1,0:T(8,128)S(1)}, bf16[4,64,640]{2,1,0:T(8,128)(2,1)S(1)}, f32[32,64]{1,0:T(8,128)S(1)}) custom-call(f32[64,512]{1,0:T(8,128)S(1)} %add.38.raw_a, f32[64,512]{1,0:T(8,128)S(1)} %collective-permute-done.11.raw_b, bf16[512,896]{1,0:T(8,128)(2,1)S(1)} %get-tuple-element.17.unit, bf16[5120,896]{1,0:T(8,128)(2,1)} %bitcast.29, ...), custom_call_target="tpu_custom_call" | custom-call | flops 1761607680 | bytes 12000000 | tf_op jit(solution)/shard_map/factor/pallas_call | solution.py:210
  58.6 0.1 collective-permute-start.12
  58.7 0.5 collective-permute-start.25
  59.2 3.2 %collective-permute-start = (bf16[32,5120]{1,0:T(8,128)(2,1)S(1)}, bf16[32,5120]{1,0:T(8,128)(2,1)S(1)}, u32[]{:S(2)}, u32[]{:S(2)}) collective-permute-start(bf16[32,5120]{1,0:T(8,128)(2,1)S(1)} %bitcast.33), channel_id=1, source_target_pairs={{0,8},{1,9},{2,10},{3,11},{4,12},{5,13},{6,14},{7,15},{8,0},{9,1},... | collective-permute-start | bytes 983048 | tf_op jit(solution)/shard_map/ppermute | solution.py:294
  62.4 9.5 %input_grad_own.1 = (f32[128,5120]{1,0:T(8,128)S(1)}, f32[128,5120]{1,0:T(8,128)}) custom-call(bf16[512,896]{1,0:T(8,128)(2,1)S(1)} %get-tuple-element.15.refs_8_.unit, bf16[5120,896]{1,0:T(8,128)(2,1)} %bitcast.30), custom_call_target="tpu_custom_call" | custom-call | flops 2348810240 | bytes 13000000 | tf_op jit(solution)/shard_map/input_grad_own/pallas_call | solution.py:131
  71.9 0.4 collective-permute-start.13
  72.3 0.3 add_convert_fusion
  72.6 0.0 copy-start.4
  72.6 1.8 %collective-permute-start.27 = (bf16[128,5120]{1,0:T(8,128)(2,1)S(1)}, bf16[128,5120]{1,0:T(8,128)(2,1)S(1)}, u32[]{:S(2)}, u32[]{:S(2)}) collective-permute-start(bf16[128,5120]{1,0:T(8,128)(2,1)S(1)} %add_convert_fusion), channel_id=1, source_target_pairs={{0,2},{1,7},{2,0},{3,5},{4,6},{5,3},{6,4},{7,1},{8,10},{9,15},{10,... | collective-permute-start | bytes 3932168 | tf_op jit(solution)/shard_map/ppermute | solution.py:294
  74.5 0.0 copy-start.5
  74.5 0.4 collective-permute-start.1
  74.8 2.5 %collective-permute-done.13 = bf16[2,64,640]{2,1,0:T(8,128)(2,1)S(1)} collective-permute-done((bf16[2,64,640]{2,1,0:T(8,128)(2,1)S(1)}, bf16[2,64,640]{2,1,0:T(8,128)(2,1)S(1)}, u32[]{:S(2)}, u32[]{:S(2)}) %collective-permute-start.13) | collective-permute-done | bytes 163872 | tf_op jit(solution)/shard_map/ppermute | solution.py:294
  77.4 2.8 %collective-permute-start.14 = (bf16[64,640]{1,0:T(8,128)(2,1)S(1)}, bf16[64,640]{1,0:T(8,128)(2,1)S(1)}, u32[]{:S(2)}, u32[]{:S(2)}) collective-permute-start(bf16[64,640]{1,0:T(8,128)(2,1)S(1)} %fusion.2), channel_id=1, source_target_pairs={{0,6},{1,3},{2,4},{3,1},{4,2},{5,7},{6,0},{7,5},{8,14},{9,11},{10,... | collective-permute-start | bytes 245768 | tf_op jit(solution)/shard_map/ppermute | solution.py:294
  80.3 0.5 collective-permute-start.5
  80.7 25.6 %collective-permute-done.1.refs_5_ = bf16[64,5120]{1,0:T(8,128)(2,1)S(1)} collective-permute-done((bf16[64,5120]{1,0:T(8,128)(2,1)S(1)}, bf16[64,5120]{1,0:T(8,128)(2,1)S(1)}, u32[]{:S(2)}, u32[]{:S(2)}) %collective-permute-start.1) | collective-permute-done | bytes 655392 | tf_op jit(solution)/shard_map/ppermute | solution.py:294
  106.3 1.0 collective-permute-start.7
  107.3 0.0 collective-permute-done.14
  107.3 1.8 %collective-permute-start.2 = (bf16[64,5120]{1,0:T(8,128)(2,1)S(1)}, bf16[64,5120]{1,0:T(8,128)(2,1)S(1)}, u32[]{:S(2)}, u32[]{:S(2)}) collective-permute-start(bf16[64,5120]{1,0:T(8,128)(2,1)S(1)} %collective-permute-done.1.refs_5_), channel_id=1, source_target_pairs={{0,6},{1,3},{2,4},{3,1},{4,2},{5,7},{6,0},{7,5},{8,14},{9,11},{10,... | collective-permute-start | bytes 1966088 | tf_op jit(solution)/shard_map/ppermute | solution.py:294
  109.1 0.0 collective-permute-done.25
  109.1 0.4 collective-permute-start.15
  109.5 0.0 collective-permute-done.27
  109.5 0.5 convert_add_fusion
  110.0 0.1 slice.66
  110.1 1.5 collective-permute-start.28
  111.6 3.5 %collective-permute-done.15 = bf16[64,640]{1,0:T(8,128)(2,1)S(1)} collective-permute-done((bf16[64,640]{1,0:T(8,128)(2,1)S(1)}, bf16[64,640]{1,0:T(8,128)(2,1)S(1)}, u32[]{:S(2)}, u32[]{:S(2)}) %collective-permute-start.15) | collective-permute-done | bytes 81952 | tf_op jit(solution)/shard_map/ppermute | solution.py:294
  115.2 2.4 %collective-permute-start.16 = (bf16[64,640]{1,0:T(8,128)(2,1)S(1)}, bf16[64,640]{1,0:T(8,128)(2,1)S(1)}, u32[]{:S(2)}, u32[]{:S(2)}) collective-permute-start(bf16[64,640]{1,0:T(8,128)(2,1)S(1)} %add_convert_fusion.2), channel_id=1, source_target_pairs={{16,0},{32,16},{48,32},{64,48},{80,64},{96,80},{112,96},{17,1},{33... | collective-permute-start | bytes 245768 | tf_op jit(solution)/shard_map/ppermute | solution.py:314
  117.6 3.9 %collective-permute-done.16 = bf16[64,640]{1,0:T(8,128)(2,1)S(1)} collective-permute-done((bf16[64,640]{1,0:T(8,128)(2,1)S(1)}, bf16[64,640]{1,0:T(8,128)(2,1)S(1)}, u32[]{:S(2)}, u32[]{:S(2)}) %collective-permute-start.16) | collective-permute-done | bytes 81952 | tf_op jit(solution)/shard_map/ppermute | solution.py:314
  121.5 3.3 %collective-permute-start.24 = (f32[32,64]{1,0:T(8,128)S(1)}, f32[32,64]{1,0:T(8,128)S(1)}, u32[]{:S(2)}, u32[]{:S(2)}) collective-permute-start(f32[32,64]{1,0:T(8,128)S(1)} %get-tuple-element.20.refs_8_), channel_id=1, source_target_pairs={{16,0},{32,16},{48,32},{64,48},{80,64},{96,80},{112,96},{17,1},{33... | collective-permute-start | bytes 24584 | tf_op jit(solution)/shard_map/ppermute | solution.py:314
  124.8 2.3 %collective-permute-done.24.refs_9_ = f32[32,64]{1,0:T(8,128)S(1)} collective-permute-done((f32[32,64]{1,0:T(8,128)S(1)}, f32[32,64]{1,0:T(8,128)S(1)}, u32[]{:S(2)}, u32[]{:S(2)}) %collective-permute-start.24) | collective-permute-done | bytes 8224 | tf_op jit(solution)/shard_map/ppermute | solution.py:314
  127.1 0.0 collective-permute-start.17
  127.1 0.0 collective-permute-done.5.refs_6_
  127.1 0.1 collective-permute-start.4
  127.2 0.0 collective-permute-done.7.refs_3_
  127.2 0.5 collective-permute-start.6
  127.7 6.5 %collective-permute-done.17.refs_1_ = bf16[2,64,640]{2,1,0:T(8,128)(2,1)S(1)} collective-permute-done((bf16[2,64,640]{2,1,0:T(8,128)(2,1)S(1)}, bf16[2,64,640]{2,1,0:T(8,128)(2,1)S(1)}, u32[]{:S(2)}, u32[]{:S(2)}) %collective-permute-start.17) | collective-permute-done | bytes 163872 | tf_op jit(solution)/shard_map/ppermute | solution.py:294
  134.2 0.5 collective-permute-start.19
  134.7 2.7 %collective-permute-start.18 = (bf16[2,64,640]{2,1,0:T(8,128)(2,1)S(1)}, bf16[2,64,640]{2,1,0:T(8,128)(2,1)S(1)}, u32[]{:S(2)}, u32[]{:S(2)}) collective-permute-start(bf16[2,64,640]{2,1,0:T(8,128)(2,1)S(1)} %collective-permute-done.17.refs_1_), channel_id=1, source_target_pairs={{0,6},{1,3},{2,4},{3,1},{4,2},{5,7},{6,0},{7,5},{8,14},{9,11},{10,... | collective-permute-start | bytes 491528 | tf_op jit(solution)/shard_map/ppermute | solution.py:294
  137.4 0.0 collective-permute-done.28
  137.4 0.0 collective-permute-start.3
  137.4 0.1 slice_add_fusion
  137.6 3.1 %collective-permute-done.19.refs_2_ = bf16[2,64,640]{2,1,0:T(8,128)(2,1)S(1)} collective-permute-done((bf16[2,64,640]{2,1,0:T(8,128)(2,1)S(1)}, bf16[2,64,640]{2,1,0:T(8,128)(2,1)S(1)}, u32[]{:S(2)}, u32[]{:S(2)}) %collective-permute-start.19) | collective-permute-done | bytes 163872 | tf_op jit(solution)/shard_map/ppermute | solution.py:294
  140.7 0.0 collective-permute-start.23
  140.7 1.8 %collective-permute-done.18.refs_0_ = bf16[2,64,640]{2,1,0:T(8,128)(2,1)S(1)} collective-permute-done((bf16[2,64,640]{2,1,0:T(8,128)(2,1)S(1)}, bf16[2,64,640]{2,1,0:T(8,128)(2,1)S(1)}, u32[]{:S(2)}, u32[]{:S(2)}) %collective-permute-start.18) | collective-permute-done | bytes 163872 | tf_op jit(solution)/shard_map/ppermute | solution.py:294
  142.5 0.0 collective-permute-start.21
  142.5 0.5 collective-permute-start.22
  143.0 0.1 collective-permute-start.20
  143.1 1.0 collective-permute-start.29
  144.1 10.5 %weight_grad.1 = bf16[5120,896]{1,0:T(8,128)(2,1)} custom-call(bf16[64,5120]{1,0:T(8,128)(2,1)S(1)} %collective-permute-done.3.refs_0_, bf16[64,5120]{1,0:T(8,128)(2,1)S(1)} %collective-permute-done.4.refs_1_, bf16[64,5120]{1,0:T(8,128)(2,1)S(1)} %collective-permute-done.6.refs_2_, bf16[64,5120]{1,0:T(8,128)(2,1)S(1)} %collective-permute-done.7.refs_3_, ...), custom_call_target="tpu_custom_call" | custom-call | flops 4697620480 | bytes 16000000 | tf_op jit(solution)/shard_map/weight_grad/pallas_call | solution.py:245
  154.6 0.0 collective-permute-done.23.refs_7_
  154.7 0.0 collective-permute-done.22.refs_6_
  154.7 0.0 collective-permute-done.20.refs_4_
  154.7 1.6 %feedback_and_received.1 = (f32[32,5120]{1,0:T(8,128)}, f32[32,5120]{1,0:T(8,128)}) custom-call(bf16[2,64,640]{2,1,0:T(8,128)(2,1)S(1)} %collective-permute-done.18.refs_0_, bf16[2,64,640]{2,1,0:T(8,128)(2,1)S(1)} %collective-permute-done.17.refs_1_, bf16[2,64,640]{2,1,0:T(8,128)(2,1)S(1)} %collective-permute-done.19.refs_2_, ...), custom_call_target="tpu_custom_call" | custom-call | flops 83886080 | bytes 5000000 | tf_op jit(solution)/shard_map/feedback_and_received/pallas_call | solution.py:278
  (35 shorter events, 0.4 us)
Async XLA Ops:
  0.6 3.2 %copy-start.2 = (bf16[1,32,5120]{2,1,0:T(8,128)(2,1)S(1)}, bf16[1,32,5120]{2,1,0:T(8,128)(2,1)}, u32[]{:S(2)}) copy-start(bf16[1,32,5120]{2,1,0:T(8,128)(2,1)} %param.11) | copy-start | bytes 983044
  0.6 3.1 %copy-start = (f32[1,32,5120]{2,1,0:T(8,128)S(1)}, f32[1,32,5120]{2,1,0:T(8,128)}, u32[]{:S(2)}) copy-start(f32[1,32,5120]{2,1,0:T(8,128)} %param.12) | copy-start | bytes 1966084
  0.7 3.1 %copy-start.3 = (bf16[1,512,896]{2,1,0:T(8,128)(2,1)S(1)}, bf16[1,512,896]{2,1,0:T(8,128)(2,1)}, u32[]{:S(2)}) copy-start(bf16[1,512,896]{2,1,0:T(8,128)(2,1)} %param.8) | copy-start | bytes 2752516
  14.1 48.4 %copy-start.1 = (bf16[512,896]{1,0:T(8,128)(2,1)}, bf16[512,896]{1,0:T(8,128)(2,1)S(1)}, u32[]{:S(2)}) copy-start(bf16[512,896]{1,0:T(8,128)(2,1)S(1)} %get-tuple-element.15.refs_8_.unit) | copy-start | bytes 2752516
  22.9 49.4 %collective-permute-start.26 = (bf16[128,5120]{1,0:T(8,128)(2,1)S(1)}, bf16[128,5120]{1,0:T(8,128)(2,1)S(1)}, u32[]{:S(2)}, u32[]{:S(2)}) collective-permute-start(bf16[128,5120]{1,0:T(8,128)(2,1)S(1)} %get-tuple-element.24), channel_id=1, source_target_pairs={{0,1},{1,0},{2,3},{3,2},{4,5},{5,4},{6,7},{7,6},{8,9},{9,8},{10,11... | collective-permute-start | bytes 3932168 | tf_op jit(solution)/shard_map/ppermute | solution.py:294
  23.0 3.2 %collective-permute-start.8 = (f32[64,512]{1,0:T(8,128)S(1)}, f32[64,512]{1,0:T(8,128)S(1)}, u32[]{:S(2)}, u32[]{:S(2)}) collective-permute-start(f32[64,512]{1,0:T(8,128)S(1)} %get-tuple-element.16), channel_id=1, source_target_pairs={{0,1},{1,0},{2,3},{3,2},{4,5},{5,4},{6,7},{7,6},{8,9},{9,8},{10,11... | collective-permute-start | bytes 393224 | tf_op jit(solution)/shard_map/ppermute | solution.py:294
  26.2 5.0 %collective-permute-start.9 = (f32[64,512]{1,0:T(8,128)S(1)}, f32[64,512]{1,0:T(8,128)S(1)}, u32[]{:S(2)}, u32[]{:S(2)}) collective-permute-start(f32[64,512]{1,0:T(8,128)S(1)} %add.36), channel_id=1, source_target_pairs={{0,2},{1,7},{2,0},{3,5},{4,6},{5,3},{6,4},{7,1},{8,10},{9,15},{10,... | collective-permute-start | bytes 393224 | tf_op jit(solution)/shard_map/ppermute | solution.py:294
  31.3 6.3 %collective-permute-start.10 = (f32[64,512]{1,0:T(8,128)S(1)}, f32[64,512]{1,0:T(8,128)S(1)}, u32[]{:S(2)}, u32[]{:S(2)}) collective-permute-start(f32[64,512]{1,0:T(8,128)S(1)} %add.37), channel_id=1, source_target_pairs={{0,6},{1,3},{2,4},{3,1},{4,2},{5,7},{6,0},{7,5},{8,14},{9,11},{10,... | collective-permute-start | bytes 393224 | tf_op jit(solution)/shard_map/ppermute | solution.py:294
  37.6 6.6 %collective-permute-start.11 = (f32[64,512]{1,0:T(8,128)S(1)}, f32[64,512]{1,0:T(8,128)S(1)}, u32[]{:S(2)}, u32[]{:S(2)}) collective-permute-start(f32[64,512]{1,0:T(8,128)S(1)} %add.38.raw_a), channel_id=1, source_target_pairs={{0,8},{1,9},{2,10},{3,11},{4,12},{5,13},{6,14},{7,15},{8,0},{9,1},... | collective-permute-start | bytes 393224 | tf_op jit(solution)/shard_map/ppermute | solution.py:294
  44.1 15.1 %copy-start.6 = (bf16[1,32,5120]{2,1,0:T(8,128)(2,1)S(1)}, bf16[1,32,5120]{2,1,0:T(8,128)(2,1)}, u32[]{:S(2)}) copy-start(bf16[1,32,5120]{2,1,0:T(8,128)(2,1)} %param.7) | copy-start | bytes 983044
  58.6 13.3 %collective-permute-start.12 = (bf16[4,64,640]{2,1,0:T(8,128)(2,1)S(1)}, bf16[4,64,640]{2,1,0:T(8,128)(2,1)S(1)}, u32[]{:S(2)}, u32[]{:S(2)}) collective-permute-start(bf16[4,64,640]{2,1,0:T(8,128)(2,1)S(1)} %get-tuple-element.19), channel_id=1, source_target_pairs={{0,1},{1,0},{2,3},{3,2},{4,5},{5,4},{6,7},{7,6},{8,9},{9,8},{10,11... | collective-permute-start | bytes 983048 | tf_op jit(solution)/shard_map/ppermute | solution.py:294
  58.7 50.4 %collective-permute-start.25 = (bf16[128,5120]{1,0:T(8,128)(2,1)S(1)}, bf16[128,5120]{1,0:T(8,128)(2,1)S(1)}, u32[]{:S(2)}, u32[]{:S(2)}) collective-permute-start(bf16[128,5120]{1,0:T(8,128)(2,1)S(1)} %get-tuple-element.22), channel_id=1, source_target_pairs={{0,1},{1,0},{2,3},{3,2},{4,5},{5,4},{6,7},{7,6},{8,9},{9,8},{10,11... | collective-permute-start | bytes 3932168 | tf_op jit(solution)/shard_map/ppermute | solution.py:294
  59.2 15.2 %collective-permute-start = (bf16[32,5120]{1,0:T(8,128)(2,1)S(1)}, bf16[32,5120]{1,0:T(8,128)(2,1)S(1)}, u32[]{:S(2)}, u32[]{:S(2)}) collective-permute-start(bf16[32,5120]{1,0:T(8,128)(2,1)S(1)} %bitcast.33), channel_id=1, source_target_pairs={{0,8},{1,9},{2,10},{3,11},{4,12},{5,13},{6,14},{7,15},{8,0},{9,1},... | collective-permute-start | bytes 983048 | tf_op jit(solution)/shard_map/ppermute | solution.py:294
  71.9 5.4 %collective-permute-start.13 = (bf16[2,64,640]{2,1,0:T(8,128)(2,1)S(1)}, bf16[2,64,640]{2,1,0:T(8,128)(2,1)S(1)}, u32[]{:S(2)}, u32[]{:S(2)}) collective-permute-start(bf16[2,64,640]{2,1,0:T(8,128)(2,1)S(1)} %add_convert_fusion.1), channel_id=1, source_target_pairs={{0,2},{1,7},{2,0},{3,5},{4,6},{5,3},{6,4},{7,1},{8,10},{9,15},{10,... | collective-permute-start | bytes 491528 | tf_op jit(solution)/shard_map/ppermute | solution.py:294
  72.6 36.9 %copy-start.4 = (f32[128,5120]{1,0:T(8,128)S(1)}, f32[128,5120]{1,0:T(8,128)}, u32[]{:S(2)}) copy-start(f32[128,5120]{1,0:T(8,128)} %get-tuple-element.21) | copy-start | bytes 7864324
  72.6 36.9 %collective-permute-start.27 = (bf16[128,5120]{1,0:T(8,128)(2,1)S(1)}, bf16[128,5120]{1,0:T(8,128)(2,1)S(1)}, u32[]{:S(2)}, u32[]{:S(2)}) collective-permute-start(bf16[128,5120]{1,0:T(8,128)(2,1)S(1)} %add_convert_fusion), channel_id=1, source_target_pairs={{0,2},{1,7},{2,0},{3,5},{4,6},{5,3},{6,4},{7,1},{8,10},{9,15},{10,... | collective-permute-start | bytes 3932168 | tf_op jit(solution)/shard_map/ppermute | solution.py:294
  74.5 35.6 %copy-start.5 = (bf16[64,5120]{1,0:T(8,128)(2,1)}, bf16[64,5120]{1,0:T(8,128)(2,1)S(1)}, u32[]{:S(2)}) copy-start(bf16[64,5120]{1,0:T(8,128)(2,1)S(1)} %pad_maximum_fusion.refs_7_) | copy-start | bytes 1966084
  74.5 31.8 %collective-permute-start.1 = (bf16[64,5120]{1,0:T(8,128)(2,1)S(1)}, bf16[64,5120]{1,0:T(8,128)(2,1)S(1)}, u32[]{:S(2)}, u32[]{:S(2)}) collective-permute-start(bf16[64,5120]{1,0:T(8,128)(2,1)S(1)} %pad_maximum_fusion.refs_7_), channel_id=1, source_target_pairs={{0,2},{1,7},{2,0},{3,5},{4,6},{5,3},{6,4},{7,1},{8,10},{9,15},{10,... | collective-permute-start | bytes 1966088 | tf_op jit(solution)/shard_map/ppermute | solution.py:294
  77.4 29.9 %collective-permute-start.14 = (bf16[64,640]{1,0:T(8,128)(2,1)S(1)}, bf16[64,640]{1,0:T(8,128)(2,1)S(1)}, u32[]{:S(2)}, u32[]{:S(2)}) collective-permute-start(bf16[64,640]{1,0:T(8,128)(2,1)S(1)} %fusion.2), channel_id=1, source_target_pairs={{0,6},{1,3},{2,4},{3,1},{4,2},{5,7},{6,0},{7,5},{8,14},{9,11},{10,... | collective-permute-start | bytes 245768 | tf_op jit(solution)/shard_map/ppermute | solution.py:294
  80.3 46.9 %collective-permute-start.5 = (bf16[64,5120]{1,0:T(8,128)(2,1)S(1)}, bf16[64,5120]{1,0:T(8,128)(2,1)S(1)}, u32[]{:S(2)}, u32[]{:S(2)}) collective-permute-start(bf16[64,5120]{1,0:T(8,128)(2,1)S(1)} %pad_maximum_fusion.refs_7_), channel_id=1, source_target_pairs={{0,6},{1,3},{2,4},{3,1},{4,2},{5,7},{6,0},{7,5},{8,14},{9,11},{10,... | collective-permute-start | bytes 1966088 | tf_op jit(solution)/shard_map/ppermute | solution.py:294
  106.3 20.9 %collective-permute-start.7 = (bf16[64,5120]{1,0:T(8,128)(2,1)S(1)}, bf16[64,5120]{1,0:T(8,128)(2,1)S(1)}, u32[]{:S(2)}, u32[]{:S(2)}) collective-permute-start(bf16[64,5120]{1,0:T(8,128)(2,1)S(1)} %pad_maximum_fusion.refs_7_), channel_id=1, source_target_pairs={{0,1},{1,0},{2,3},{3,2},{4,5},{5,4},{6,7},{7,6},{8,9},{9,8},{10,11... | collective-permute-start | bytes 1966088 | tf_op jit(solution)/shard_map/ppermute | solution.py:294
  107.3 27.4 %collective-permute-start.2 = (bf16[64,5120]{1,0:T(8,128)(2,1)S(1)}, bf16[64,5120]{1,0:T(8,128)(2,1)S(1)}, u32[]{:S(2)}, u32[]{:S(2)}) collective-permute-start(bf16[64,5120]{1,0:T(8,128)(2,1)S(1)} %collective-permute-done.1.refs_5_), channel_id=1, source_target_pairs={{0,6},{1,3},{2,4},{3,1},{4,2},{5,7},{6,0},{7,5},{8,14},{9,11},{10,... | collective-permute-start | bytes 1966088 | tf_op jit(solution)/shard_map/ppermute | solution.py:294
  109.1 6.0 %collective-permute-start.15 = (bf16[64,640]{1,0:T(8,128)(2,1)S(1)}, bf16[64,640]{1,0:T(8,128)(2,1)S(1)}, u32[]{:S(2)}, u32[]{:S(2)}) collective-permute-start(bf16[64,640]{1,0:T(8,128)(2,1)S(1)} %fusion.1), channel_id=1, source_target_pairs={{0,8},{1,9},{2,10},{3,11},{4,12},{5,13},{6,14},{7,15},{8,0},{9,1},... | collective-permute-start | bytes 245768 | tf_op jit(solution)/shard_map/ppermute | solution.py:294
  110.1 27.3 %collective-permute-start.28 = (bf16[64,5120]{1,0:T(8,128)(2,1)S(1)}, bf16[64,5120]{1,0:T(8,128)(2,1)S(1)}, u32[]{:S(2)}, u32[]{:S(2)}) collective-permute-start(bf16[64,5120]{1,0:T(8,128)(2,1)S(1)} %slice.66), channel_id=1, source_target_pairs={{0,6},{1,3},{2,4},{3,1},{4,2},{5,7},{6,0},{7,5},{8,14},{9,11},{10,... | collective-permute-start | bytes 1966088 | tf_op jit(solution)/shard_map/ppermute | solution.py:294
  115.2 6.3 %collective-permute-start.16 = (bf16[64,640]{1,0:T(8,128)(2,1)S(1)}, bf16[64,640]{1,0:T(8,128)(2,1)S(1)}, u32[]{:S(2)}, u32[]{:S(2)}) collective-permute-start(bf16[64,640]{1,0:T(8,128)(2,1)S(1)} %add_convert_fusion.2), channel_id=1, source_target_pairs={{16,0},{32,16},{48,32},{64,48},{80,64},{96,80},{112,96},{17,1},{33... | collective-permute-start | bytes 245768 | tf_op jit(solution)/shard_map/ppermute | solution.py:314
  121.5 5.6 %collective-permute-start.24 = (f32[32,64]{1,0:T(8,128)S(1)}, f32[32,64]{1,0:T(8,128)S(1)}, u32[]{:S(2)}, u32[]{:S(2)}) collective-permute-start(f32[32,64]{1,0:T(8,128)S(1)} %get-tuple-element.20.refs_8_), channel_id=1, source_target_pairs={{16,0},{32,16},{48,32},{64,48},{80,64},{96,80},{112,96},{17,1},{33... | collective-permute-start | bytes 24584 | tf_op jit(solution)/shard_map/ppermute | solution.py:314
  127.1 7.1 %collective-permute-start.17 = (bf16[2,64,640]{2,1,0:T(8,128)(2,1)S(1)}, bf16[2,64,640]{2,1,0:T(8,128)(2,1)S(1)}, u32[]{:S(2)}, u32[]{:S(2)}) collective-permute-start(bf16[2,64,640]{2,1,0:T(8,128)(2,1)S(1)} %pad_maximum_fusion.1.refs_3_), channel_id=1, source_target_pairs={{0,2},{1,7},{2,0},{3,5},{4,6},{5,3},{6,4},{7,1},{8,10},{9,15},{10,... | collective-permute-start | bytes 491528 | tf_op jit(solution)/shard_map/ppermute | solution.py:294
  127.1 10.4 %copy-start.7 = (bf16[64,5120]{1,0:T(8,128)(2,1)}, bf16[64,5120]{1,0:T(8,128)(2,1)S(1)}, u32[]{:S(2)}) copy-start(bf16[64,5120]{1,0:T(8,128)(2,1)S(1)} %collective-permute-done.5.refs_6_) | copy-start | bytes 1966084
  127.1 15.3 %collective-permute-start.4 = (bf16[64,5120]{1,0:T(8,128)(2,1)S(1)}, bf16[64,5120]{1,0:T(8,128)(2,1)S(1)}, u32[]{:S(2)}, u32[]{:S(2)}) collective-permute-start(bf16[64,5120]{1,0:T(8,128)(2,1)S(1)} %collective-permute-done.1.refs_5_), channel_id=1, source_target_pairs={{0,1},{1,0},{2,3},{3,2},{4,5},{5,4},{6,7},{7,6},{8,9},{9,8},{10,11... | collective-permute-start | bytes 1966088 | tf_op jit(solution)/shard_map/ppermute | solution.py:294
  127.2 15.8 %collective-permute-start.6 = (bf16[64,5120]{1,0:T(8,128)(2,1)S(1)}, bf16[64,5120]{1,0:T(8,128)(2,1)S(1)}, u32[]{:S(2)}, u32[]{:S(2)}) collective-permute-start(bf16[64,5120]{1,0:T(8,128)(2,1)S(1)} %collective-permute-done.5.refs_6_), channel_id=1, source_target_pairs={{0,1},{1,0},{2,3},{3,2},{4,5},{5,4},{6,7},{7,6},{8,9},{9,8},{10,11... | collective-permute-start | bytes 1966088 | tf_op jit(solution)/shard_map/ppermute | solution.py:294
  134.2 6.5 %collective-permute-start.19 = (bf16[2,64,640]{2,1,0:T(8,128)(2,1)S(1)}, bf16[2,64,640]{2,1,0:T(8,128)(2,1)S(1)}, u32[]{:S(2)}, u32[]{:S(2)}) collective-permute-start(bf16[2,64,640]{2,1,0:T(8,128)(2,1)S(1)} %pad_maximum_fusion.1.refs_3_), channel_id=1, source_target_pairs={{0,6},{1,3},{2,4},{3,1},{4,2},{5,7},{6,0},{7,5},{8,14},{9,11},{10,... | collective-permute-start | bytes 491528 | tf_op jit(solution)/shard_map/ppermute | solution.py:294
  134.7 7.8 %collective-permute-start.18 = (bf16[2,64,640]{2,1,0:T(8,128)(2,1)S(1)}, bf16[2,64,640]{2,1,0:T(8,128)(2,1)S(1)}, u32[]{:S(2)}, u32[]{:S(2)}) collective-permute-start(bf16[2,64,640]{2,1,0:T(8,128)(2,1)S(1)} %collective-permute-done.17.refs_1_), channel_id=1, source_target_pairs={{0,6},{1,3},{2,4},{3,1},{4,2},{5,7},{6,0},{7,5},{8,14},{9,11},{10,... | collective-permute-start | bytes 491528 | tf_op jit(solution)/shard_map/ppermute | solution.py:294
  137.4 5.6 %collective-permute-start.3 = (bf16[64,5120]{1,0:T(8,128)(2,1)S(1)}, bf16[64,5120]{1,0:T(8,128)(2,1)S(1)}, u32[]{:S(2)}, u32[]{:S(2)}) collective-permute-start(bf16[64,5120]{1,0:T(8,128)(2,1)S(1)} %collective-permute-done.2.refs_4_), channel_id=1, source_target_pairs={{0,1},{1,0},{2,3},{3,2},{4,5},{5,4},{6,7},{7,6},{8,9},{9,8},{10,11... | collective-permute-start | bytes 1966088 | tf_op jit(solution)/shard_map/ppermute | solution.py:294
  140.7 13.9 %collective-permute-start.23 = (bf16[2,64,640]{2,1,0:T(8,128)(2,1)S(1)}, bf16[2,64,640]{2,1,0:T(8,128)(2,1)S(1)}, u32[]{:S(2)}, u32[]{:S(2)}) collective-permute-start(bf16[2,64,640]{2,1,0:T(8,128)(2,1)S(1)} %pad_maximum_fusion.1.refs_3_), channel_id=1, source_target_pairs={{0,1},{1,0},{2,3},{3,2},{4,5},{5,4},{6,7},{7,6},{8,9},{9,8},{10,11... | collective-permute-start | bytes 491528 | tf_op jit(solution)/shard_map/ppermute | solution.py:294
  142.5 12.2 %collective-permute-start.21 = (bf16[2,64,640]{2,1,0:T(8,128)(2,1)S(1)}, bf16[2,64,640]{2,1,0:T(8,128)(2,1)S(1)}, u32[]{:S(2)}, u32[]{:S(2)}) collective-permute-start(bf16[2,64,640]{2,1,0:T(8,128)(2,1)S(1)} %collective-permute-done.17.refs_1_), channel_id=1, source_target_pairs={{0,1},{1,0},{2,3},{3,2},{4,5},{5,4},{6,7},{7,6},{8,9},{9,8},{10,11... | collective-permute-start | bytes 491528 | tf_op jit(solution)/shard_map/ppermute | solution.py:294
  142.5 12.2 %collective-permute-start.22 = (bf16[2,64,640]{2,1,0:T(8,128)(2,1)S(1)}, bf16[2,64,640]{2,1,0:T(8,128)(2,1)S(1)}, u32[]{:S(2)}, u32[]{:S(2)}) collective-permute-start(bf16[2,64,640]{2,1,0:T(8,128)(2,1)S(1)} %collective-permute-done.19.refs_2_), channel_id=1, source_target_pairs={{0,1},{1,0},{2,3},{3,2},{4,5},{5,4},{6,7},{7,6},{8,9},{9,8},{10,11... | collective-permute-start | bytes 491528 | tf_op jit(solution)/shard_map/ppermute | solution.py:294
  143.0 11.7 %collective-permute-start.20 = (bf16[2,64,640]{2,1,0:T(8,128)(2,1)S(1)}, bf16[2,64,640]{2,1,0:T(8,128)(2,1)S(1)}, u32[]{:S(2)}, u32[]{:S(2)}) collective-permute-start(bf16[2,64,640]{2,1,0:T(8,128)(2,1)S(1)} %collective-permute-done.18.refs_0_), channel_id=1, source_target_pairs={{0,1},{1,0},{2,3},{3,2},{4,5},{5,4},{6,7},{7,6},{8,9},{9,8},{10,11... | collective-permute-start | bytes 491528 | tf_op jit(solution)/shard_map/ppermute | solution.py:294
  143.1 11.6 %collective-permute-start.29 = (bf16[32,5120]{1,0:T(8,128)(2,1)S(1)}, bf16[32,5120]{1,0:T(8,128)(2,1)S(1)}, u32[]{:S(2)}, u32[]{:S(2)}) collective-permute-start(bf16[32,5120]{1,0:T(8,128)(2,1)S(1)} %slice.67), channel_id=1, source_target_pairs={{0,8},{1,9},{2,10},{3,11},{4,12},{5,13},{6,14},{7,15},{8,0},{9,1},... | collective-permute-start | bytes 983048 | tf_op jit(solution)/shard_map/ppermute | solution.py:294

commit v2 on v0

v2 whole, which is shorter than its diff:
```python
import jax
import jax.numpy as jnp
from jax import lax
from jax.experimental import pallas as pl
from jax.experimental.pallas import tpu as pltpu
from jax.sharding import PartitionSpec as P

D = 5120
F = 896
R = 64
T = 512
TILE = 640
STEPS = D // TILE
BF = jnp.bfloat16
F32 = jnp.float32
VMEM_LIMIT = 24 * 1024 * 1024


def params(limit=VMEM_LIMIT):
    return pltpu.CompilerParams(vmem_limit_bytes=limit)


def place():
    index = lax.axis_index("fsdp")
    y, x, core = index // 8, (index // 2) % 4, index % 2
    return index, y, x, core


def xor_x(x, mask):
    return x + mask - 2 * (x & mask)


def pieces(value, count):
    out = []
    for _ in range(count):
        part = value.astype(BF)
        out.append(part)
        value = value - part.astype(F32)
    return out


def nn(a, b):
    return lax.dot_general(a, b, (((1,), (0,)), ((), ())), preferred_element_type=F32)


def nt(a, b):
    return lax.dot_general(a, b, (((1,), (1,)), ((), ())), preferred_element_type=F32)


def tn(a, b):
    return lax.dot_general(a, b, (((0,), (0,)), ((), ())), preferred_element_type=F32)


def row_blocks(y, x, core):
    out = []
    for c in (1 - core, core):
        first, second = 1 + 2 * c, 3 - 2 * c
        for xx in (xor_x(x, 2), xor_x(x, first), xor_x(x, second), x):
            for yy in (1 - y, y):
                out.append(yy * 8 + xx * 2 + c)
    return out


def unit_kernel(
    gate_hbm, hidden_hbm, weight, basis_hbm, resid_hbm, fb_hbm,
    unit, ordered, raw_t, held, gate, hidden, basis_t, resid, feedback, small, sems,
):
    def copied(source, target, sem):
        copy = pltpu.make_async_copy(source, target, sem)
        copy.start()
        return copy

    loads = []
    for k, (source, target) in enumerate(((basis_hbm, basis_t), (resid_hbm, resid), (fb_hbm, feedback))):
        loads.append(copied(source, target, small.at[k]))
    copies = []
    for i in range(STEPS):
        rows = pl.ds(i * TILE, TILE)
        copies.append(copied(weight.at[rows], held.at[rows], sems.at[i]))
        if i == 1:
            loads.append(copied(gate_hbm, gate, small.at[3]))
            loads.append(copied(hidden_hbm, hidden, small.at[4]))
    for load in loads[:3]:
        load.wait()
    index, y, x, core = place()
    wb = jnp.zeros((3 * R, F), F32)
    own = jnp.zeros((R, 32), F32)
    for i in range(STEPS):
        columns = slice(i * TILE, (i + 1) * TILE)
        split = jnp.concatenate(pieces(basis_t[:, columns], 3), axis=0)
        rows = jnp.concatenate(pieces(resid[:, columns].astype(F32) + feedback[:, columns], 3), axis=0)
        rb = nt(split, rows)
        rb = rb[0:R] + rb[R : 2 * R] + rb[2 * R : 3 * R]
        own = own + (rb[:, 0:32] + rb[:, 32:64] + rb[:, 64:96])
        copies[i].wait()
        wb = wb + nn(split, held[columns, :])
        if i == 1:
            loads[3].wait()
            loads[4].wait()
        if i >= 1 and i < 7:
            for k in range(16 * (i - 1) // 6, 16 * i // 6):
                rows = slice(k * 32, (k + 1) * 32)
                g = gate[rows].astype(F32)
                unit[rows] = (hidden[rows].astype(F32) * (g / (1.0 + jnp.exp(-g)))).astype(BF)
    for place_to, block in enumerate(row_blocks(y, x, core)):
        ordered[pl.ds(place_to * 32, 32), :] = unit[pl.ds(pl.multiple_of(block * 32, 32), 32), :]
    total = wb[0:R, :] + wb[R : 2 * R, :] + wb[2 * R : 3 * R, :]
    raw3 = nt(jnp.concatenate(pieces(total, 3), axis=0), unit[...])
    raw = raw3[0:R] + raw3[R : 2 * R] + raw3[2 * R : 3 * R]
    placed = nn(jnp.concatenate(pieces(own, 3), axis=0), selection(index))
    raw_t[...] = raw + placed[0:R] + placed[R : 2 * R] + placed[2 * R : 3 * R]


def selection(index):
    spot = lax.broadcasted_iota(jnp.int32, (32, T), 1) - index * 32
    return (spot == lax.broadcasted_iota(jnp.int32, (32, T), 0)).astype(BF)


VMEM = pl.BlockSpec(memory_space=pltpu.VMEM)
ANY = pl.BlockSpec(memory_space=pl.ANY)
TOKEN = jax.ShapeDtypeStruct((8, 128), F32)


def whole(kernel, out_shape, name, operands, deps=(), flops=0, moved=0, out_specs=None, scratch=(), in_specs=None, limit=VMEM_LIMIT):
    count = len(operands)

    def body(*refs):
        kernel(*refs[:count], *refs[count + len(deps) :])

    return pl.pallas_call(
        body,
        in_specs=(in_specs or [VMEM] * count) + [ANY] * len(deps),
        out_specs=out_specs or [VMEM] * len(out_shape),
        out_shape=out_shape,
        scratch_shapes=list(scratch),
        compiler_params=params(limit),
        cost_estimate=pl.CostEstimate(flops=1000, bytes_accessed=1000, transcendentals=0),
        name=name,
    )(*operands, *deps)


def shape(*dims, dtype=F32):
    return jax.ShapeDtypeStruct(dims, dtype)


def unit_call(gate, hidden, weight, basis_t, resid, feedback):
    return whole(
        unit_kernel,
        [shape(T, F, dtype=BF), shape(T, F, dtype=BF), shape(R, T)],
        "unit_and_raw",
        (gate, hidden, weight, basis_t, resid, feedback),
        flops=2 * D * F * 192,
        moved=15_000_000,
        in_specs=[pl.BlockSpec(memory_space=pltpu.HBM)] * 6,
        limit=60 * 1024 * 1024,
        scratch=[
            pltpu.VMEM((D, F), BF),
            pltpu.VMEM((T, F), BF),
            pltpu.VMEM((T, F), BF),
            pltpu.VMEM((R, D), F32),
            pltpu.VMEM((32, D), BF),
            pltpu.VMEM((32, D), F32),
            pltpu.SemaphoreType.DMA((5,)),
            pltpu.SemaphoreType.DMA((STEPS,)),
        ],
    )


def partial_call(ordered, weight, quarter, earlier, deps):
    column = lambda i: (0, quarter * 2 + i)
    count = len(earlier) + len(deps)

    def kernel(unit, held, *refs):
        rows = pl.ds(pl.multiple_of((quarter * 2 + pl.program_id(0)) * TILE, TILE), TILE)
        product = nt(unit[...], held[rows, :])
        refs[count][...] = product[0:256].astype(BF)
        refs[count + 1][...] = product[256:512]
        refs[-1][...] = jnp.zeros((8, 128), F32)

    return pl.pallas_call(
        kernel,
        grid=(2,),
        in_specs=[VMEM, VMEM] + [ANY] * count,
        out_specs=[pl.BlockSpec((256, TILE), column)] * 2 + [pl.BlockSpec((8, 128), lambda i: (0, 0))],
        out_shape=[shape(256, D, dtype=BF), shape(256, D), TOKEN],
        input_output_aliases={2 + k: k for k in range(len(earlier))},
        compiler_params=params(),
        cost_estimate=pl.CostEstimate(flops=1000, bytes_accessed=1000, transcendentals=0),
        name="input_grad_part",
    )(ordered, weight, *earlier, *deps)


def added(a, b, deps=()):
    def kernel(a_ref, b_ref, out):
        out[...] = a_ref[...] + b_ref[...]

    return whole(kernel, [shape(*a.shape)], "raw_sum", (a, b), deps, moved=400_000)[0]


def stacked(values, deps):
    rows = values[0].shape[0]

    def kernel(*refs):
        for k, ref in enumerate(refs[:-1]):
            refs[-1][k * rows : (k + 1) * rows] = ref[...]

    return whole(kernel, [shape(len(values) * rows, D, dtype=BF)], "stack", values, deps, moved=1_300_000)[0]


def grad_start(own, come, deps):
    def kernel(own_ref, come_ref, send, kept):
        send[...] = (own_ref[0:128] + come_ref[0:128].astype(F32)).astype(BF)
        kept[...] = own_ref[128:256] + come_ref[128:256].astype(F32)

    shapes = [shape(128, D, dtype=BF), shape(128, D)]
    return whole(kernel, shapes, "input_grad_sum", (own, come), deps, moved=8_000_000)


def grad_step(kept, come, deps):
    half = kept.shape[0] // 2

    def kernel(kept_ref, come_ref, send, out):
        send[...] = (kept_ref[0:half] + come_ref[0:half].astype(F32)).astype(BF)
        out[...] = kept_ref[half:] + come_ref[half:].astype(F32)

    shapes = [shape(half, D, dtype=BF), shape(half, D)]
    return whole(kernel, shapes, "input_grad_sum", (kept, come), deps, moved=6_000_000)


def chunk_pair(right, right_next, deps):
    def kernel(a, b, out):
        out[0:1] = a[...]
        out[1:2] = b[...]

    return whole(kernel, [shape(2, R, TILE, dtype=BF)], "chunk_pair", (right, right_next), deps, moved=300_000)[0]


def eliminated(gram):
    rows = lax.broadcasted_iota(jnp.int32, (R, 2 * R), 0)
    lanes = lax.broadcasted_iota(jnp.int32, (R, 2 * R), 1)
    work = jnp.concatenate([gram, jnp.zeros((R, R), F32)], axis=1)
    work = jnp.where(lanes == rows + R, 1.0, work)
    scales = []
    for j in range(R):
        column = work[:, j : j + 1]
        pivot = column[j : j + 1, :]
        row = work[j : j + 1, :]
        scales.append(row * lax.rsqrt(pivot))
        work = work - jnp.where(rows[:, 0:1] > j, column, 0.0) * (row / pivot)
    return jnp.concatenate(scales, axis=0)[:, R:]


def exact(op, a, b):
    a1, a2, a3 = pieces(a, 3)
    b1, b2, b3 = pieces(b, 3)
    low = op(a1, b3) + op(a2, b2) + op(a3, b1)
    return op(a1, b1) + (op(a1, b2) + op(a2, b1) + low)


def basis_kernel(raw_a, raw_b, unit, z, left, left_t):
    index, _, _, _ = place()
    raw = raw_a[...] + raw_b[...]
    inverse = eliminated(exact(nt, raw, raw))
    parts = jnp.concatenate(pieces(exact(nn, inverse, raw), 3), axis=0)
    z3 = nn(parts, unit[...])
    z[...] = jnp.concatenate(pieces(z3[0:R] + z3[R : 2 * R] + z3[2 * R : 3 * R], 2), axis=0)
    select = selection(index)
    own3 = nt(select, parts)
    left[...] = own3[:, 0:R] + own3[:, R : 2 * R] + own3[:, 2 * R : 3 * R]
    own_t = nt(parts, select)
    left_t[...] = own_t[0:R] + own_t[R : 2 * R] + own_t[2 * R : 3 * R]


def basis_call(raw_a, raw_b, unit, deps):
    return whole(
        basis_kernel,
        [shape(2 * R, F, dtype=BF), shape(32, R), shape(R, 32)],
        "left_factor",
        (raw_a, raw_b, unit),
        deps,
        flops=7_000_000_000,
        moved=2_000_000,
    )


def factor_kernel(z, left_t, weight, resid, feedback, own_out, other_out):
    _, _, x, core = place()
    l1, l2 = pieces(left_t[...], 2)
    for step in range(STEPS):
        columns = slice(step * TILE, (step + 1) * TILE)
        both = nt(z[...], weight[columns, :])
        value = both[0:R] + both[R : 2 * R]
        r1, r2 = pieces(resid[:, columns].astype(F32) + feedback[:, columns], 2)
        value = value + (nn(l1, r1) + (nn(l1, r2) + nn(l2, r1)))
        c = step // 4
        apart = xor_x(step % 4, x)
        spot = jnp.where(apart == 0, 3, jnp.where(apart == 2, 0, jnp.where(apart == 1 + 2 * c, 1, 2)))

        @pl.when(core == c)
        def _():
            own_out[spot] = value

        @pl.when(core != c)
        def _():
            other_out[spot] = value.astype(BF)


def factor_call(z, left_t, weight, resid, feedback, deps):
    return whole(
        factor_kernel,
        [shape(4, R, TILE), shape(4, R, TILE, dtype=BF)],
        "right_factor",
        (z, left_t, weight, resid, feedback),
        deps,
        flops=2 * D * F * 192,
        moved=12_000_000,
    )


def right_step(total, come, deps):
    keep = total.shape[0] // 2

    def kernel(total_ref, come_ref, send, kept):
        value = total_ref[...] + come_ref[...].astype(F32)
        send[...] = value[0:keep].astype(BF)
        kept[...] = value[keep:]

    shapes = [shape(keep, R, TILE, dtype=BF), shape(keep, R, TILE)]
    return whole(kernel, shapes, "right_sum", (total, come), deps, moved=1_500_000)


def right_last(kept, come, deps, dtype=F32):
    def kernel(kept_ref, come_ref, out):
        out[...] = (kept_ref[...] + come_ref[...]).astype(out.dtype)

    return whole(kernel, [shape(1, R, TILE, dtype=dtype)], "right_sum", (kept, come), deps, moved=500_000)[0]


def grad_call(tokens, ordered, quarter, earlier, deps):
    count = len(earlier) + len(deps)
    ins = len(tokens)

    def kernel(*refs):
        unit, out, token, held, sems = refs[ins], *refs[ins + 1 + count :]
        copies = []
        for k in (0, 1):
            start = (quarter * 2 + k) * TILE
            columns = slice(start, start + TILE)
            blocks = []
            for near, far in (refs[0:2], refs[2:4]):
                for group in (3, 1, 2, 0):
                    rows = slice(group * 32, group * 32 + 32)
                    blocks += [far[rows, columns], near[rows, columns]]
            held[k] = tn(jnp.concatenate(blocks, axis=0), unit[...]).astype(BF)
            copies.append(pltpu.make_async_copy(held.at[k], out.at[pl.ds(start, TILE)], sems.at[k]))
            copies[-1].start()
        token[...] = jnp.zeros((8, 128), F32)
        for copy in copies:
            copy.wait()

    return pl.pallas_call(
        kernel,
        in_specs=[VMEM] * (ins + 1) + [ANY] * count,
        out_specs=[ANY, VMEM],
        out_shape=[shape(D, F, dtype=BF), TOKEN],
        scratch_shapes=[pltpu.VMEM((2, TILE, F), BF), pltpu.SemaphoreType.DMA((2,))],
        input_output_aliases={ins + 1: 0} if earlier else {},
        compiler_params=params(),
        cost_estimate=pl.CostEstimate(flops=1000, bytes_accessed=1000, transcendentals=0),
        name="weight_grad_part",
    )(*tokens, ordered, *earlier, *deps)


def final_kernel(*refs):
    chunks, (left, left_next, resid, feedback, mine, partner, out, received) = refs[:8], refs[8:]
    _, _, x, core = place()
    l3 = jnp.concatenate(pieces(left[...], 2), axis=0)
    n3 = jnp.concatenate(pieces(left_next[...], 2), axis=0)
    for h in (0, 1):
        c = core if h == 0 else 1 - core
        first, second = 1 + 2 * c, 3 - 2 * c
        for k, xx in enumerate((xor_x(x, 2), xor_x(x, first), xor_x(x, second), x)):
            columns = pl.ds(pl.multiple_of((c * 4 + xx) * TILE, 128), TILE)
            chunk = chunks[h * 4 + k]
            here = nn(l3, chunk[0])
            there = nn(n3, chunk[1])
            merged = resid[:, columns].astype(F32) + feedback[:, columns]
            merged = merged + (mine[:, columns] + partner[:, columns].astype(F32))
            out[:, columns] = merged - (here[0:32] + here[32:64])
            received[:, columns] = there[0:32] + there[32:64]


def final_call(chunks, left, left_next, resid, feedback, mine, partner):
    vmem = pl.BlockSpec(memory_space=pltpu.VMEM)
    return pl.pallas_call(
        final_kernel,
        in_specs=[vmem] * 14,
        out_specs=[vmem, vmem],
        out_shape=[jax.ShapeDtypeStruct((32, D), F32)] * 2,
        compiler_params=params(),
        cost_estimate=pl.CostEstimate(flops=1000, bytes_accessed=1000, transcendentals=0),
        name="feedback_and_received",
    )(*chunks, left, left_next, resid, feedback, mine, partner)


def sent(value, move):
    pairs = []
    for index in range(16):
        y, x, core = move(index // 8, (index // 2) % 4, index % 2)
        pairs.append((index, y * 8 + x * 2 + core))
    return lax.ppermute(value, "fsdp", pairs)


def to_core(value):
    return sent(value, lambda y, x, c: (y, x, 1 - c))


def to_first(value):
    return sent(value, lambda y, x, c: (y, x ^ (1 + 2 * c), c))


def to_second(value):
    return sent(value, lambda y, x, c: (y, x ^ (3 - 2 * c), c))


def to_far(value):
    return sent(value, lambda y, x, c: (y, x ^ 2, c))


def to_y(value):
    return sent(value, lambda y, x, c: (1 - y, x, c))


def to_previous(value):
    return lax.ppermute(value, "section", [(s, s - 1) for s in range(1, 8)])


def on_device(activations, gate_preact, hidden_grad, up_weight, resid_grad, feedback, start_basis):
    acts, resid, fb = activations[0], resid_grad[0], feedback[0]
    basis_t = jnp.swapaxes(start_basis[0], 0, 1)

    weight = up_weight[0]
    moved = to_first(acts), to_second(acts), to_far(acts)
    unit, ordered, raw = unit_call(gate_preact[0], hidden_grad[0], weight, basis_t, resid, fb)

    raw = added(raw, to_core(raw))
    come = to_first(raw)
    *parts, token = partial_call(ordered, weight, 0, (), (raw,))
    *parts, token = partial_call(ordered, weight, 1, parts, (token,))
    raw = added(raw, come, (token, *moved))
    come = to_second(raw)
    *parts, token = partial_call(ordered, weight, 2, parts, (raw,))
    other, own, token = partial_call(ordered, weight, 3, parts, (token,))
    raw = added(raw, come, (token,))
    come = to_y(raw)
    come_grad = to_core(other)
    near = stacked((acts, *moved), (raw,))
    far = to_y(near)

    send, grad_kept = grad_start(own, come_grad, (come,))
    grad_first = to_first(send)
    z, left, left_t = basis_call(raw, come, unit, (send,))
    left_next = to_previous(left)
    own, other = factor_call(z, left_t, weight, resid, fb, ())

    come = to_core(other)
    send, kept = right_step(own, come, (grad_first,))
    come = to_first(send)
    send, kept = right_step(kept, come, (left_next,))
    come = to_second(send)
    far = stacked((far,), (kept,))
    tokens = [to_core(near), to_core(far), near, far]
    half_sum = right_last(kept, come, ())
    come = to_y(half_sum)
    send, grad_kept = grad_step(grad_kept, grad_first, (half_sum,))
    grad_second = to_second(send)
    grad, token = grad_call(tokens, ordered, 0, (), (send,))
    grad, token = grad_call(tokens, ordered, 1, (grad,), (token,))
    right = right_last(half_sum, come, (token,), BF)
    right_next = to_previous(right)
    send, mine = grad_step(grad_kept, grad_second, (right,))
    partner = to_y(send)
    grad, token = grad_call(tokens, ordered, 2, (grad,), (send,))
    weight_grad, token = grad_call(tokens, ordered, 3, (grad,), (token,))

    both = chunk_pair(right, right_next, (token,))
    both_first, both_second, both_far = to_first(both), to_second(both), to_far(both)
    own_chunks = [both_far, both_first, both_second, both]
    chunks = own_chunks + [to_core(value) for value in own_chunks]

    new_feedback, received = final_call(chunks, left, left_next, resid, fb, mine, partner)
    return (weight_grad[None], new_feedback[None], received[None])


def solution(mesh):
    return jax.shard_map(
        on_device,
        mesh=mesh,
        in_specs=(
            P("section", "fsdp", None),
            P("section", None, "fsdp"),
            P("section", None, "fsdp"),
            P("section", None, "fsdp"),
            P("section", "fsdp", None),
            P("section", "fsdp", None),
            P("section", None, None),
        ),
        out_specs=(
            P("section", None, "fsdp"),
            P("section", "fsdp", None),
            P("section", "fsdp", None),
        ),
        check_vma=False,
    )
```

time: 462 us -> 120 us (0.26)
  waiting for transfers between devices: 318 us -> 32 us
  blocking collectives: 65.2 us -> 0 us
  Pallas kernels: 0 us -> 43.5 us
  matrix products: 30.9 us -> 0 us
  starting transfers between devices: 6.06 us -> 34.9 us
  other arithmetic: 13.2 us -> 0.01 us
  between operations: 13.8 us -> 1 us
  local copies, waits for them, and re-layouts: 12.9 us -> 7.37 us
    psum x1 -> x0, waiting for transfers between devices: 140 us -> none  [on_device(): lax.psum(jnp.dot(merged.T, left_factor, precision=highest), 'fsdp')]
    reduce_scatter x1 -> x0, waiting for transfers between devices: 113 us -> none  [on_device(): lax.psum_scatter(lax.dot_general(unit_grad, weight_local, (((1,), (1,)),...]
    psum x1 -> x0, blocking collectives: 65.2 us -> none  [on_device(): gram_total = lax.psum(gram_local, 'fsdp')]
    all_gather x1 -> x0, waiting for transfers between devices: 62.8 us -> none  [on_device(): all_acts = lax.all_gather(own_acts, 'fsdp', axis=0, tiled=True)]
    pallas_call x0 -> x25, Pallas kernels: none -> 43.5 us  [the longest x16 23.1 us: whole(): pl.pallas_call(body, in_specs=(in_specs or [VMEM] * count) + [ANY] * len(...]
    dot_general x7 -> x0, matrix products: 30.8 us -> none  [the longest x1 11.4 us: on_device(): lax.dot_general(all_acts, unit_grad, (((0,), (0,)), ((), ())), preferred_...]
    ppermute x2 -> x27, waiting for transfers between devices: 1.33 us -> 32 us  [the longest x25 22.3 us: sent(): return lax.ppermute(value, 'fsdp', pairs)]
    ppermute x2 -> x27, starting transfers between devices: 5.94 us -> 34.9 us  [the longest x25 29.3 us: sent(): return lax.ppermute(value, 'fsdp', pairs)]
  transfers between devices with their start and end apart: 5 -> 27, of which waited for: 4 -> 11; matrix products, arithmetic and copies ran while one was open for 6% -> 0% of each run, Pallas kernels for 0% -> 31%
where the time goes in v2:
time: 120 us; the launch traced here: 119 us
  Pallas kernels  43.5 us (36%)
  starting transfers between devices  34.9 us (29%)
  waiting for transfers between devices  32 us (27%)
  local copies, waits for them, and re-layouts  7.37 us (6%)
    ppermute x25, starting transfers between devices, sent(): return lax.ppermute(value, 'fsdp', pairs)  29.3 us
    pallas_call x16, Pallas kernels, whole(): pl.pallas_call(body, in_specs=(in_specs or [VMEM] * count) + [ANY] * len(...  23.1 us
    ppermute x25, waiting for transfers between devices, sent(): return lax.ppermute(value, 'fsdp', pairs)  22.3 us
    pallas_call x4, Pallas kernels, grad_call(): pl.pallas_call(kernel, in_specs=[VMEM] * (ins + 1) + [ANY] * count, out_s...  10.3 us
    ppermute x2, waiting for transfers between devices, to_previous(): return lax.ppermute(value, 'section', [(s, s - 1) for s in range(1, 8)])  9.73 us
    pallas_call x4, Pallas kernels, partial_call(): pl.pallas_call(kernel, grid=(2,), in_specs=[VMEM, VMEM] + [ANY] * count,...  8.58 us
    unnamed x22, local copies, waits for them, and re-layouts  7.37 us
    ppermute x2, starting transfers between devices, to_previous(): return lax.ppermute(value, 'section', [(s, s - 1) for s in range(1, 8)])  5.61 us
  transfers between devices with their start and end apart: 27, of which 11 were waited for; matrix products, arithmetic and copies ran while one was open for 0% of the time, Pallas kernels for 31%

profile of v2, /device:TPU:96, one launch (start us, length us, event | category | flops | bytes accessed | tf_op | source)
XLA Modules:
  0.0 118.8 jit_solution(2930261934220397913)
XLA Ops:
  0.6 1.6 %collective-permute-start = (bf16[32,5120]{1,0:T(8,128)(2,1)}, bf16[32,5120]{1,0:T(8,128)(2,1)S(1)}, u32[]{:S(2)}, u32[]{:S(2)}) collective-permute-start(bf16[32,5120]{1,0:T(8,128)(2,1)} %bitcast.26), channel_id=1, source_target_pairs={{0,2},{1,7},{2,0},{3,5},{4,6},{5,3},{6,4},{7,1},{8,10},{9,15},{10,... | collective-permute-start | bytes 983048 | tf_op jit(solution)/shard_map/ppermute | solution.py:411
  2.2 2.1 %collective-permute-start.1 = (bf16[32,5120]{1,0:T(8,128)(2,1)}, bf16[32,5120]{1,0:T(8,128)(2,1)S(1)}, u32[]{:S(2)}, u32[]{:S(2)}) collective-permute-start(bf16[32,5120]{1,0:T(8,128)(2,1)} %bitcast.27), channel_id=1, source_target_pairs={{0,6},{1,3},{2,4},{3,1},{4,2},{5,7},{6,0},{7,5},{8,14},{9,11},{10,... | collective-permute-start | bytes 983048 | tf_op jit(solution)/shard_map/ppermute | solution.py:411
  4.3 0.6 collective-permute-start.2
  4.9 10.6 %unit_and_raw.1 = (bf16[512,896]{1,0:T(8,128)(2,1)}, bf16[512,896]{1,0:T(8,128)(2,1)}, f32[64,512]{1,0:T(8,128)}) custom-call(bf16[512,896]{1,0:T(8,128)(2,1)} %bitcast.32, bf16[512,896]{1,0:T(8,128)(2,1)} %bitcast.33, bf16[5120,896]{1,0:T(8,128)(2,1)} %bitcast.12, f32[64,5120]{1,0:T(8,128)} %bitcast.31, bf16[32,5120]{1,0:T(8,128)(2,1)} %bitcast.23, ...), custom_call_target="tpu_custom_call" | custom-call | flops 1000 | bytes 1000 | tf_op jit(solution)/shard_map/unit_and_raw/pallas_call | solution.py:130
  15.6 0.1 collective-permute-start.3
  15.7 1.5 %collective-permute-done.3.refs_1_ = f32[64,512]{1,0:T(8,128)S(1)} collective-permute-done((f32[64,512]{1,0:T(8,128)}, f32[64,512]{1,0:T(8,128)S(1)}, u32[]{:S(2)}, u32[]{:S(2)}) %collective-permute-start.3) | collective-permute-done | bytes 131104 | tf_op jit(solution)/shard_map/ppermute | solution.py:411
  17.2 0.9 copy-done.7
  18.1 1.4 %collective-permute-start.4 = (f32[64,512]{1,0:T(8,128)S(1)}, f32[64,512]{1,0:T(8,128)S(1)}, u32[]{:S(2)}, u32[]{:S(2)}) collective-permute-start(f32[64,512]{1,0:T(8,128)S(1)} %raw_sum.3.refs_0_), channel_id=1, source_target_pairs={{0,2},{1,7},{2,0},{3,5},{4,6},{5,3},{6,4},{7,1},{8,10},{9,15},{10,... | collective-permute-start | bytes 393224 | tf_op jit(solution)/shard_map/ppermute | solution.py:411
  19.6 3.6 %copy-done = bf16[1,5120,896]{2,1,0:T(8,128)(2,1)S(1)} copy-done((bf16[1,5120,896]{2,1,0:T(8,128)(2,1)S(1)}, bf16[1,5120,896]{2,1,0:T(8,128)(2,1)}, u32[]{:S(2)}) %copy-start) | copy-done | bytes 9175064
  23.2 1.2 copy-done.1
  24.4 2.1 %input_grad_part.4 = (bf16[256,5120]{1,0:T(8,128)(2,1)S(1)}, f32[256,5120]{1,0:T(8,128)S(1)}, f32[8,128]{1,0:T(8,128)S(1)}) custom-call(bf16[512,896]{1,0:T(8,128)(2,1)S(1)} %copy-done.1, bf16[5120,896]{1,0:T(8,128)(2,1)S(1)} %bitcast.13, f32[64,512]{1,0:T(8,128)S(1)} %raw_sum.3.refs_0_), custom_call_target="tpu_custom_call" | custom-call | flops 1000 | bytes 1000 | tf_op jit(solution)/shard_map/input_grad_part/pallas_call | solution.py:180
  26.5 0.0 slice-start
  26.5 0.0 slice-start.1
  26.5 2.2 %input_grad_part.5 = (bf16[256,5120]{1,0:T(8,128)(2,1)S(1)}, f32[256,5120]{1,0:T(8,128)S(1)}, f32[8,128]{1,0:T(8,128)S(1)}) custom-call(bf16[512,896]{1,0:T(8,128)(2,1)S(1)} %copy-done.1, bf16[5120,896]{1,0:T(8,128)(2,1)S(1)} %bitcast.14, bf16[256,5120]{1,0:T(8,128)(2,1)S(1)} %get-tuple-element.45.refs_0_, ...), custom_call_target="tpu_custom_call", output_to_operand_aliasing={{0}: (2, {}), {1}: (3, {})} | custom-call | flops 1000 | bytes 1000 | tf_op jit(solution)/shard_map/input_grad_part/pallas_call | solution.py:180
  28.8 1.2 %slice-done.1 = s8[4194304]{0:T(1024)(128)(4,1)S(1)} async-done(((s8[9175040]{0:T(1024)(128)(4,1)}), s8[4194304]{0:T(1024)(128)(4,1)S(1)}, s32[]{:S(2)}) %slice-start.1) | async-done | bytes 4194328
  29.9 0.1 slice-done.2
  30.1 2.1 %input_grad_part.6 = (bf16[256,5120]{1,0:T(8,128)(2,1)S(1)}, f32[256,5120]{1,0:T(8,128)S(1)}, f32[8,128]{1,0:T(8,128)S(1)}) custom-call(bf16[512,896]{1,0:T(8,128)(2,1)S(1)} %copy-done.1, bf16[5120,896]{1,0:T(8,128)(2,1)S(1)} %bitcast.17, bf16[256,5120]{1,0:T(8,128)(2,1)S(1)} %get-tuple-element.49.refs_0_, ...), custom_call_target="tpu_custom_call", output_to_operand_aliasing={{0}: (2, {}), {1}: (3, {})} | custom-call | flops 1000 | bytes 1000 | tf_op jit(solution)/shard_map/input_grad_part/pallas_call | solution.py:180
  32.2 2.2 %input_grad_part.7 = (bf16[256,5120]{1,0:T(8,128)(2,1)S(1)}, f32[256,5120]{1,0:T(8,128)S(1)}, f32[8,128]{1,0:T(8,128)S(1)}) custom-call(bf16[512,896]{1,0:T(8,128)(2,1)S(1)} %copy-done.1, bf16[5120,896]{1,0:T(8,128)(2,1)S(1)} %bitcast.18, bf16[256,5120]{1,0:T(8,128)(2,1)S(1)} %get-tuple-element.51.refs_0_, ...), custom_call_target="tpu_custom_call", output_to_operand_aliasing={{0}: (2, {}), {1}: (3, {})} | custom-call | flops 1000 | bytes 1000 | tf_op jit(solution)/shard_map/input_grad_part/pallas_call | solution.py:180
  34.4 1.2 %collective-permute-start.9 = (bf16[256,5120]{1,0:T(8,128)(2,1)S(1)}, bf16[256,5120]{1,0:T(8,128)(2,1)S(1)}, u32[]{:S(2)}, u32[]{:S(2)}) collective-permute-start(bf16[256,5120]{1,0:T(8,128)(2,1)S(1)} %get-tuple-element.57), channel_id=1, source_target_pairs={{0,1},{1,0},{2,3},{3,2},{4,5},{5,4},{6,7},{7,6},{8,9},{9,8},{10,11... | collective-permute-start | bytes 7864328 | tf_op jit(solution)/shard_map/ppermute | solution.py:411
  35.6 1.0 collective-permute-start.5
  36.7 5.1 %collective-permute-done.5.refs_1_ = f32[64,512]{1,0:T(8,128)S(1)} collective-permute-done((f32[64,512]{1,0:T(8,128)S(1)}, f32[64,512]{1,0:T(8,128)S(1)}, u32[]{:S(2)}, u32[]{:S(2)}) %collective-permute-start.5) | collective-permute-done | bytes 131104 | tf_op jit(solution)/shard_map/ppermute | solution.py:411
  41.8 3.3 %collective-permute-start.8 = (f32[64,512]{1,0:T(8,128)S(1)}, f32[64,512]{1,0:T(8,128)S(1)}, u32[]{:S(2)}, u32[]{:S(2)}) collective-permute-start(f32[64,512]{1,0:T(8,128)S(1)} %raw_sum.5.refs_4_.refs_0_), channel_id=1, source_target_pairs={{0,8},{1,9},{2,10},{3,11},{4,12},{5,13},{6,14},{7,15},{8,0},{9,1},... | collective-permute-start | bytes 393224 | tf_op jit(solution)/shard_map/ppermute | solution.py:411
  45.1 3.3 %collective-permute-done.8.refs_2_.refs_1_ = f32[64,512]{1,0:T(8,128)S(1)} collective-permute-done((f32[64,512]{1,0:T(8,128)S(1)}, f32[64,512]{1,0:T(8,128)S(1)}, u32[]{:S(2)}, u32[]{:S(2)}) %collective-permute-start.8) | collective-permute-done | bytes 131104 | tf_op jit(solution)/shard_map/ppermute | solution.py:411
  48.4 0.5 input_grad_sum.3
  48.9 0.0 copy-start.5
  48.9 0.0 copy-start.3
  48.9 0.0 copy-start.4
  48.9 0.1 collective-permute-start.11
  49.0 0.3 copy-done.6
  49.3 0.1 stack.2.refs_2_
  49.4 3.4 %collective-permute-start.7 = (bf16[128,5120]{1,0:T(8,128)(2,1)S(1)}, bf16[128,5120]{1,0:T(8,128)(2,1)S(1)}, u32[]{:S(2)}, u32[]{:S(2)}) collective-permute-start(bf16[128,5120]{1,0:T(8,128)(2,1)S(1)} %stack.2.refs_2_), channel_id=1, source_target_pairs={{0,8},{1,9},{2,10},{3,11},{4,12},{5,13},{6,14},{7,15},{8,0},{9,1},... | collective-permute-start | bytes 3932168 | tf_op jit(solution)/shard_map/ppermute | solution.py:411
  52.9 6.4 %left_factor.1 = (bf16[128,896]{1,0:T(8,128)(2,1)S(1)}, f32[32,64]{1,0:T(8,128)S(1)}, f32[64,32]{1,0:T(8,128)S(1)}) custom-call(f32[64,512]{1,0:T(8,128)S(1)} %raw_sum.5.refs_4_.refs_0_, f32[64,512]{1,0:T(8,128)S(1)} %collective-permute-done.8.refs_2_.refs_1_, bf16[512,896]{1,0:T(8,128)(2,1)S(1)} %copy-done.5, bf16[128,5120]{1,0:T(8,128)(2,1)S(1)} %get-tuple-element.58.refs_3_), custom_call_target="tpu_custom_call" | custom-call | flops 1000 | bytes 1000 | tf_op jit(solution)/shard_map/left_factor/pallas_call | solution.py:130
  59.3 0.0 copy-done.4
  59.3 4.7 %right_factor.1 = (f32[4,64,640]{2,1,0:T(8,128)S(1)}, bf16[4,64,640]{2,1,0:T(8,128)(2,1)S(1)}) custom-call(bf16[128,896]{1,0:T(8,128)(2,1)S(1)} %get-tuple-element.59.refs_0_, f32[64,32]{1,0:T(8,128)S(1)} %get-tuple-element.60.refs_1_, bf16[5120,896]{1,0:T(8,128)(2,1)S(1)} %bitcast.19, bf16[32,5120]{1,0:T(8,128)(2,1)S(1)} %bitcast.24, f32[32,5120]{1,0:T(8,128)S(1)} %bitcast.21), custom_call_target="tpu_custom_call" | custom-call | flops 1000 | bytes 1000 | tf_op jit(solution)/shard_map/right_factor/pallas_call | solution.py:130
  64.1 0.1 collective-permute-start.10
  64.2 1.6 %collective-permute-done.10.refs_1_ = bf16[4,64,640]{2,1,0:T(8,128)(2,1)S(1)} collective-permute-done((bf16[4,64,640]{2,1,0:T(8,128)(2,1)S(1)}, bf16[4,64,640]{2,1,0:T(8,128)(2,1)S(1)}, u32[]{:S(2)}, u32[]{:S(2)}) %collective-permute-start.10) | collective-permute-done | bytes 327712 | tf_op jit(solution)/shard_map/ppermute | solution.py:411
  65.8 0.8 collective-permute-done.11.refs_2_.refs_1_
  66.6 0.1 right_sum.4
  66.7 1.0 collective-permute-start.12
  67.6 2.5 %collective-permute-start.13 = (f32[32,64]{1,0:T(8,128)S(1)}, f32[32,64]{1,0:T(8,128)S(1)}, u32[]{:S(2)}, u32[]{:S(2)}) collective-permute-start(f32[32,64]{1,0:T(8,128)S(1)} %get-tuple-element.65.refs_8_), channel_id=1, source_target_pairs={{16,0},{32,16},{48,32},{64,48},{80,64},{96,80},{112,96},{17,1},{33... | collective-permute-start | bytes 24584 | tf_op jit(solution)/shard_map/ppermute | solution.py:435
  70.1 0.1 collective-permute-start.6
  70.2 9.7 %collective-permute-done.13.refs_2_.refs_9_ = f32[32,64]{1,0:T(8,128)S(1)} collective-permute-done((f32[32,64]{1,0:T(8,128)S(1)}, f32[32,64]{1,0:T(8,128)S(1)}, u32[]{:S(2)}, u32[]{:S(2)}) %collective-permute-start.13) | collective-permute-done | bytes 8224 | tf_op jit(solution)/shard_map/ppermute | solution.py:435
  80.0 0.1 stack.3.refs_3_
  80.1 0.1 collective-permute-start.14
  80.2 1.9 %collective-permute-start.15 = (bf16[1,64,640]{2,1,0:T(8,128)(2,1)S(1)}, bf16[1,64,640]{2,1,0:T(8,128)(2,1)S(1)}, u32[]{:S(2)}, u32[]{:S(2)}) collective-permute-start(bf16[1,64,640]{2,1,0:T(8,128)(2,1)S(1)} %get-tuple-element.68), channel_id=1, source_target_pairs={{0,6},{1,3},{2,4},{3,1},{4,2},{5,7},{6,0},{7,5},{8,14},{9,11},{10,... | collective-permute-start | bytes 245768 | tf_op jit(solution)/shard_map/ppermute | solution.py:411
  82.1 3.8 %collective-permute-done.15.refs_1_ = bf16[1,64,640]{2,1,0:T(8,128)(2,1)S(1)} collective-permute-done((bf16[1,64,640]{2,1,0:T(8,128)(2,1)S(1)}, bf16[1,64,640]{2,1,0:T(8,128)(2,1)S(1)}, u32[]{:S(2)}, u32[]{:S(2)}) %collective-permute-start.15) | collective-permute-done | bytes 81952 | tf_op jit(solution)/shard_map/ppermute | solution.py:411
  85.9 0.2 input_grad_sum.4
  86.1 1.9 %collective-permute-start.16 = (bf16[64,5120]{1,0:T(8,128)(2,1)S(1)}, bf16[64,5120]{1,0:T(8,128)(2,1)S(1)}, u32[]{:S(2)}, u32[]{:S(2)}) collective-permute-start(bf16[64,5120]{1,0:T(8,128)(2,1)S(1)} %get-tuple-element.69.refs_5_), channel_id=1, source_target_pairs={{0,6},{1,3},{2,4},{3,1},{4,2},{5,7},{6,0},{7,5},{8,14},{9,11},{10,... | collective-permute-start | bytes 1966088 | tf_op jit(solution)/shard_map/ppermute | solution.py:411
  88.1 2.6 %collective-permute-start.17 = (f32[1,64,640]{2,1,0:T(8,128)S(1)}, f32[1,64,640]{2,1,0:T(8,128)S(1)}, u32[]{:S(2)}, u32[]{:S(2)}) collective-permute-start(f32[1,64,640]{2,1,0:T(8,128)S(1)} %right_sum.6.refs_2_.refs_0_), channel_id=1, source_target_pairs={{0,8},{1,9},{2,10},{3,11},{4,12},{5,13},{6,14},{7,15},{8,0},{9,1},... | collective-permute-start | bytes 491528 | tf_op jit(solution)/shard_map/ppermute | solution.py:411
  90.7 2.6 %weight_grad_part.4 = (bf16[5120,896]{1,0:T(8,128)(2,1)}, f32[8,128]{1,0:T(8,128)S(1)}) custom-call(bf16[128,5120]{1,0:T(8,128)(2,1)S(1)} %collective-permute-done.6.refs_0_, bf16[128,5120]{1,0:T(8,128)(2,1)S(1)} %collective-permute-done.14.refs_1_, bf16[128,5120]{1,0:T(8,128)(2,1)S(1)} %stack.2.refs_2_, bf16[128,5120]{1,0:T(8,128)(2,1)S(1)} %stack.3.refs_3_, ...), custom_call_target="tpu_custom_call" | custom-call | flops 1000 | bytes 1000 | tf_op jit(solution)/shard_map/weight_grad_part/pallas_call | solution.py:361
  93.3 2.6 %weight_grad_part.5 = (bf16[5120,896]{1,0:T(8,128)(2,1)}, f32[8,128]{1,0:T(8,128)S(1)}) custom-call(bf16[128,5120]{1,0:T(8,128)(2,1)S(1)} %collective-permute-done.6.refs_0_, bf16[128,5120]{1,0:T(8,128)(2,1)S(1)} %collective-permute-done.14.refs_1_, bf16[128,5120]{1,0:T(8,128)(2,1)S(1)} %stack.2.refs_2_, ...), custom_call_target="tpu_custom_call", output_to_operand_aliasing={{0}: (5, {})} | custom-call | flops 1000 | bytes 1000 | tf_op jit(solution)/shard_map/weight_grad_part/pallas_call | solution.py:361
  95.9 3.1 %collective-permute-start.18 = (bf16[1,64,640]{2,1,0:T(8,128)(2,1)S(1)}, bf16[1,64,640]{2,1,0:T(8,128)(2,1)S(1)}, u32[]{:S(2)}, u32[]{:S(2)}) collective-permute-start(bf16[1,64,640]{2,1,0:T(8,128)(2,1)S(1)} %right_sum.7.refs_2_.refs_0_), channel_id=1, source_target_pairs={{16,0},{32,16},{48,32},{64,48},{80,64},{96,80},{112,96},{17,1},{33... | collective-permute-start | bytes 245768 | tf_op jit(solution)/shard_map/ppermute | solution.py:435
  99.1 0.2 input_grad_sum.5
  99.3 2.6 %weight_grad_part.6 = (bf16[5120,896]{1,0:T(8,128)(2,1)}, f32[8,128]{1,0:T(8,128)S(1)}) custom-call(bf16[128,5120]{1,0:T(8,128)(2,1)S(1)} %collective-permute-done.6.refs_0_, bf16[128,5120]{1,0:T(8,128)(2,1)S(1)} %collective-permute-done.14.refs_1_, bf16[128,5120]{1,0:T(8,128)(2,1)S(1)} %stack.2.refs_2_, ...), custom_call_target="tpu_custom_call", output_to_operand_aliasing={{0}: (5, {})} | custom-call | flops 1000 | bytes 1000 | tf_op jit(solution)/shard_map/weight_grad_part/pallas_call | solution.py:361
  101.9 2.6 %weight_grad_part.7 = (bf16[5120,896]{1,0:T(8,128)(2,1)}, f32[8,128]{1,0:T(8,128)S(1)}) custom-call(bf16[128,5120]{1,0:T(8,128)(2,1)S(1)} %collective-permute-done.6.refs_0_, bf16[128,5120]{1,0:T(8,128)(2,1)S(1)} %collective-permute-done.14.refs_1_, bf16[128,5120]{1,0:T(8,128)(2,1)S(1)} %stack.2.refs_2_, ...), custom_call_target="tpu_custom_call", output_to_operand_aliasing={{0}: (5, {})} | custom-call | flops 1000 | bytes 1000 | tf_op jit(solution)/shard_map/weight_grad_part/pallas_call | solution.py:361
  104.5 0.1 collective-permute-start.19
  104.6 2.6 %collective-permute-start.26 = (bf16[32,5120]{1,0:T(8,128)(2,1)S(1)}, bf16[32,5120]{1,0:T(8,128)(2,1)S(1)}, u32[]{:S(2)}, u32[]{:S(2)}) collective-permute-start(bf16[32,5120]{1,0:T(8,128)(2,1)S(1)} %get-tuple-element.75.refs_6_), channel_id=1, source_target_pairs={{0,8},{1,9},{2,10},{3,11},{4,12},{5,13},{6,14},{7,15},{8,0},{9,1},... | collective-permute-start | bytes 983048 | tf_op jit(solution)/shard_map/ppermute | solution.py:411
  107.2 2.1 %collective-permute-start.20 = (bf16[2,64,640]{2,1,0:T(8,128)(2,1)S(1)}, bf16[2,64,640]{2,1,0:T(8,128)(2,1)S(1)}, u32[]{:S(2)}, u32[]{:S(2)}) collective-permute-start(bf16[2,64,640]{2,1,0:T(8,128)(2,1)S(1)} %chunk_pair.1.refs_3_), channel_id=1, source_target_pairs={{0,2},{1,7},{2,0},{3,5},{4,6},{5,3},{6,4},{7,1},{8,10},{9,15},{10,... | collective-permute-start | bytes 491528 | tf_op jit(solution)/shard_map/ppermute | solution.py:411
  109.3 1.9 %collective-permute-start.21 = (bf16[2,64,640]{2,1,0:T(8,128)(2,1)S(1)}, bf16[2,64,640]{2,1,0:T(8,128)(2,1)S(1)}, u32[]{:S(2)}, u32[]{:S(2)}) collective-permute-start(bf16[2,64,640]{2,1,0:T(8,128)(2,1)S(1)} %chunk_pair.1.refs_3_), channel_id=1, source_target_pairs={{0,6},{1,3},{2,4},{3,1},{4,2},{5,7},{6,0},{7,5},{8,14},{9,11},{10,... | collective-permute-start | bytes 491528 | tf_op jit(solution)/shard_map/ppermute | solution.py:411
  111.2 1.5 %collective-permute-done.19.refs_0_ = bf16[2,64,640]{2,1,0:T(8,128)(2,1)S(1)} collective-permute-done((bf16[2,64,640]{2,1,0:T(8,128)(2,1)S(1)}, bf16[2,64,640]{2,1,0:T(8,128)(2,1)S(1)}, u32[]{:S(2)}, u32[]{:S(2)}) %collective-permute-start.19) | collective-permute-done | bytes 163872 | tf_op jit(solution)/shard_map/ppermute | solution.py:411
  112.6 1.0 collective-permute-done.20.refs_1_
  113.6 2.2 %collective-permute-done.21.refs_2_ = bf16[2,64,640]{2,1,0:T(8,128)(2,1)S(1)} collective-permute-done((bf16[2,64,640]{2,1,0:T(8,128)(2,1)S(1)}, bf16[2,64,640]{2,1,0:T(8,128)(2,1)S(1)}, u32[]{:S(2)}, u32[]{:S(2)}) %collective-permute-start.21) | collective-permute-done | bytes 163872 | tf_op jit(solution)/shard_map/ppermute | solution.py:411
  115.9 1.4 %collective-permute-done.24.refs_6_ = bf16[2,64,640]{2,1,0:T(8,128)(2,1)S(1)} collective-permute-done((bf16[2,64,640]{2,1,0:T(8,128)(2,1)S(1)}, bf16[2,64,640]{2,1,0:T(8,128)(2,1)S(1)}, u32[]{:S(2)}, u32[]{:S(2)}) %collective-permute-start.24) | collective-permute-done | bytes 163872 | tf_op jit(solution)/shard_map/ppermute | solution.py:411
  117.2 1.6 %feedback_and_received.1 = (f32[32,5120]{1,0:T(8,128)}, f32[32,5120]{1,0:T(8,128)}) custom-call(bf16[2,64,640]{2,1,0:T(8,128)(2,1)S(1)} %collective-permute-done.19.refs_0_, bf16[2,64,640]{2,1,0:T(8,128)(2,1)S(1)} %collective-permute-done.20.refs_1_, bf16[2,64,640]{2,1,0:T(8,128)(2,1)S(1)} %collective-permute-done.21.refs_2_, ...), custom_call_target="tpu_custom_call" | custom-call | flops 1000 | bytes 1000 | tf_op jit(solution)/shard_map/feedback_and_received/pallas_call | solution.py:395
  (38 shorter events, 0.2 us)
Async XLA Ops:
  0.6 28.1 %collective-permute-start = (bf16[32,5120]{1,0:T(8,128)(2,1)}, bf16[32,5120]{1,0:T(8,128)(2,1)S(1)}, u32[]{:S(2)}, u32[]{:S(2)}) collective-permute-start(bf16[32,5120]{1,0:T(8,128)(2,1)} %bitcast.26), channel_id=1, source_target_pairs={{0,2},{1,7},{2,0},{3,5},{4,6},{5,3},{6,4},{7,1},{8,10},{9,15},{10,... | collective-permute-start | bytes 983048 | tf_op jit(solution)/shard_map/ppermute | solution.py:411
  2.2 26.5 %collective-permute-start.1 = (bf16[32,5120]{1,0:T(8,128)(2,1)}, bf16[32,5120]{1,0:T(8,128)(2,1)S(1)}, u32[]{:S(2)}, u32[]{:S(2)}) collective-permute-start(bf16[32,5120]{1,0:T(8,128)(2,1)} %bitcast.27), channel_id=1, source_target_pairs={{0,6},{1,3},{2,4},{3,1},{4,2},{5,7},{6,0},{7,5},{8,14},{9,11},{10,... | collective-permute-start | bytes 983048 | tf_op jit(solution)/shard_map/ppermute | solution.py:411
  4.3 24.4 %collective-permute-start.2 = (bf16[32,5120]{1,0:T(8,128)(2,1)}, bf16[32,5120]{1,0:T(8,128)(2,1)S(1)}, u32[]{:S(2)}, u32[]{:S(2)}) collective-permute-start(bf16[32,5120]{1,0:T(8,128)(2,1)} %bitcast.28), channel_id=1, source_target_pairs={{0,4},{1,5},{2,6},{3,7},{4,0},{5,1},{6,2},{7,3},{8,12},{9,13},{10,... | collective-permute-start | bytes 983048 | tf_op jit(solution)/shard_map/ppermute | solution.py:411
  15.6 1.6 %collective-permute-start.3 = (f32[64,512]{1,0:T(8,128)}, f32[64,512]{1,0:T(8,128)S(1)}, u32[]{:S(2)}, u32[]{:S(2)}) collective-permute-start(f32[64,512]{1,0:T(8,128)} %get-tuple-element.43.refs_0_), channel_id=1, source_target_pairs={{0,1},{1,0},{2,3},{3,2},{4,5},{5,4},{6,7},{7,6},{8,9},{9,8},{10,11... | collective-permute-start | bytes 393224 | tf_op jit(solution)/shard_map/ppermute | solution.py:411
  17.2 0.9 copy-start.7
  18.1 10.6 %collective-permute-start.4 = (f32[64,512]{1,0:T(8,128)S(1)}, f32[64,512]{1,0:T(8,128)S(1)}, u32[]{:S(2)}, u32[]{:S(2)}) collective-permute-start(f32[64,512]{1,0:T(8,128)S(1)} %raw_sum.3.refs_0_), channel_id=1, source_target_pairs={{0,2},{1,7},{2,0},{3,5},{4,6},{5,3},{6,4},{7,1},{8,10},{9,15},{10,... | collective-permute-start | bytes 393224 | tf_op jit(solution)/shard_map/ppermute | solution.py:411
  19.6 3.6 %copy-start = (bf16[1,5120,896]{2,1,0:T(8,128)(2,1)S(1)}, bf16[1,5120,896]{2,1,0:T(8,128)(2,1)}, u32[]{:S(2)}) copy-start(bf16[1,5120,896]{2,1,0:T(8,128)(2,1)} %param.10) | copy-start | bytes 27525124
  23.2 1.2 copy-start.1
  26.5 2.3 %slice-start = ((s8[9175040]{0:T(1024)(128)(4,1)}), s8[4194304]{0:T(1024)(128)(4,1)S(1)}, s32[]{:S(2)}) async-start(s8[9175040]{0:T(1024)(128)(4,1)} %bitcast.15), calls=%async_computation | async-start | bytes 8388608
  26.5 3.5 %slice-start.1 = ((s8[9175040]{0:T(1024)(128)(4,1)}), s8[4194304]{0:T(1024)(128)(4,1)S(1)}, s32[]{:S(2)}) async-start(s8[9175040]{0:T(1024)(128)(4,1)} %bitcast.15), calls=%async_computation.1 | async-start | bytes 8388608
  26.5 3.6 %slice-start.2 = ((s8[9175040]{0:T(1024)(128)(4,1)}), s8[786432]{0:T(1024)(128)(4,1)S(1)}, s32[]{:S(2)}) async-start(s8[9175040]{0:T(1024)(128)(4,1)} %bitcast.15), calls=%async_computation.2 | async-start | bytes 1572864
  34.4 14.0 %collective-permute-start.9 = (bf16[256,5120]{1,0:T(8,128)(2,1)S(1)}, bf16[256,5120]{1,0:T(8,128)(2,1)S(1)}, u32[]{:S(2)}, u32[]{:S(2)}) collective-permute-start(bf16[256,5120]{1,0:T(8,128)(2,1)S(1)} %get-tuple-element.57), channel_id=1, source_target_pairs={{0,1},{1,0},{2,3},{3,2},{4,5},{5,4},{6,7},{7,6},{8,9},{9,8},{10,11... | collective-permute-start | bytes 7864328 | tf_op jit(solution)/shard_map/ppermute | solution.py:411
  35.6 6.2 %collective-permute-start.5 = (f32[64,512]{1,0:T(8,128)S(1)}, f32[64,512]{1,0:T(8,128)S(1)}, u32[]{:S(2)}, u32[]{:S(2)}) collective-permute-start(f32[64,512]{1,0:T(8,128)S(1)} %raw_sum.4.refs_2_.refs_0_), channel_id=1, source_target_pairs={{0,6},{1,3},{2,4},{3,1},{4,2},{5,7},{6,0},{7,5},{8,14},{9,11},{10,... | collective-permute-start | bytes 393224 | tf_op jit(solution)/shard_map/ppermute | solution.py:411
  41.8 6.6 %collective-permute-start.8 = (f32[64,512]{1,0:T(8,128)S(1)}, f32[64,512]{1,0:T(8,128)S(1)}, u32[]{:S(2)}, u32[]{:S(2)}) collective-permute-start(f32[64,512]{1,0:T(8,128)S(1)} %raw_sum.5.refs_4_.refs_0_), channel_id=1, source_target_pairs={{0,8},{1,9},{2,10},{3,11},{4,12},{5,13},{6,14},{7,15},{8,0},{9,1},... | collective-permute-start | bytes 393224 | tf_op jit(solution)/shard_map/ppermute | solution.py:411
  48.4 1.0 copy-start.6
  48.9 4.0 %copy-start.5 = (bf16[512,896]{1,0:T(8,128)(2,1)S(1)}, bf16[512,896]{1,0:T(8,128)(2,1)}, u32[]{:S(2)}) copy-start(bf16[512,896]{1,0:T(8,128)(2,1)} %get-tuple-element.55.refs_2_) | copy-start | bytes 2752516
  48.9 10.4 %copy-start.3 = (f32[1,32,5120]{2,1,0:T(8,128)S(1)}, f32[1,32,5120]{2,1,0:T(8,128)}, u32[]{:S(2)}) copy-start(f32[1,32,5120]{2,1,0:T(8,128)} %param.12) | copy-start | bytes 1966084
  48.9 10.4 %copy-start.4 = (bf16[1,32,5120]{2,1,0:T(8,128)(2,1)S(1)}, bf16[1,32,5120]{2,1,0:T(8,128)(2,1)}, u32[]{:S(2)}) copy-start(bf16[1,32,5120]{2,1,0:T(8,128)(2,1)} %param.11) | copy-start | bytes 983044
  48.9 17.7 %collective-permute-start.11 = (bf16[128,5120]{1,0:T(8,128)(2,1)S(1)}, bf16[128,5120]{1,0:T(8,128)(2,1)S(1)}, u32[]{:S(2)}, u32[]{:S(2)}) collective-permute-start(bf16[128,5120]{1,0:T(8,128)(2,1)S(1)} %get-tuple-element.58.refs_3_), channel_id=1, source_target_pairs={{0,2},{1,7},{2,0},{3,5},{4,6},{5,3},{6,4},{7,1},{8,10},{9,15},{10,... | collective-permute-start | bytes 3932168 | tf_op jit(solution)/shard_map/ppermute | solution.py:411
  49.4 30.5 %collective-permute-start.7 = (bf16[128,5120]{1,0:T(8,128)(2,1)S(1)}, bf16[128,5120]{1,0:T(8,128)(2,1)S(1)}, u32[]{:S(2)}, u32[]{:S(2)}) collective-permute-start(bf16[128,5120]{1,0:T(8,128)(2,1)S(1)} %stack.2.refs_2_), channel_id=1, source_target_pairs={{0,8},{1,9},{2,10},{3,11},{4,12},{5,13},{6,14},{7,15},{8,0},{9,1},... | collective-permute-start | bytes 3932168 | tf_op jit(solution)/shard_map/ppermute | solution.py:411
  64.1 1.7 %collective-permute-start.10 = (bf16[4,64,640]{2,1,0:T(8,128)(2,1)S(1)}, bf16[4,64,640]{2,1,0:T(8,128)(2,1)S(1)}, u32[]{:S(2)}, u32[]{:S(2)}) collective-permute-start(bf16[4,64,640]{2,1,0:T(8,128)(2,1)S(1)} %get-tuple-element.62), channel_id=1, source_target_pairs={{0,1},{1,0},{2,3},{3,2},{4,5},{5,4},{6,7},{7,6},{8,9},{9,8},{10,11... | collective-permute-start | bytes 983048 | tf_op jit(solution)/shard_map/ppermute | solution.py:411
  66.7 13.2 %collective-permute-start.12 = (bf16[2,64,640]{2,1,0:T(8,128)(2,1)S(1)}, bf16[2,64,640]{2,1,0:T(8,128)(2,1)S(1)}, u32[]{:S(2)}, u32[]{:S(2)}) collective-permute-start(bf16[2,64,640]{2,1,0:T(8,128)(2,1)S(1)} %get-tuple-element.64), channel_id=1, source_target_pairs={{0,2},{1,7},{2,0},{3,5},{4,6},{5,3},{6,4},{7,1},{8,10},{9,15},{10,... | collective-permute-start | bytes 491528 | tf_op jit(solution)/shard_map/ppermute | solution.py:411
  67.6 12.3 %collective-permute-start.13 = (f32[32,64]{1,0:T(8,128)S(1)}, f32[32,64]{1,0:T(8,128)S(1)}, u32[]{:S(2)}, u32[]{:S(2)}) collective-permute-start(f32[32,64]{1,0:T(8,128)S(1)} %get-tuple-element.65.refs_8_), channel_id=1, source_target_pairs={{16,0},{32,16},{48,32},{64,48},{80,64},{96,80},{112,96},{17,1},{33... | collective-permute-start | bytes 24584 | tf_op jit(solution)/shard_map/ppermute | solution.py:435
  70.1 20.6 %collective-permute-start.6 = (bf16[128,5120]{1,0:T(8,128)(2,1)S(1)}, bf16[128,5120]{1,0:T(8,128)(2,1)S(1)}, u32[]{:S(2)}, u32[]{:S(2)}) collective-permute-start(bf16[128,5120]{1,0:T(8,128)(2,1)S(1)} %stack.2.refs_2_), channel_id=1, source_target_pairs={{0,1},{1,0},{2,3},{3,2},{4,5},{5,4},{6,7},{7,6},{8,9},{9,8},{10,11... | collective-permute-start | bytes 3932168 | tf_op jit(solution)/shard_map/ppermute | solution.py:411
  80.0 10.6 %copy-start.2 = (bf16[512,896]{1,0:T(8,128)(2,1)S(1)}, bf16[512,896]{1,0:T(8,128)(2,1)}, u32[]{:S(2)}) copy-start(bf16[512,896]{1,0:T(8,128)(2,1)} %get-tuple-element.44.unit.refs_4_) | copy-start | bytes 2752516
  80.1 10.6 %collective-permute-start.14 = (bf16[128,5120]{1,0:T(8,128)(2,1)S(1)}, bf16[128,5120]{1,0:T(8,128)(2,1)S(1)}, u32[]{:S(2)}, u32[]{:S(2)}) collective-permute-start(bf16[128,5120]{1,0:T(8,128)(2,1)S(1)} %stack.3.refs_3_), channel_id=1, source_target_pairs={{0,1},{1,0},{2,3},{3,2},{4,5},{5,4},{6,7},{7,6},{8,9},{9,8},{10,11... | collective-permute-start | bytes 3932168 | tf_op jit(solution)/shard_map/ppermute | solution.py:411
  80.2 5.7 %collective-permute-start.15 = (bf16[1,64,640]{2,1,0:T(8,128)(2,1)S(1)}, bf16[1,64,640]{2,1,0:T(8,128)(2,1)S(1)}, u32[]{:S(2)}, u32[]{:S(2)}) collective-permute-start(bf16[1,64,640]{2,1,0:T(8,128)(2,1)S(1)} %get-tuple-element.68), channel_id=1, source_target_pairs={{0,6},{1,3},{2,4},{3,1},{4,2},{5,7},{6,0},{7,5},{8,14},{9,11},{10,... | collective-permute-start | bytes 245768 | tf_op jit(solution)/shard_map/ppermute | solution.py:411
  86.1 13.0 %collective-permute-start.16 = (bf16[64,5120]{1,0:T(8,128)(2,1)S(1)}, bf16[64,5120]{1,0:T(8,128)(2,1)S(1)}, u32[]{:S(2)}, u32[]{:S(2)}) collective-permute-start(bf16[64,5120]{1,0:T(8,128)(2,1)S(1)} %get-tuple-element.69.refs_5_), channel_id=1, source_target_pairs={{0,6},{1,3},{2,4},{3,1},{4,2},{5,7},{6,0},{7,5},{8,14},{9,11},{10,... | collective-permute-start | bytes 1966088 | tf_op jit(solution)/shard_map/ppermute | solution.py:411
  88.1 7.8 %collective-permute-start.17 = (f32[1,64,640]{2,1,0:T(8,128)S(1)}, f32[1,64,640]{2,1,0:T(8,128)S(1)}, u32[]{:S(2)}, u32[]{:S(2)}) collective-permute-start(f32[1,64,640]{2,1,0:T(8,128)S(1)} %right_sum.6.refs_2_.refs_0_), channel_id=1, source_target_pairs={{0,8},{1,9},{2,10},{3,11},{4,12},{5,13},{6,14},{7,15},{8,0},{9,1},... | collective-permute-start | bytes 491528 | tf_op jit(solution)/shard_map/ppermute | solution.py:411
  95.9 8.5 %collective-permute-start.18 = (bf16[1,64,640]{2,1,0:T(8,128)(2,1)S(1)}, bf16[1,64,640]{2,1,0:T(8,128)(2,1)S(1)}, u32[]{:S(2)}, u32[]{:S(2)}) collective-permute-start(bf16[1,64,640]{2,1,0:T(8,128)(2,1)S(1)} %right_sum.7.refs_2_.refs_0_), channel_id=1, source_target_pairs={{16,0},{32,16},{48,32},{64,48},{80,64},{96,80},{112,96},{17,1},{33... | collective-permute-start | bytes 245768 | tf_op jit(solution)/shard_map/ppermute | solution.py:435
  104.5 8.2 %collective-permute-start.19 = (bf16[2,64,640]{2,1,0:T(8,128)(2,1)S(1)}, bf16[2,64,640]{2,1,0:T(8,128)(2,1)S(1)}, u32[]{:S(2)}, u32[]{:S(2)}) collective-permute-start(bf16[2,64,640]{2,1,0:T(8,128)(2,1)S(1)} %chunk_pair.1.refs_3_), channel_id=1, source_target_pairs={{0,4},{1,5},{2,6},{3,7},{4,0},{5,1},{6,2},{7,3},{8,12},{9,13},{10,... | collective-permute-start | bytes 491528 | tf_op jit(solution)/shard_map/ppermute | solution.py:411
  104.6 11.3 %collective-permute-start.26 = (bf16[32,5120]{1,0:T(8,128)(2,1)S(1)}, bf16[32,5120]{1,0:T(8,128)(2,1)S(1)}, u32[]{:S(2)}, u32[]{:S(2)}) collective-permute-start(bf16[32,5120]{1,0:T(8,128)(2,1)S(1)} %get-tuple-element.75.refs_6_), channel_id=1, source_target_pairs={{0,8},{1,9},{2,10},{3,11},{4,12},{5,13},{6,14},{7,15},{8,0},{9,1},... | collective-permute-start | bytes 983048 | tf_op jit(solution)/shard_map/ppermute | solution.py:411
  107.2 6.4 %collective-permute-start.20 = (bf16[2,64,640]{2,1,0:T(8,128)(2,1)S(1)}, bf16[2,64,640]{2,1,0:T(8,128)(2,1)S(1)}, u32[]{:S(2)}, u32[]{:S(2)}) collective-permute-start(bf16[2,64,640]{2,1,0:T(8,128)(2,1)S(1)} %chunk_pair.1.refs_3_), channel_id=1, source_target_pairs={{0,2},{1,7},{2,0},{3,5},{4,6},{5,3},{6,4},{7,1},{8,10},{9,15},{10,... | collective-permute-start | bytes 491528 | tf_op jit(solution)/shard_map/ppermute | solution.py:411
  109.3 6.5 %collective-permute-start.21 = (bf16[2,64,640]{2,1,0:T(8,128)(2,1)S(1)}, bf16[2,64,640]{2,1,0:T(8,128)(2,1)S(1)}, u32[]{:S(2)}, u32[]{:S(2)}) collective-permute-start(bf16[2,64,640]{2,1,0:T(8,128)(2,1)S(1)} %chunk_pair.1.refs_3_), channel_id=1, source_target_pairs={{0,6},{1,3},{2,4},{3,1},{4,2},{5,7},{6,0},{7,5},{8,14},{9,11},{10,... | collective-permute-start | bytes 491528 | tf_op jit(solution)/shard_map/ppermute | solution.py:411
  111.2 4.7 %collective-permute-start.25 = (bf16[2,64,640]{2,1,0:T(8,128)(2,1)S(1)}, bf16[2,64,640]{2,1,0:T(8,128)(2,1)S(1)}, u32[]{:S(2)}, u32[]{:S(2)}) collective-permute-start(bf16[2,64,640]{2,1,0:T(8,128)(2,1)S(1)} %chunk_pair.1.refs_3_), channel_id=1, source_target_pairs={{0,1},{1,0},{2,3},{3,2},{4,5},{5,4},{6,7},{7,6},{8,9},{9,8},{10,11... | collective-permute-start | bytes 491528 | tf_op jit(solution)/shard_map/ppermute | solution.py:411
  112.6 3.2 %collective-permute-start.22 = (bf16[2,64,640]{2,1,0:T(8,128)(2,1)S(1)}, bf16[2,64,640]{2,1,0:T(8,128)(2,1)S(1)}, u32[]{:S(2)}, u32[]{:S(2)}) collective-permute-start(bf16[2,64,640]{2,1,0:T(8,128)(2,1)S(1)} %collective-permute-done.19.refs_0_), channel_id=1, source_target_pairs={{0,1},{1,0},{2,3},{3,2},{4,5},{5,4},{6,7},{7,6},{8,9},{9,8},{10,11... | collective-permute-start | bytes 491528 | tf_op jit(solution)/shard_map/ppermute | solution.py:411
  113.6 2.3 %collective-permute-start.23 = (bf16[2,64,640]{2,1,0:T(8,128)(2,1)S(1)}, bf16[2,64,640]{2,1,0:T(8,128)(2,1)S(1)}, u32[]{:S(2)}, u32[]{:S(2)}) collective-permute-start(bf16[2,64,640]{2,1,0:T(8,128)(2,1)S(1)} %collective-permute-done.20.refs_1_), channel_id=1, source_target_pairs={{0,1},{1,0},{2,3},{3,2},{4,5},{5,4},{6,7},{7,6},{8,9},{9,8},{10,11... | collective-permute-start | bytes 491528 | tf_op jit(solution)/shard_map/ppermute | solution.py:411
  115.8 1.4 %collective-permute-start.24 = (bf16[2,64,640]{2,1,0:T(8,128)(2,1)S(1)}, bf16[2,64,640]{2,1,0:T(8,128)(2,1)S(1)}, u32[]{:S(2)}, u32[]{:S(2)}) collective-permute-start(bf16[2,64,640]{2,1,0:T(8,128)(2,1)S(1)} %collective-permute-done.21.refs_2_), channel_id=1, source_target_pairs={{0,1},{1,0},{2,3},{3,2},{4,5},{5,4},{6,7},{7,6},{8,9},{9,8},{10,11... | collective-permute-start | bytes 491528 | tf_op jit(solution)/shard_map/ppermute | solution.py:411

commit v3 on v2

--- a/solution.py
+++ b/solution.py
@@ -61,27 +61,7 @@
     return out
 
 
-def unit_kernel(
-    gate_hbm, hidden_hbm, weight, basis_hbm, resid_hbm, fb_hbm,
-    unit, ordered, raw_t, held, gate, hidden, basis_t, resid, feedback, small, sems,
-):
-    def copied(source, target, sem):
-        copy = pltpu.make_async_copy(source, target, sem)
-        copy.start()
-        return copy
-
-    loads = []
-    for k, (source, target) in enumerate(((basis_hbm, basis_t), (resid_hbm, resid), (fb_hbm, feedback))):
-        loads.append(copied(source, target, small.at[k]))
-    copies = []
-    for i in range(STEPS):
-        rows = pl.ds(i * TILE, TILE)
-        copies.append(copied(weight.at[rows], held.at[rows], sems.at[i]))
-        if i == 1:
-            loads.append(copied(gate_hbm, gate, small.at[3]))
-            loads.append(copied(hidden_hbm, hidden, small.at[4]))
-    for load in loads[:3]:
-        load.wait()
+def unit_kernel(gate, hidden, weight, basis_t, resid, feedback, unit, ordered, raw_t):
     index, y, x, core = place()
     wb = jnp.zeros((3 * R, F), F32)
     own = jnp.zeros((R, 32), F32)
@@ -92,16 +72,11 @@
         rb = nt(split, rows)
         rb = rb[0:R] + rb[R : 2 * R] + rb[2 * R : 3 * R]
         own = own + (rb[:, 0:32] + rb[:, 32:64] + rb[:, 64:96])
-        copies[i].wait()
-        wb = wb + nn(split, held[columns, :])
-        if i == 1:
-            loads[3].wait()
-            loads[4].wait()
-        if i >= 1 and i < 7:
-            for k in range(16 * (i - 1) // 6, 16 * i // 6):
-                rows = slice(k * 32, (k + 1) * 32)
-                g = gate[rows].astype(F32)
-                unit[rows] = (hidden[rows].astype(F32) * (g / (1.0 + jnp.exp(-g)))).astype(BF)
+        wb = wb + nn(split, weight[columns, :])
+        for k in range(2 * i, 2 * i + 2):
+            rows = slice(k * 32, (k + 1) * 32)
+            g = gate[rows].astype(F32)
+            unit[rows] = (hidden[rows].astype(F32) * (g / (1.0 + jnp.exp(-g)))).astype(BF)
     for place_to, block in enumerate(row_blocks(y, x, core)):
         ordered[pl.ds(place_to * 32, 32), :] = unit[pl.ds(pl.multiple_of(block * 32, 32), 32), :]
     total = wb[0:R, :] + wb[R : 2 * R, :] + wb[2 * R : 3 * R, :]
@@ -121,7 +96,7 @@
 TOKEN = jax.ShapeDtypeStruct((8, 128), F32)
 
 
-def whole(kernel, out_shape, name, operands, deps=(), flops=0, moved=0, out_specs=None, scratch=(), in_specs=None, limit=VMEM_LIMIT):
+def whole(kernel, out_shape, name, operands, deps=(), flops=1000, out_specs=None, scratch=(), in_specs=None, limit=VMEM_LIMIT):
     count = len(operands)
 
     def body(*refs):
@@ -134,7 +109,7 @@
         out_shape=out_shape,
         scratch_shapes=list(scratch),
         compiler_params=params(limit),
-        cost_estimate=pl.CostEstimate(flops=1000, bytes_accessed=1000, transcendentals=0),
+        cost_estimate=pl.CostEstimate(flops=flops, bytes_accessed=1000, transcendentals=0),
         name=name,
     )(*operands, *deps)
 
@@ -143,26 +118,14 @@
     return jax.ShapeDtypeStruct(dims, dtype)
 
 
-def unit_call(gate, hidden, weight, basis_t, resid, feedback):
+def unit_call(gate, hidden, weight, basis_t, resid, feedback, deps):
     return whole(
         unit_kernel,
         [shape(T, F, dtype=BF), shape(T, F, dtype=BF), shape(R, T)],
         "unit_and_raw",
         (gate, hidden, weight, basis_t, resid, feedback),
-        flops=2 * D * F * 192,
-        moved=15_000_000,
-        in_specs=[pl.BlockSpec(memory_space=pltpu.HBM)] * 6,
-        limit=60 * 1024 * 1024,
-        scratch=[
-            pltpu.VMEM((D, F), BF),
-            pltpu.VMEM((T, F), BF),
-            pltpu.VMEM((T, F), BF),
-            pltpu.VMEM((R, D), F32),
-            pltpu.VMEM((32, D), BF),
-            pltpu.VMEM((32, D), F32),
-            pltpu.SemaphoreType.DMA((5,)),
-            pltpu.SemaphoreType.DMA((STEPS,)),
-        ],
+        deps,
+        flops=20_000_000_000,
     )
 
 
@@ -194,7 +157,7 @@
     def kernel(a_ref, b_ref, out):
         out[...] = a_ref[...] + b_ref[...]
 
-    return whole(kernel, [shape(*a.shape)], "raw_sum", (a, b), deps, moved=400_000)[0]
+    return whole(kernel, [shape(*a.shape)], "raw_sum", (a, b), deps)[0]
 
 
 def stacked(values, deps):
@@ -204,7 +167,7 @@
         for k, ref in enumerate(refs[:-1]):
             refs[-1][k * rows : (k + 1) * rows] = ref[...]
 
-    return whole(kernel, [shape(len(values) * rows, D, dtype=BF)], "stack", values, deps, moved=1_300_000)[0]
+    return whole(kernel, [shape(len(values) * rows, D, dtype=BF)], "stack", values, deps)[0]
 
 
 def grad_start(own, come, deps):
@@ -213,7 +176,7 @@
         kept[...] = own_ref[128:256] + come_ref[128:256].astype(F32)
 
     shapes = [shape(128, D, dtype=BF), shape(128, D)]
-    return whole(kernel, shapes, "input_grad_sum", (own, come), deps, moved=8_000_000)
+    return whole(kernel, shapes, "input_grad_sum", (own, come), deps)
 
 
 def grad_step(kept, come, deps):
@@ -224,15 +187,22 @@
         out[...] = kept_ref[half:] + come_ref[half:].astype(F32)
 
     shapes = [shape(half, D, dtype=BF), shape(half, D)]
-    return whole(kernel, shapes, "input_grad_sum", (kept, come), deps, moved=6_000_000)
-
-
-def chunk_pair(right, right_next, deps):
-    def kernel(a, b, out):
-        out[0:1] = a[...]
-        out[1:2] = b[...]
-
-    return whole(kernel, [shape(2, R, TILE, dtype=BF)], "chunk_pair", (right, right_next), deps, moved=300_000)[0]
+    return whole(kernel, shapes, "input_grad_sum", (kept, come), deps)
+
+
+def chunk_pair(half, come, ahead, ahead_far, deps):
+    def kernel(a, b, c, d, out):
+        out[0:1] = (a[...] + b[...].astype(F32)).astype(BF)
+        out[1:2] = (c[...] + d[...].astype(F32)).astype(BF)
+
+    return whole(kernel, [shape(2, R, TILE, dtype=BF)], "chunk_pair", (half, come, ahead, ahead_far), deps)[0]
+
+
+def copied_whole(value, deps, flops=1000):
+    def kernel(ref, out):
+        out[...] = ref[...]
+
+    return whole(kernel, [shape(*value.shape, dtype=value.dtype)], "copied", (value,), deps, flops)[0]
 
 
 def eliminated(gram):
@@ -241,12 +211,19 @@
     work = jnp.concatenate([gram, jnp.zeros((R, R), F32)], axis=1)
     work = jnp.where(lanes == rows + R, 1.0, work)
     scales = []
-    for j in range(R):
-        column = work[:, j : j + 1]
-        pivot = column[j : j + 1, :]
-        row = work[j : j + 1, :]
-        scales.append(row * lax.rsqrt(pivot))
-        work = work - jnp.where(rows[:, 0:1] > j, column, 0.0) * (row / pivot)
+    for j in range(0, R, 8):
+        columns = [jnp.broadcast_to(work[:, j + k : j + k + 1], (R, 2 * R)) for k in range(8)]
+        block = [work[j + k : j + k + 1, :] for k in range(8)]
+        for k in range(8):
+            pivot = columns[k][j + k : j + k + 1, :]
+            inverse = 1.0 / pivot
+            scales.append(block[k] * lax.rsqrt(pivot))
+            row = block[k] * inverse
+            for m in range(k + 1, 8):
+                factor = columns[k][j + m : j + m + 1, :]
+                columns[m] = columns[m] - columns[k] * (factor * inverse)
+                block[m] = block[m] - row * factor
+            work = work - jnp.where(rows > j + k, columns[k], 0.0) * row
     return jnp.concatenate(scales, axis=0)[:, R:]
 
 
@@ -278,8 +255,7 @@
         "left_factor",
         (raw_a, raw_b, unit),
         deps,
-        flops=7_000_000_000,
-        moved=2_000_000,
+
     )
 
 
@@ -312,8 +288,6 @@
         "right_factor",
         (z, left_t, weight, resid, feedback),
         deps,
-        flops=2 * D * F * 192,
-        moved=12_000_000,
     )
 
 
@@ -326,14 +300,17 @@
         kept[...] = value[keep:]
 
     shapes = [shape(keep, R, TILE, dtype=BF), shape(keep, R, TILE)]
-    return whole(kernel, shapes, "right_sum", (total, come), deps, moved=1_500_000)
-
-
-def right_last(kept, come, deps, dtype=F32):
-    def kernel(kept_ref, come_ref, out):
-        out[...] = (kept_ref[...] + come_ref[...]).astype(out.dtype)
-
-    return whole(kernel, [shape(1, R, TILE, dtype=dtype)], "right_sum", (kept, come), deps, moved=500_000)[0]
+    return whole(kernel, shapes, "right_sum", (total, come), deps)
+
+
+def right_sum(total, come, deps):
+    def kernel(total_ref, come_ref, send, kept):
+        value = total_ref[...] + come_ref[...].astype(F32)
+        send[...] = value.astype(BF)
+        kept[...] = value
+
+    shapes = [shape(*total.shape, dtype=BF), shape(*total.shape)]
+    return whole(kernel, shapes, "right_sum", (total, come), deps)
 
 
 def grad_call(tokens, ordered, quarter, earlier, deps):
@@ -435,55 +412,64 @@
     return lax.ppermute(value, "section", [(s, s - 1) for s in range(1, 8)])
 
 
+def to_previous_second(value):
+    pairs = []
+    for s in range(1, 8):
+        for i in range(16):
+            pairs.append((s * 16 + i, (s - 1) * 16 + (i ^ (2 * (3 - 2 * (i % 2))))))
+    return lax.ppermute(value, ("section", "fsdp"), pairs)
+
+
 def on_device(activations, gate_preact, hidden_grad, up_weight, resid_grad, feedback, start_basis):
     acts, resid, fb = activations[0], resid_grad[0], feedback[0]
     basis_t = jnp.swapaxes(start_basis[0], 0, 1)
 
     weight = up_weight[0]
-    moved = to_first(acts), to_second(acts), to_far(acts)
-    unit, ordered, raw = unit_call(gate_preact[0], hidden_grad[0], weight, basis_t, resid, fb)
-
-    raw = added(raw, to_core(raw))
+    first_acts = copied_whole(acts, (), 20_000_000_000)
+    moved_first, moved_second, acts_y = to_first(first_acts), to_second(first_acts), to_y(first_acts)
+    unit, ordered, raw = unit_call(gate_preact[0], hidden_grad[0], weight, basis_t, resid, fb, ())
+
+    come = to_core(raw)
+    sent_first, sent_second = stacked((acts_y,), (raw, moved_second)), stacked((acts_y, moved_first), (raw, moved_second))
+    gone_first, gone_second = to_first(sent_first), to_second(sent_second)
+    *parts, token = partial_call(ordered, weight, 0, (), (raw,))
+    raw = added(raw, come, (token,))
+    come = to_y(raw)
+    *parts, token = partial_call(ordered, weight, 1, parts, (raw,))
+    raw = added(raw, come, (token,))
     come = to_first(raw)
-    *parts, token = partial_call(ordered, weight, 0, (), (raw,))
-    *parts, token = partial_call(ordered, weight, 1, parts, (token,))
-    raw = added(raw, come, (token, *moved))
-    come = to_second(raw)
     *parts, token = partial_call(ordered, weight, 2, parts, (raw,))
     other, own, token = partial_call(ordered, weight, 3, parts, (token,))
-    raw = added(raw, come, (token,))
-    come = to_y(raw)
-    come_grad = to_core(other)
-    near = stacked((acts, *moved), (raw,))
-    far = to_y(near)
-
-    send, grad_kept = grad_start(own, come_grad, (come,))
+    raw = added(raw, come, (token, gone_first, gone_second))
+    gone_far = to_first(gone_second[0:32])
+    near = stacked((acts, moved_first, moved_second, gone_second[32:64]), (raw,))
+    come = to_second(raw)
+    come_grad = to_core(stacked((other,), (raw,)))
+
+    far = stacked((acts_y, gone_first, gone_second[0:32], gone_far), (come,))
+    send, grad_kept = grad_start(own, come_grad, (come, far))
     grad_first = to_first(send)
     z, left, left_t = basis_call(raw, come, unit, (send,))
     left_next = to_previous(left)
     own, other = factor_call(z, left_t, weight, resid, fb, ())
 
     come = to_core(other)
-    send, kept = right_step(own, come, (grad_first,))
+    send, kept = right_step(own, come, ())
     come = to_first(send)
-    send, kept = right_step(kept, come, (left_next,))
-    come = to_second(send)
-    far = stacked((far,), (kept,))
     tokens = [to_core(near), to_core(far), near, far]
-    half_sum = right_last(kept, come, ())
-    come = to_y(half_sum)
-    send, grad_kept = grad_step(grad_kept, grad_first, (half_sum,))
+    grad, token = grad_call(tokens, ordered, 0, (), (kept,))
+    send, kept = right_sum(kept, come, (left_next, token))
+    come = to_y(send)
+    send, grad_kept = grad_step(grad_kept, grad_first, (kept,))
     grad_second = to_second(send)
-    grad, token = grad_call(tokens, ordered, 0, (), (send,))
-    grad, token = grad_call(tokens, ordered, 1, (grad,), (token,))
-    right = right_last(half_sum, come, (token,), BF)
-    right_next = to_previous(right)
-    send, mine = grad_step(grad_kept, grad_second, (right,))
+    grad, token = grad_call(tokens, ordered, 1, (grad,), (send,))
+    grad, token = grad_call(tokens, ordered, 2, (grad,), (token,))
+    send, kept = right_step(kept, come, (token,))
+    come, ahead, ahead_far = to_second(send), to_previous(kept), to_previous_second(send)
+    weight_grad, token = grad_call(tokens, ordered, 3, (grad,), (kept,))
+    both = chunk_pair(kept, come, ahead, ahead_far, (token,))
+    send, mine = grad_step(grad_kept, grad_second, (both,))
     partner = to_y(send)
-    grad, token = grad_call(tokens, ordered, 2, (grad,), (send,))
-    weight_grad, token = grad_call(tokens, ordered, 3, (grad,), (token,))
-
-    both = chunk_pair(right, right_next, (token,))
     both_first, both_second, both_far = to_first(both), to_second(both), to_far(both)
     own_chunks = [both_far, both_first, both_second, both]
     chunks = own_chunks + [to_core(value) for value in own_chunks]

time: 120 us -> 101 us (0.84)
  Pallas kernels: 43.5 us -> 33.4 us
  local copies, waits for them, and re-layouts: 7.37 us -> 1.04 us
  waiting for transfers between devices: 32 us -> 28.8 us
  starting transfers between devices: 34.9 us -> 36.2 us
    pallas_call x16 -> x19, Pallas kernels: 23.1 us -> 12.9 us  [whole(): pl.pallas_call(body, in_specs=(in_specs or [VMEM] * count) + [ANY] * len(...]
    ppermute x2, waiting for transfers between devices: 9.73 us -> 0.68 us  [to_previous(): return lax.ppermute(value, 'section', [(s, s - 1) for s in range(1, 8)])]
    unnamed x22 -> x16, local copies, waits for them, and re-layouts: 7.37 us -> 1 us
    ppermute x25 -> x27, waiting for transfers between devices: 22.3 us -> 28 us  [sent(): return lax.ppermute(value, 'fsdp', pairs)]
    ppermute x0 -> x1, starting transfers between devices: none -> 3.96 us  [to_previous_second(): return lax.ppermute(value, ('section', 'fsdp'), pairs)]
    ppermute x25 -> x27, starting transfers between devices: 29.3 us -> 27.1 us  [sent(): return lax.ppermute(value, 'fsdp', pairs)]
  transfers between devices with their start and end apart: 27 -> 30, of which waited for: 11 -> 14; matrix products, arithmetic and copies ran while one was open for 0% -> 0% of each run, Pallas kernels for 31% -> 31%
where the time goes in v3:
time: 101 us; the launch traced here: 100 us
  starting transfers between devices  36.2 us (36%)
  Pallas kernels  33.4 us (33%)
  waiting for transfers between devices  28.8 us (29%)
  local copies, waits for them, and re-layouts  1.04 us (1%)
    ppermute x27, waiting for transfers between devices, sent(): return lax.ppermute(value, 'fsdp', pairs)  28 us
    ppermute x27, starting transfers between devices, sent(): return lax.ppermute(value, 'fsdp', pairs)  27.1 us
    pallas_call x19, Pallas kernels, whole(): pl.pallas_call(body, in_specs=(in_specs or [VMEM] * count) + [ANY] * len(...  12.9 us
    pallas_call x4, Pallas kernels, grad_call(): pl.pallas_call(kernel, in_specs=[VMEM] * (ins + 1) + [ANY] * count, out_s...  10.4 us
    pallas_call x4, Pallas kernels, partial_call(): pl.pallas_call(kernel, grid=(2,), in_specs=[VMEM, VMEM] + [ANY] * count,...  8.61 us
    ppermute x2, starting transfers between devices, to_previous(): return lax.ppermute(value, 'section', [(s, s - 1) for s in range(1, 8)])  5.15 us
    ppermute x1, starting transfers between devices, to_previous_second(): return lax.ppermute(value, ('section', 'fsdp'), pairs)  3.96 us
  transfers between devices with their start and end apart: 30, of which 14 were waited for; matrix products, arithmetic and copies ran while one was open for 0% of the time, Pallas kernels for 31%

profile of v3, /device:TPU:96, one launch (start us, length us, event | category | flops | bytes accessed | tf_op | source)
XLA Modules:
  0.0 100.4 jit_solution(17086940999514716803)
XLA Ops:
  0.6 0.0 copy-start.3
  0.6 1.0 copy-done.3
  1.7 3.3 %collective-permute-start.2 = (bf16[32,5120]{1,0:T(8,128)(2,1)S(1)}, bf16[32,5120]{1,0:T(8,128)(2,1)S(1)}, u32[]{:S(2)}, u32[]{:S(2)}) collective-permute-start(bf16[32,5120]{1,0:T(8,128)(2,1)S(1)} %copied.1), channel_id=1, source_target_pairs={{0,8},{1,9},{2,10},{3,11},{4,12},{5,13},{6,14},{7,15},{8,0},{9,1},... | collective-permute-start | bytes 983048 | tf_op jit(solution)/shard_map/ppermute | solution.py:388
  4.9 2.8 %collective-permute-start.1 = (bf16[32,5120]{1,0:T(8,128)(2,1)S(1)}, bf16[32,5120]{1,0:T(8,128)(2,1)S(1)}, u32[]{:S(2)}, u32[]{:S(2)}) collective-permute-start(bf16[32,5120]{1,0:T(8,128)(2,1)S(1)} %copied.1), channel_id=1, source_target_pairs={{0,6},{1,3},{2,4},{3,1},{4,2},{5,7},{6,0},{7,5},{8,14},{9,11},{10,... | collective-permute-start | bytes 983048 | tf_op jit(solution)/shard_map/ppermute | solution.py:388
  7.7 0.2 collective-permute-start
  8.0 3.9 %unit_and_raw.1 = (bf16[512,896]{1,0:T(8,128)(2,1)S(1)}, bf16[512,896]{1,0:T(8,128)(2,1)S(1)}, f32[64,512]{1,0:T(8,128)S(1)}) custom-call(bf16[512,896]{1,0:T(8,128)(2,1)S(1)} %bitcast.27, bf16[512,896]{1,0:T(8,128)(2,1)S(1)} %bitcast.28, bf16[5120,896]{1,0:T(8,128)(2,1)S(1)} %bitcast.12, f32[64,5120]{1,0:T(8,128)S(1)} %bitcast.26, ...), custom_call_target="tpu_custom_call" | custom-call | flops 20000000000 | bytes 1000 | tf_op jit(solution)/shard_map/unit_and_raw/pallas_call | solution.py:105
  11.9 0.8 collective-permute-done.2.refs_0_
  12.7 3.8 %collective-permute-done.1.refs_3_.refs_2_ = bf16[32,5120]{1,0:T(8,128)(2,1)S(1)} collective-permute-done((bf16[32,5120]{1,0:T(8,128)(2,1)S(1)}, bf16[32,5120]{1,0:T(8,128)(2,1)S(1)}, u32[]{:S(2)}, u32[]{:S(2)}) %collective-permute-start.1) | collective-permute-done | bytes 327712 | tf_op jit(solution)/shard_map/ppermute | solution.py:388
  16.5 0.0 collective-permute-done.refs_1_
  16.6 2.2 %collective-permute-start.3 = (bf16[64,5120]{1,0:T(8,128)(2,1)S(1)}, bf16[64,5120]{1,0:T(8,128)(2,1)S(1)}, u32[]{:S(2)}, u32[]{:S(2)}) collective-permute-start(bf16[64,5120]{1,0:T(8,128)(2,1)S(1)} %stack.5), channel_id=1, source_target_pairs={{0,6},{1,3},{2,4},{3,1},{4,2},{5,7},{6,0},{7,5},{8,14},{9,11},{10,... | collective-permute-start | bytes 1966088 | tf_op jit(solution)/shard_map/ppermute | solution.py:388
  18.8 0.1 collective-permute-start.7
  18.9 2.2 %input_grad_part.4 = (bf16[256,5120]{1,0:T(8,128)(2,1)S(1)}, f32[256,5120]{1,0:T(8,128)S(1)}, f32[8,128]{1,0:T(8,128)S(1)}) custom-call(bf16[512,896]{1,0:T(8,128)(2,1)S(1)} %get-tuple-element.46.unit.refs_4_, bf16[5120,896]{1,0:T(8,128)(2,1)S(1)} %bitcast.13, f32[64,512]{1,0:T(8,128)S(1)} %get-tuple-element.45.refs_2_.refs_0_.refs_1_), custom_call_target="tpu_custom_call" | custom-call | flops 1000 | bytes 1000 | tf_op jit(solution)/shard_map/input_grad_part/pallas_call | solution.py:143
  21.1 0.5 collective-permute-start.5
  21.5 2.1 %input_grad_part.5 = (bf16[256,5120]{1,0:T(8,128)(2,1)S(1)}, f32[256,5120]{1,0:T(8,128)S(1)}, f32[8,128]{1,0:T(8,128)S(1)}) custom-call(bf16[512,896]{1,0:T(8,128)(2,1)S(1)} %get-tuple-element.46.unit.refs_4_, bf16[5120,896]{1,0:T(8,128)(2,1)S(1)} %bitcast.14, ...), custom_call_target="tpu_custom_call", output_to_operand_aliasing={{0}: (2, {}), {1}: (3, {})} | custom-call | flops 1000 | bytes 1000 | tf_op jit(solution)/shard_map/input_grad_part/pallas_call | solution.py:143
  23.7 5.1 %collective-permute-done.5.refs_1_ = f32[64,512]{1,0:T(8,128)S(1)} collective-permute-done((f32[64,512]{1,0:T(8,128)S(1)}, f32[64,512]{1,0:T(8,128)S(1)}, u32[]{:S(2)}, u32[]{:S(2)}) %collective-permute-start.5) | collective-permute-done | bytes 131104 | tf_op jit(solution)/shard_map/ppermute | solution.py:388
  28.8 1.0 collective-permute-start.6
  29.7 2.1 %input_grad_part.6 = (bf16[256,5120]{1,0:T(8,128)(2,1)S(1)}, f32[256,5120]{1,0:T(8,128)S(1)}, f32[8,128]{1,0:T(8,128)S(1)}) custom-call(bf16[512,896]{1,0:T(8,128)(2,1)S(1)} %get-tuple-element.46.unit.refs_4_, bf16[5120,896]{1,0:T(8,128)(2,1)S(1)} %bitcast.15, ...), custom_call_target="tpu_custom_call", output_to_operand_aliasing={{0}: (2, {}), {1}: (3, {})} | custom-call | flops 1000 | bytes 1000 | tf_op jit(solution)/shard_map/input_grad_part/pallas_call | solution.py:143
  31.9 2.2 %input_grad_part.7 = (bf16[256,5120]{1,0:T(8,128)(2,1)S(1)}, f32[256,5120]{1,0:T(8,128)S(1)}, f32[8,128]{1,0:T(8,128)S(1)}) custom-call(bf16[512,896]{1,0:T(8,128)(2,1)S(1)} %get-tuple-element.46.unit.refs_4_, bf16[5120,896]{1,0:T(8,128)(2,1)S(1)} %bitcast.16, ...), custom_call_target="tpu_custom_call", output_to_operand_aliasing={{0}: (2, {}), {1}: (3, {})} | custom-call | flops 1000 | bytes 1000 | tf_op jit(solution)/shard_map/input_grad_part/pallas_call | solution.py:143
  34.1 0.0 collective-permute-done.7.refs_3_.refs_1_
  34.1 0.0 copy-start.4
  34.1 0.2 stack.9
  34.3 0.2 collective-permute-start.12
  34.5 1.2 %collective-permute-start.9 = (bf16[32,5120]{1,0:T(8,128)(2,1)S(1)}, bf16[32,5120]{1,0:T(8,128)(2,1)S(1)}, u32[]{:S(2)}, u32[]{:S(2)}) collective-permute-start(bf16[32,5120]{1,0:T(8,128)(2,1)S(1)} %get-tuple-element.87.refs_2_), channel_id=1, source_target_pairs={{0,2},{1,7},{2,0},{3,5},{4,6},{5,3},{6,4},{7,1},{8,10},{9,15},{10,... | collective-permute-start | bytes 983048 | tf_op jit(solution)/shard_map/ppermute | solution.py:388
  35.7 1.1 %collective-permute-start.10 = (f32[64,512]{1,0:T(8,128)S(1)}, f32[64,512]{1,0:T(8,128)S(1)}, u32[]{:S(2)}, u32[]{:S(2)}) collective-permute-start(f32[64,512]{1,0:T(8,128)S(1)} %raw_sum.5.refs_4_.refs_1_.refs_0_), channel_id=1, source_target_pairs={{0,6},{1,3},{2,4},{3,1},{4,2},{5,7},{6,0},{7,5},{8,14},{9,11},{10,... | collective-permute-start | bytes 393224 | tf_op jit(solution)/shard_map/ppermute | solution.py:388
  36.8 0.1 stack.7.refs_2_
  36.9 0.1 collective-permute-start.8
  37.0 6.3 %collective-permute-done.10.refs_4_.refs_2_.refs_1_ = f32[64,512]{1,0:T(8,128)S(1)} collective-permute-done((f32[64,512]{1,0:T(8,128)S(1)}, f32[64,512]{1,0:T(8,128)S(1)}, u32[]{:S(2)}, u32[]{:S(2)}) %collective-permute-start.10) | collective-permute-done | bytes 131104 | tf_op jit(solution)/shard_map/ppermute | solution.py:388
  43.3 0.1 stack.8.refs_3_
  43.4 0.3 collective-permute-start.11
  43.7 0.4 input_grad_sum.3
  44.2 0.9 collective-permute-start.14
  45.0 2.6 %left_factor.1 = (bf16[128,896]{1,0:T(8,128)(2,1)S(1)}, f32[32,64]{1,0:T(8,128)S(1)}, f32[64,32]{1,0:T(8,128)S(1)}) custom-call(f32[64,512]{1,0:T(8,128)S(1)} %raw_sum.5.refs_4_.refs_1_.refs_0_, f32[64,512]{1,0:T(8,128)S(1)} %collective-permute-done.10.refs_4_.refs_2_.refs_1_, bf16[512,896]{1,0:T(8,128)(2,1)S(1)} %get-tuple-element.57.refs_2_, ...), custom_call_target="tpu_custom_call" | custom-call | flops 1000 | bytes 1000 | tf_op jit(solution)/shard_map/left_factor/pallas_call | solution.py:105
  47.7 4.7 %right_factor.1 = (f32[4,64,640]{2,1,0:T(8,128)S(1)}, bf16[4,64,640]{2,1,0:T(8,128)(2,1)S(1)}) custom-call(bf16[128,896]{1,0:T(8,128)(2,1)S(1)} %get-tuple-element.61.refs_0_, f32[64,32]{1,0:T(8,128)S(1)} %get-tuple-element.62.refs_1_, bf16[5120,896]{1,0:T(8,128)(2,1)S(1)} %bitcast.17, bf16[32,5120]{1,0:T(8,128)(2,1)S(1)} %bitcast.22, f32[32,5120]{1,0:T(8,128)S(1)} %bitcast.19), custom_call_target="tpu_custom_call" | custom-call | flops 1000 | bytes 1000 | tf_op jit(solution)/shard_map/right_factor/pallas_call | solution.py:105
  52.4 1.3 %collective-permute-start.13 = (bf16[4,64,640]{2,1,0:T(8,128)(2,1)S(1)}, bf16[4,64,640]{2,1,0:T(8,128)(2,1)S(1)}, u32[]{:S(2)}, u32[]{:S(2)}) collective-permute-start(bf16[4,64,640]{2,1,0:T(8,128)(2,1)S(1)} %get-tuple-element.64), channel_id=1, source_target_pairs={{0,1},{1,0},{2,3},{3,2},{4,5},{5,4},{6,7},{7,6},{8,9},{9,8},{10,11... | collective-permute-start | bytes 983048 | tf_op jit(solution)/shard_map/ppermute | solution.py:388
  53.7 1.3 %collective-permute-done.13.refs_1_ = bf16[4,64,640]{2,1,0:T(8,128)(2,1)S(1)} collective-permute-done((bf16[4,64,640]{2,1,0:T(8,128)(2,1)S(1)}, bf16[4,64,640]{2,1,0:T(8,128)(2,1)S(1)}, u32[]{:S(2)}, u32[]{:S(2)}) %collective-permute-start.13) | collective-permute-done | bytes 327712 | tf_op jit(solution)/shard_map/ppermute | solution.py:388
  55.0 0.1 right_sum.3
  55.1 0.6 collective-permute-start.15
  55.7 2.4 %collective-permute-start.16 = (f32[32,64]{1,0:T(8,128)S(1)}, f32[32,64]{1,0:T(8,128)S(1)}, u32[]{:S(2)}, u32[]{:S(2)}) collective-permute-start(f32[32,64]{1,0:T(8,128)S(1)} %get-tuple-element.69.refs_8_), channel_id=1, source_target_pairs={{16,0},{32,16},{48,32},{64,48},{80,64},{96,80},{112,96},{17,1},{33... | collective-permute-start | bytes 24584 | tf_op jit(solution)/shard_map/ppermute | solution.py:412
  58.2 2.6 %weight_grad_part.4 = (bf16[5120,896]{1,0:T(8,128)(2,1)}, f32[8,128]{1,0:T(8,128)S(1)}) custom-call(bf16[128,5120]{1,0:T(8,128)(2,1)S(1)} %collective-permute-done.8.refs_0_, bf16[128,5120]{1,0:T(8,128)(2,1)S(1)} %collective-permute-done.11.refs_1_, bf16[128,5120]{1,0:T(8,128)(2,1)S(1)} %stack.7.refs_2_, bf16[128,5120]{1,0:T(8,128)(2,1)S(1)} %stack.8.refs_3_, ...), custom_call_target="tpu_custom_call" | custom-call | flops 1000 | bytes 1000 | tf_op jit(solution)/shard_map/weight_grad_part/pallas_call | solution.py:338
  60.8 0.7 collective-permute-done.16.refs_2_.refs_9_
  61.5 2.3 %collective-permute-done.15.refs_1_ = bf16[2,64,640]{2,1,0:T(8,128)(2,1)S(1)} collective-permute-done((bf16[2,64,640]{2,1,0:T(8,128)(2,1)S(1)}, bf16[2,64,640]{2,1,0:T(8,128)(2,1)S(1)}, u32[]{:S(2)}, u32[]{:S(2)}) %collective-permute-start.15) | collective-permute-done | bytes 163872 | tf_op jit(solution)/shard_map/ppermute | solution.py:388
  63.8 0.3 input_grad_sum.4
  64.2 1.8 %collective-permute-start.28 = (bf16[64,5120]{1,0:T(8,128)(2,1)S(1)}, bf16[64,5120]{1,0:T(8,128)(2,1)S(1)}, u32[]{:S(2)}, u32[]{:S(2)}) collective-permute-start(bf16[64,5120]{1,0:T(8,128)(2,1)S(1)} %get-tuple-element.72.refs_6_), channel_id=1, source_target_pairs={{0,6},{1,3},{2,4},{3,1},{4,2},{5,7},{6,0},{7,5},{8,14},{9,11},{10,... | collective-permute-start | bytes 1966088 | tf_op jit(solution)/shard_map/ppermute | solution.py:388
  66.0 0.7 collective-permute-start.17
  66.6 2.6 %weight_grad_part.5 = (bf16[5120,896]{1,0:T(8,128)(2,1)}, f32[8,128]{1,0:T(8,128)S(1)}) custom-call(bf16[128,5120]{1,0:T(8,128)(2,1)S(1)} %collective-permute-done.8.refs_0_, bf16[128,5120]{1,0:T(8,128)(2,1)S(1)} %collective-permute-done.11.refs_1_, bf16[128,5120]{1,0:T(8,128)(2,1)S(1)} %stack.7.refs_2_, ...), custom_call_target="tpu_custom_call", output_to_operand_aliasing={{0}: (5, {})} | custom-call | flops 1000 | bytes 1000 | tf_op jit(solution)/shard_map/weight_grad_part/pallas_call | solution.py:338
  69.2 2.6 %weight_grad_part.6 = (bf16[5120,896]{1,0:T(8,128)(2,1)}, f32[8,128]{1,0:T(8,128)S(1)}) custom-call(bf16[128,5120]{1,0:T(8,128)(2,1)S(1)} %collective-permute-done.8.refs_0_, bf16[128,5120]{1,0:T(8,128)(2,1)S(1)} %collective-permute-done.11.refs_1_, bf16[128,5120]{1,0:T(8,128)(2,1)S(1)} %stack.7.refs_2_, ...), custom_call_target="tpu_custom_call", output_to_operand_aliasing={{0}: (5, {})} | custom-call | flops 1000 | bytes 1000 | tf_op jit(solution)/shard_map/weight_grad_part/pallas_call | solution.py:338
  71.8 1.0 collective-permute-done.17.refs_1_
  72.8 2.7 %collective-permute-start.19 = (f32[1,64,640]{2,1,0:T(8,128)S(1)}, f32[1,64,640]{2,1,0:T(8,128)S(1)}, u32[]{:S(2)}, u32[]{:S(2)}) collective-permute-start(f32[1,64,640]{2,1,0:T(8,128)S(1)} %get-tuple-element.78.refs_6_.refs_0_), channel_id=1, source_target_pairs={{16,0},{32,16},{48,32},{64,48},{80,64},{96,80},{112,96},{17,1},{33... | collective-permute-start | bytes 491528 | tf_op jit(solution)/shard_map/ppermute | solution.py:412
  75.5 4.0 %collective-permute-start.20 = (bf16[1,64,640]{2,1,0:T(8,128)(2,1)S(1)}, bf16[1,64,640]{2,1,0:T(8,128)(2,1)S(1)}, u32[]{:S(2)}, u32[]{:S(2)}) collective-permute-start(bf16[1,64,640]{2,1,0:T(8,128)(2,1)S(1)} %get-tuple-element.80), channel_id=1, source_target_pairs={{16,6},{17,3},{18,4},{19,1},{20,2},{21,7},{22,0},{23,5},{24,14},{2... | collective-permute-start | bytes 245768 | tf_op jit(solution)/shard_map/ppermute | solution.py:420
  79.5 1.8 %collective-permute-start.18 = (bf16[1,64,640]{2,1,0:T(8,128)(2,1)S(1)}, bf16[1,64,640]{2,1,0:T(8,128)(2,1)S(1)}, u32[]{:S(2)}, u32[]{:S(2)}) collective-permute-start(bf16[1,64,640]{2,1,0:T(8,128)(2,1)S(1)} %get-tuple-element.80), channel_id=1, source_target_pairs={{0,6},{1,3},{2,4},{3,1},{4,2},{5,7},{6,0},{7,5},{8,14},{9,11},{10,... | collective-permute-start | bytes 245768 | tf_op jit(solution)/shard_map/ppermute | solution.py:388
  81.3 2.6 %weight_grad_part.7 = (bf16[5120,896]{1,0:T(8,128)(2,1)}, f32[8,128]{1,0:T(8,128)S(1)}) custom-call(bf16[128,5120]{1,0:T(8,128)(2,1)S(1)} %collective-permute-done.8.refs_0_, bf16[128,5120]{1,0:T(8,128)(2,1)S(1)} %collective-permute-done.11.refs_1_, bf16[128,5120]{1,0:T(8,128)(2,1)S(1)} %stack.7.refs_2_, ...), custom_call_target="tpu_custom_call", output_to_operand_aliasing={{0}: (5, {})} | custom-call | flops 1000 | bytes 1000 | tf_op jit(solution)/shard_map/weight_grad_part/pallas_call | solution.py:338
  83.9 0.1 collective-permute-done.20.refs_3_
  84.0 1.3 %collective-permute-done.18.refs_1_ = bf16[1,64,640]{2,1,0:T(8,128)(2,1)S(1)} collective-permute-done((bf16[1,64,640]{2,1,0:T(8,128)(2,1)S(1)}, bf16[1,64,640]{2,1,0:T(8,128)(2,1)S(1)}, u32[]{:S(2)}, u32[]{:S(2)}) %collective-permute-start.18) | collective-permute-done | bytes 81952 | tf_op jit(solution)/shard_map/ppermute | solution.py:388
  85.3 1.8 %collective-permute-start.23 = (bf16[2,64,640]{2,1,0:T(8,128)(2,1)S(1)}, bf16[2,64,640]{2,1,0:T(8,128)(2,1)S(1)}, u32[]{:S(2)}, u32[]{:S(2)}) collective-permute-start(bf16[2,64,640]{2,1,0:T(8,128)(2,1)S(1)} %chunk_pair.1.refs_2_.refs_3_), channel_id=1, source_target_pairs={{0,6},{1,3},{2,4},{3,1},{4,2},{5,7},{6,0},{7,5},{8,14},{9,11},{10,... | collective-permute-start | bytes 491528 | tf_op jit(solution)/shard_map/ppermute | solution.py:388
  87.1 3.0 %collective-permute-start.21 = (bf16[2,64,640]{2,1,0:T(8,128)(2,1)S(1)}, bf16[2,64,640]{2,1,0:T(8,128)(2,1)S(1)}, u32[]{:S(2)}, u32[]{:S(2)}) collective-permute-start(bf16[2,64,640]{2,1,0:T(8,128)(2,1)S(1)} %chunk_pair.1.refs_2_.refs_3_), channel_id=1, source_target_pairs={{0,4},{1,5},{2,6},{3,7},{4,0},{5,1},{6,2},{7,3},{8,12},{9,13},{10,... | collective-permute-start | bytes 491528 | tf_op jit(solution)/shard_map/ppermute | solution.py:388
  90.1 0.1 input_grad_sum.5
  90.2 2.0 %collective-permute-start.29 = (bf16[32,5120]{1,0:T(8,128)(2,1)S(1)}, bf16[32,5120]{1,0:T(8,128)(2,1)S(1)}, u32[]{:S(2)}, u32[]{:S(2)}) collective-permute-start(bf16[32,5120]{1,0:T(8,128)(2,1)S(1)} %get-tuple-element.84), channel_id=1, source_target_pairs={{0,8},{1,9},{2,10},{3,11},{4,12},{5,13},{6,14},{7,15},{8,0},{9,1},... | collective-permute-start | bytes 983048 | tf_op jit(solution)/shard_map/ppermute | solution.py:388
  92.2 0.1 collective-permute-done.23.refs_2_
  92.3 0.4 collective-permute-start.26
  92.7 0.1 collective-permute-start.25
  92.8 2.3 %collective-permute-done.21.refs_0_ = bf16[2,64,640]{2,1,0:T(8,128)(2,1)S(1)} collective-permute-done((bf16[2,64,640]{2,1,0:T(8,128)(2,1)S(1)}, bf16[2,64,640]{2,1,0:T(8,128)(2,1)S(1)}, u32[]{:S(2)}, u32[]{:S(2)}) %collective-permute-start.21) | collective-permute-done | bytes 163872 | tf_op jit(solution)/shard_map/ppermute | solution.py:388
  95.1 1.4 %collective-permute-done.24.refs_4_ = bf16[2,64,640]{2,1,0:T(8,128)(2,1)S(1)} collective-permute-done((bf16[2,64,640]{2,1,0:T(8,128)(2,1)S(1)}, bf16[2,64,640]{2,1,0:T(8,128)(2,1)S(1)}, u32[]{:S(2)}, u32[]{:S(2)}) %collective-permute-start.24) | collective-permute-done | bytes 163872 | tf_op jit(solution)/shard_map/ppermute | solution.py:388
  96.5 2.4 %collective-permute-done.29.refs_13_ = bf16[32,5120]{1,0:T(8,128)(2,1)S(1)} collective-permute-done((bf16[32,5120]{1,0:T(8,128)(2,1)S(1)}, bf16[32,5120]{1,0:T(8,128)(2,1)S(1)}, u32[]{:S(2)}, u32[]{:S(2)}) %collective-permute-start.29) | collective-permute-done | bytes 327712 | tf_op jit(solution)/shard_map/ppermute | solution.py:388
  98.9 1.6 %feedback_and_received.1 = (f32[32,5120]{1,0:T(8,128)}, f32[32,5120]{1,0:T(8,128)}) custom-call(bf16[2,64,640]{2,1,0:T(8,128)(2,1)S(1)} %collective-permute-done.21.refs_0_, bf16[2,64,640]{2,1,0:T(8,128)(2,1)S(1)} %collective-permute-done.22.refs_1_, bf16[2,64,640]{2,1,0:T(8,128)(2,1)S(1)} %collective-permute-done.23.refs_2_, ...), custom_call_target="tpu_custom_call" | custom-call | flops 1000 | bytes 1000 | tf_op jit(solution)/shard_map/feedback_and_received/pallas_call | solution.py:372
  (41 shorter events, 0.4 us)
Async XLA Ops:
  0.6 1.0 copy-start.3
  1.6 6.3 %copy-start = (bf16[1,5120,896]{2,1,0:T(8,128)(2,1)S(1)}, bf16[1,5120,896]{2,1,0:T(8,128)(2,1)}, u32[]{:S(2)}) copy-start(bf16[1,5120,896]{2,1,0:T(8,128)(2,1)} %param.10) | copy-start | bytes 27525124
  1.6 6.3 %copy-start.1 = (f32[1,32,5120]{2,1,0:T(8,128)S(1)}, f32[1,32,5120]{2,1,0:T(8,128)}, u32[]{:S(2)}) copy-start(f32[1,32,5120]{2,1,0:T(8,128)} %param.12) | copy-start | bytes 1966084
  1.6 6.3 %copy-start.2 = (bf16[1,32,5120]{2,1,0:T(8,128)(2,1)S(1)}, bf16[1,32,5120]{2,1,0:T(8,128)(2,1)}, u32[]{:S(2)}) copy-start(bf16[1,32,5120]{2,1,0:T(8,128)(2,1)} %param.11) | copy-start | bytes 983044
  1.6 6.3 %copy-start.5 = (f32[1,5120,64]{1,2,0:T(8,128)S(1)}, f32[1,5120,64]{1,2,0:T(8,128)}, u32[]{:S(2)}) copy-start(f32[1,5120,64]{1,2,0:T(8,128)} %param.13) | copy-start | bytes 3932164
  1.6 6.3 %copy-start.6 = (bf16[1,512,896]{2,1,0:T(8,128)(2,1)S(1)}, bf16[1,512,896]{2,1,0:T(8,128)(2,1)}, u32[]{:S(2)}) copy-start(bf16[1,512,896]{2,1,0:T(8,128)(2,1)} %param.8) | copy-start | bytes 2752516
  1.6 6.3 %copy-start.7 = (bf16[1,512,896]{2,1,0:T(8,128)(2,1)S(1)}, bf16[1,512,896]{2,1,0:T(8,128)(2,1)}, u32[]{:S(2)}) copy-start(bf16[1,512,896]{2,1,0:T(8,128)(2,1)} %param.9) | copy-start | bytes 2752516
  1.7 11.0 %collective-permute-start.2 = (bf16[32,5120]{1,0:T(8,128)(2,1)S(1)}, bf16[32,5120]{1,0:T(8,128)(2,1)S(1)}, u32[]{:S(2)}, u32[]{:S(2)}) collective-permute-start(bf16[32,5120]{1,0:T(8,128)(2,1)S(1)} %copied.1), channel_id=1, source_target_pairs={{0,8},{1,9},{2,10},{3,11},{4,12},{5,13},{6,14},{7,15},{8,0},{9,1},... | collective-permute-start | bytes 983048 | tf_op jit(solution)/shard_map/ppermute | solution.py:388
  4.9 11.6 %collective-permute-start.1 = (bf16[32,5120]{1,0:T(8,128)(2,1)S(1)}, bf16[32,5120]{1,0:T(8,128)(2,1)S(1)}, u32[]{:S(2)}, u32[]{:S(2)}) collective-permute-start(bf16[32,5120]{1,0:T(8,128)(2,1)S(1)} %copied.1), channel_id=1, source_target_pairs={{0,6},{1,3},{2,4},{3,1},{4,2},{5,7},{6,0},{7,5},{8,14},{9,11},{10,... | collective-permute-start | bytes 983048 | tf_op jit(solution)/shard_map/ppermute | solution.py:388
  7.7 8.8 %collective-permute-start = (bf16[32,5120]{1,0:T(8,128)(2,1)S(1)}, bf16[32,5120]{1,0:T(8,128)(2,1)S(1)}, u32[]{:S(2)}, u32[]{:S(2)}) collective-permute-start(bf16[32,5120]{1,0:T(8,128)(2,1)S(1)} %copied.1), channel_id=1, source_target_pairs={{0,2},{1,7},{2,0},{3,5},{4,6},{5,3},{6,4},{7,1},{8,10},{9,15},{10,... | collective-permute-start | bytes 983048 | tf_op jit(solution)/shard_map/ppermute | solution.py:388
  16.6 17.5 %collective-permute-start.3 = (bf16[64,5120]{1,0:T(8,128)(2,1)S(1)}, bf16[64,5120]{1,0:T(8,128)(2,1)S(1)}, u32[]{:S(2)}, u32[]{:S(2)}) collective-permute-start(bf16[64,5120]{1,0:T(8,128)(2,1)S(1)} %stack.5), channel_id=1, source_target_pairs={{0,6},{1,3},{2,4},{3,1},{4,2},{5,7},{6,0},{7,5},{8,14},{9,11},{10,... | collective-permute-start | bytes 1966088 | tf_op jit(solution)/shard_map/ppermute | solution.py:388
  18.8 2.3 %collective-permute-start.4 = (f32[64,512]{1,0:T(8,128)S(1)}, f32[64,512]{1,0:T(8,128)S(1)}, u32[]{:S(2)}, u32[]{:S(2)}) collective-permute-start(f32[64,512]{1,0:T(8,128)S(1)} %get-tuple-element.45.refs_2_.refs_0_.refs_1_), channel_id=1, source_target_pairs={{0,1},{1,0},{2,3},{3,2},{4,5},{5,4},{6,7},{7,6},{8,9},{9,8},{10,11... | collective-permute-start | bytes 393224 | tf_op jit(solution)/shard_map/ppermute | solution.py:388
  18.8 15.3 %collective-permute-start.7 = (bf16[32,5120]{1,0:T(8,128)(2,1)S(1)}, bf16[32,5120]{1,0:T(8,128)(2,1)S(1)}, u32[]{:S(2)}, u32[]{:S(2)}) collective-permute-start(bf16[32,5120]{1,0:T(8,128)(2,1)S(1)} %stack.6), channel_id=1, source_target_pairs={{0,2},{1,7},{2,0},{3,5},{4,6},{5,3},{6,4},{7,1},{8,10},{9,15},{10,... | collective-permute-start | bytes 983048 | tf_op jit(solution)/shard_map/ppermute | solution.py:388
  21.1 7.7 %collective-permute-start.5 = (f32[64,512]{1,0:T(8,128)S(1)}, f32[64,512]{1,0:T(8,128)S(1)}, u32[]{:S(2)}, u32[]{:S(2)}) collective-permute-start(f32[64,512]{1,0:T(8,128)S(1)} %raw_sum.3.refs_2_.refs_0_), channel_id=1, source_target_pairs={{0,8},{1,9},{2,10},{3,11},{4,12},{5,13},{6,14},{7,15},{8,0},{9,1},... | collective-permute-start | bytes 393224 | tf_op jit(solution)/shard_map/ppermute | solution.py:388
  28.8 5.3 %collective-permute-start.6 = (f32[64,512]{1,0:T(8,128)S(1)}, f32[64,512]{1,0:T(8,128)S(1)}, u32[]{:S(2)}, u32[]{:S(2)}) collective-permute-start(f32[64,512]{1,0:T(8,128)S(1)} %raw_sum.4.refs_2_.refs_0_), channel_id=1, source_target_pairs={{0,2},{1,7},{2,0},{3,5},{4,6},{5,3},{6,4},{7,1},{8,10},{9,15},{10,... | collective-permute-start | bytes 393224 | tf_op jit(solution)/shard_map/ppermute | solution.py:388
  34.1 2.7 %copy-start.4 = (bf16[1,32,5120]{2,1,0:T(8,128)(2,1)S(1)}, bf16[1,32,5120]{2,1,0:T(8,128)(2,1)}, u32[]{:S(2)}) copy-start(bf16[1,32,5120]{2,1,0:T(8,128)(2,1)} %param.7) | copy-start | bytes 983044
  34.3 9.4 %collective-permute-start.12 = (bf16[256,5120]{1,0:T(8,128)(2,1)S(1)}, bf16[256,5120]{1,0:T(8,128)(2,1)S(1)}, u32[]{:S(2)}, u32[]{:S(2)}) collective-permute-start(bf16[256,5120]{1,0:T(8,128)(2,1)S(1)} %stack.9), channel_id=1, source_target_pairs={{0,1},{1,0},{2,3},{3,2},{4,5},{5,4},{6,7},{7,6},{8,9},{9,8},{10,11... | collective-permute-start | bytes 7864328 | tf_op jit(solution)/shard_map/ppermute | solution.py:388
  34.5 8.8 %collective-permute-start.9 = (bf16[32,5120]{1,0:T(8,128)(2,1)S(1)}, bf16[32,5120]{1,0:T(8,128)(2,1)S(1)}, u32[]{:S(2)}, u32[]{:S(2)}) collective-permute-start(bf16[32,5120]{1,0:T(8,128)(2,1)S(1)} %get-tuple-element.87.refs_2_), channel_id=1, source_target_pairs={{0,2},{1,7},{2,0},{3,5},{4,6},{5,3},{6,4},{7,1},{8,10},{9,15},{10,... | collective-permute-start | bytes 983048 | tf_op jit(solution)/shard_map/ppermute | solution.py:388
  35.7 7.6 %collective-permute-start.10 = (f32[64,512]{1,0:T(8,128)S(1)}, f32[64,512]{1,0:T(8,128)S(1)}, u32[]{:S(2)}, u32[]{:S(2)}) collective-permute-start(f32[64,512]{1,0:T(8,128)S(1)} %raw_sum.5.refs_4_.refs_1_.refs_0_), channel_id=1, source_target_pairs={{0,6},{1,3},{2,4},{3,1},{4,2},{5,7},{6,0},{7,5},{8,14},{9,11},{10,... | collective-permute-start | bytes 393224 | tf_op jit(solution)/shard_map/ppermute | solution.py:388
  36.9 21.3 %collective-permute-start.8 = (bf16[128,5120]{1,0:T(8,128)(2,1)S(1)}, bf16[128,5120]{1,0:T(8,128)(2,1)S(1)}, u32[]{:S(2)}, u32[]{:S(2)}) collective-permute-start(bf16[128,5120]{1,0:T(8,128)(2,1)S(1)} %stack.7.refs_2_), channel_id=1, source_target_pairs={{0,1},{1,0},{2,3},{3,2},{4,5},{5,4},{6,7},{7,6},{8,9},{9,8},{10,11... | collective-permute-start | bytes 3932168 | tf_op jit(solution)/shard_map/ppermute | solution.py:388
  43.4 14.8 %collective-permute-start.11 = (bf16[128,5120]{1,0:T(8,128)(2,1)S(1)}, bf16[128,5120]{1,0:T(8,128)(2,1)S(1)}, u32[]{:S(2)}, u32[]{:S(2)}) collective-permute-start(bf16[128,5120]{1,0:T(8,128)(2,1)S(1)} %stack.8.refs_3_), channel_id=1, source_target_pairs={{0,1},{1,0},{2,3},{3,2},{4,5},{5,4},{6,7},{7,6},{8,9},{9,8},{10,11... | collective-permute-start | bytes 3932168 | tf_op jit(solution)/shard_map/ppermute | solution.py:388
  44.2 19.7 %collective-permute-start.14 = (bf16[128,5120]{1,0:T(8,128)(2,1)S(1)}, bf16[128,5120]{1,0:T(8,128)(2,1)S(1)}, u32[]{:S(2)}, u32[]{:S(2)}) collective-permute-start(bf16[128,5120]{1,0:T(8,128)(2,1)S(1)} %get-tuple-element.60.refs_3_), channel_id=1, source_target_pairs={{0,2},{1,7},{2,0},{3,5},{4,6},{5,3},{6,4},{7,1},{8,10},{9,15},{10,... | collective-permute-start | bytes 3932168 | tf_op jit(solution)/shard_map/ppermute | solution.py:388
  52.4 2.6 %collective-permute-start.13 = (bf16[4,64,640]{2,1,0:T(8,128)(2,1)S(1)}, bf16[4,64,640]{2,1,0:T(8,128)(2,1)S(1)}, u32[]{:S(2)}, u32[]{:S(2)}) collective-permute-start(bf16[4,64,640]{2,1,0:T(8,128)(2,1)S(1)} %get-tuple-element.64), channel_id=1, source_target_pairs={{0,1},{1,0},{2,3},{3,2},{4,5},{5,4},{6,7},{7,6},{8,9},{9,8},{10,11... | collective-permute-start | bytes 983048 | tf_op jit(solution)/shard_map/ppermute | solution.py:388
  55.1 8.7 %collective-permute-start.15 = (bf16[2,64,640]{2,1,0:T(8,128)(2,1)S(1)}, bf16[2,64,640]{2,1,0:T(8,128)(2,1)S(1)}, u32[]{:S(2)}, u32[]{:S(2)}) collective-permute-start(bf16[2,64,640]{2,1,0:T(8,128)(2,1)S(1)} %get-tuple-element.68), channel_id=1, source_target_pairs={{0,2},{1,7},{2,0},{3,5},{4,6},{5,3},{6,4},{7,1},{8,10},{9,15},{10,... | collective-permute-start | bytes 491528 | tf_op jit(solution)/shard_map/ppermute | solution.py:388
  55.7 5.7 %collective-permute-start.16 = (f32[32,64]{1,0:T(8,128)S(1)}, f32[32,64]{1,0:T(8,128)S(1)}, u32[]{:S(2)}, u32[]{:S(2)}) collective-permute-start(f32[32,64]{1,0:T(8,128)S(1)} %get-tuple-element.69.refs_8_), channel_id=1, source_target_pairs={{16,0},{32,16},{48,32},{64,48},{80,64},{96,80},{112,96},{17,1},{33... | collective-permute-start | bytes 24584 | tf_op jit(solution)/shard_map/ppermute | solution.py:412
  64.2 25.9 %collective-permute-start.28 = (bf16[64,5120]{1,0:T(8,128)(2,1)S(1)}, bf16[64,5120]{1,0:T(8,128)(2,1)S(1)}, u32[]{:S(2)}, u32[]{:S(2)}) collective-permute-start(bf16[64,5120]{1,0:T(8,128)(2,1)S(1)} %get-tuple-element.72.refs_6_), channel_id=1, source_target_pairs={{0,6},{1,3},{2,4},{3,1},{4,2},{5,7},{6,0},{7,5},{8,14},{9,11},{10,... | collective-permute-start | bytes 1966088 | tf_op jit(solution)/shard_map/ppermute | solution.py:388
  66.0 6.8 %collective-permute-start.17 = (bf16[2,64,640]{2,1,0:T(8,128)(2,1)S(1)}, bf16[2,64,640]{2,1,0:T(8,128)(2,1)S(1)}, u32[]{:S(2)}, u32[]{:S(2)}) collective-permute-start(bf16[2,64,640]{2,1,0:T(8,128)(2,1)S(1)} %get-tuple-element.76), channel_id=1, source_target_pairs={{0,8},{1,9},{2,10},{3,11},{4,12},{5,13},{6,14},{7,15},{8,0},{9,1},... | collective-permute-start | bytes 491528 | tf_op jit(solution)/shard_map/ppermute | solution.py:388
  72.8 12.4 %collective-permute-start.19 = (f32[1,64,640]{2,1,0:T(8,128)S(1)}, f32[1,64,640]{2,1,0:T(8,128)S(1)}, u32[]{:S(2)}, u32[]{:S(2)}) collective-permute-start(f32[1,64,640]{2,1,0:T(8,128)S(1)} %get-tuple-element.78.refs_6_.refs_0_), channel_id=1, source_target_pairs={{16,0},{32,16},{48,32},{64,48},{80,64},{96,80},{112,96},{17,1},{33... | collective-permute-start | bytes 491528 | tf_op jit(solution)/shard_map/ppermute | solution.py:412
  75.5 8.4 %collective-permute-start.20 = (bf16[1,64,640]{2,1,0:T(8,128)(2,1)S(1)}, bf16[1,64,640]{2,1,0:T(8,128)(2,1)S(1)}, u32[]{:S(2)}, u32[]{:S(2)}) collective-permute-start(bf16[1,64,640]{2,1,0:T(8,128)(2,1)S(1)} %get-tuple-element.80), channel_id=1, source_target_pairs={{16,6},{17,3},{18,4},{19,1},{20,2},{21,7},{22,0},{23,5},{24,14},{2... | collective-permute-start | bytes 245768 | tf_op jit(solution)/shard_map/ppermute | solution.py:420
  79.5 5.7 %collective-permute-start.18 = (bf16[1,64,640]{2,1,0:T(8,128)(2,1)S(1)}, bf16[1,64,640]{2,1,0:T(8,128)(2,1)S(1)}, u32[]{:S(2)}, u32[]{:S(2)}) collective-permute-start(bf16[1,64,640]{2,1,0:T(8,128)(2,1)S(1)} %get-tuple-element.80), channel_id=1, source_target_pairs={{0,6},{1,3},{2,4},{3,1},{4,2},{5,7},{6,0},{7,5},{8,14},{9,11},{10,... | collective-permute-start | bytes 245768 | tf_op jit(solution)/shard_map/ppermute | solution.py:388
  85.3 7.0 %collective-permute-start.23 = (bf16[2,64,640]{2,1,0:T(8,128)(2,1)S(1)}, bf16[2,64,640]{2,1,0:T(8,128)(2,1)S(1)}, u32[]{:S(2)}, u32[]{:S(2)}) collective-permute-start(bf16[2,64,640]{2,1,0:T(8,128)(2,1)S(1)} %chunk_pair.1.refs_2_.refs_3_), channel_id=1, source_target_pairs={{0,6},{1,3},{2,4},{3,1},{4,2},{5,7},{6,0},{7,5},{8,14},{9,11},{10,... | collective-permute-start | bytes 491528 | tf_op jit(solution)/shard_map/ppermute | solution.py:388
  87.1 5.7 %collective-permute-start.22 = (bf16[2,64,640]{2,1,0:T(8,128)(2,1)S(1)}, bf16[2,64,640]{2,1,0:T(8,128)(2,1)S(1)}, u32[]{:S(2)}, u32[]{:S(2)}) collective-permute-start(bf16[2,64,640]{2,1,0:T(8,128)(2,1)S(1)} %chunk_pair.1.refs_2_.refs_3_), channel_id=1, source_target_pairs={{0,2},{1,7},{2,0},{3,5},{4,6},{5,3},{6,4},{7,1},{8,10},{9,15},{10,... | collective-permute-start | bytes 491528 | tf_op jit(solution)/shard_map/ppermute | solution.py:388
  87.1 8.1 %collective-permute-start.21 = (bf16[2,64,640]{2,1,0:T(8,128)(2,1)S(1)}, bf16[2,64,640]{2,1,0:T(8,128)(2,1)S(1)}, u32[]{:S(2)}, u32[]{:S(2)}) collective-permute-start(bf16[2,64,640]{2,1,0:T(8,128)(2,1)S(1)} %chunk_pair.1.refs_2_.refs_3_), channel_id=1, source_target_pairs={{0,4},{1,5},{2,6},{3,7},{4,0},{5,1},{6,2},{7,3},{8,12},{9,13},{10,... | collective-permute-start | bytes 491528 | tf_op jit(solution)/shard_map/ppermute | solution.py:388
  90.2 8.7 %collective-permute-start.29 = (bf16[32,5120]{1,0:T(8,128)(2,1)S(1)}, bf16[32,5120]{1,0:T(8,128)(2,1)S(1)}, u32[]{:S(2)}, u32[]{:S(2)}) collective-permute-start(bf16[32,5120]{1,0:T(8,128)(2,1)S(1)} %get-tuple-element.84), channel_id=1, source_target_pairs={{0,8},{1,9},{2,10},{3,11},{4,12},{5,13},{6,14},{7,15},{8,0},{9,1},... | collective-permute-start | bytes 983048 | tf_op jit(solution)/shard_map/ppermute | solution.py:388
  92.2 2.9 %collective-permute-start.27 = (bf16[2,64,640]{2,1,0:T(8,128)(2,1)S(1)}, bf16[2,64,640]{2,1,0:T(8,128)(2,1)S(1)}, u32[]{:S(2)}, u32[]{:S(2)}) collective-permute-start(bf16[2,64,640]{2,1,0:T(8,128)(2,1)S(1)} %chunk_pair.1.refs_2_.refs_3_), channel_id=1, source_target_pairs={{0,1},{1,0},{2,3},{3,2},{4,5},{5,4},{6,7},{7,6},{8,9},{9,8},{10,11... | collective-permute-start | bytes 491528 | tf_op jit(solution)/shard_map/ppermute | solution.py:388
  92.3 2.8 %collective-permute-start.26 = (bf16[2,64,640]{2,1,0:T(8,128)(2,1)S(1)}, bf16[2,64,640]{2,1,0:T(8,128)(2,1)S(1)}, u32[]{:S(2)}, u32[]{:S(2)}) collective-permute-start(bf16[2,64,640]{2,1,0:T(8,128)(2,1)S(1)} %collective-permute-done.23.refs_2_), channel_id=1, source_target_pairs={{0,1},{1,0},{2,3},{3,2},{4,5},{5,4},{6,7},{7,6},{8,9},{9,8},{10,11... | collective-permute-start | bytes 491528 | tf_op jit(solution)/shard_map/ppermute | solution.py:388
  92.7 2.4 %collective-permute-start.25 = (bf16[2,64,640]{2,1,0:T(8,128)(2,1)S(1)}, bf16[2,64,640]{2,1,0:T(8,128)(2,1)S(1)}, u32[]{:S(2)}, u32[]{:S(2)}) collective-permute-start(bf16[2,64,640]{2,1,0:T(8,128)(2,1)S(1)} %collective-permute-done.22.refs_1_), channel_id=1, source_target_pairs={{0,1},{1,0},{2,3},{3,2},{4,5},{5,4},{6,7},{7,6},{8,9},{9,8},{10,11... | collective-permute-start | bytes 491528 | tf_op jit(solution)/shard_map/ppermute | solution.py:388
  95.1 1.4 %collective-permute-start.24 = (bf16[2,64,640]{2,1,0:T(8,128)(2,1)S(1)}, bf16[2,64,640]{2,1,0:T(8,128)(2,1)S(1)}, u32[]{:S(2)}, u32[]{:S(2)}) collective-permute-start(bf16[2,64,640]{2,1,0:T(8,128)(2,1)S(1)} %collective-permute-done.21.refs_0_), channel_id=1, source_target_pairs={{0,1},{1,0},{2,3},{3,2},{4,5},{5,4},{6,7},{7,6},{8,9},{9,8},{10,11... | collective-permute-start | bytes 491528 | tf_op jit(solution)/shard_map/ppermute | solution.py:388

commit v4 on v3

--- a/solution.py
+++ b/solution.py
@@ -190,12 +190,19 @@
     return whole(kernel, shapes, "input_grad_sum", (kept, come), deps)
 
 
-def chunk_pair(half, come, ahead, ahead_far, deps):
-    def kernel(a, b, c, d, out):
-        out[0:1] = (a[...] + b[...].astype(F32)).astype(BF)
-        out[1:2] = (c[...] + d[...].astype(F32)).astype(BF)
-
-    return whole(kernel, [shape(2, R, TILE, dtype=BF)], "chunk_pair", (half, come, ahead, ahead_far), deps)[0]
+def chunk_pair(right, right_next, deps):
+    def kernel(a, b, out):
+        out[0:1] = a[...]
+        out[1:2] = b[...]
+
+    return whole(kernel, [shape(2, R, TILE, dtype=BF)], "chunk_pair", (right, right_next), deps)[0]
+
+
+def right_last(kept, come, deps):
+    def kernel(kept_ref, come_ref, out):
+        out[...] = (kept_ref[...] + come_ref[...].astype(F32)).astype(BF)
+
+    return whole(kernel, [shape(1, R, TILE, dtype=BF)], "right_sum", (kept, come), deps)[0]
 
 
 def copied_whole(value, deps, flops=1000):
@@ -412,14 +419,6 @@
     return lax.ppermute(value, "section", [(s, s - 1) for s in range(1, 8)])
 
 
-def to_previous_second(value):
-    pairs = []
-    for s in range(1, 8):
-        for i in range(16):
-            pairs.append((s * 16 + i, (s - 1) * 16 + (i ^ (2 * (3 - 2 * (i % 2))))))
-    return lax.ppermute(value, ("section", "fsdp"), pairs)
-
-
 def on_device(activations, gate_preact, hidden_grad, up_weight, resid_grad, feedback, start_basis):
     acts, resid, fb = activations[0], resid_grad[0], feedback[0]
     basis_t = jnp.swapaxes(start_basis[0], 0, 1)
@@ -430,10 +429,11 @@
     unit, ordered, raw = unit_call(gate_preact[0], hidden_grad[0], weight, basis_t, resid, fb, ())
 
     come = to_core(raw)
-    sent_first, sent_second = stacked((acts_y,), (raw, moved_second)), stacked((acts_y, moved_first), (raw, moved_second))
-    gone_first, gone_second = to_first(sent_first), to_second(sent_second)
     *parts, token = partial_call(ordered, weight, 0, (), (raw,))
-    raw = added(raw, come, (token,))
+    raw = added(raw, come, (token, moved_first, moved_second))
+    late = (raw,)
+    gone_first = to_first(stacked((acts_y,), late))
+    gone_second = to_second(stacked((acts_y, moved_first), late))
     come = to_y(raw)
     *parts, token = partial_call(ordered, weight, 1, parts, (raw,))
     raw = added(raw, come, (token,))
@@ -465,13 +465,14 @@
     grad, token = grad_call(tokens, ordered, 1, (grad,), (send,))
     grad, token = grad_call(tokens, ordered, 2, (grad,), (token,))
     send, kept = right_step(kept, come, (token,))
-    come, ahead, ahead_far = to_second(send), to_previous(kept), to_previous_second(send)
+    come = to_second(send)
     weight_grad, token = grad_call(tokens, ordered, 3, (grad,), (kept,))
-    both = chunk_pair(kept, come, ahead, ahead_far, (token,))
-    send, mine = grad_step(grad_kept, grad_second, (both,))
+    right = right_last(kept, come, (token,))
+    right_next = to_previous(right)
+    send, mine = grad_step(grad_kept, grad_second, (right,))
     partner = to_y(send)
-    both_first, both_second, both_far = to_first(both), to_second(both), to_far(both)
-    own_chunks = [both_far, both_first, both_second, both]
+    both = chunk_pair(right, right_next, (send,))
+    own_chunks = [to_far(both), to_first(both), to_second(both), both]
     chunks = own_chunks + [to_core(value) for value in own_chunks]
 
     new_feedback, received = final_call(chunks, left, left_next, resid, fb, mine, partner)

time: 101 us -> 98.4 us (0.974)
  starting transfers between devices: 36.2 us -> 33.7 us
    ppermute x1 -> x0, starting transfers between devices: 3.96 us -> none  [to_previous_second(): return lax.ppermute(value, ('section', 'fsdp'), pairs)]
    ppermute x2, waiting for transfers between devices: 0.68 us -> 4.36 us  [to_previous(): return lax.ppermute(value, 'section', [(s, s - 1) for s in range(1, 8)])]
    ppermute x27, waiting for transfers between devices: 28 us -> 24.7 us  [sent(): return lax.ppermute(value, 'fsdp', pairs)]
    ppermute x27, starting transfers between devices: 27.1 us -> 28.8 us  [sent(): return lax.ppermute(value, 'fsdp', pairs)]
    pallas_call x19 -> x20, Pallas kernels: 12.9 us -> 12.8 us  [whole(): pl.pallas_call(body, in_specs=(in_specs or [VMEM] * count) + [ANY] * len(...]
  transfers between devices with their start and end apart: 30 -> 29, of which waited for: 14 -> 13; matrix products, arithmetic and copies ran while one was open for 0% -> 0% of each run, Pallas kernels for 31% -> 32%
where the time goes in v4:
time: 98.4 us; the launch traced here: 98.2 us
  starting transfers between devices  33.7 us (34%)
  Pallas kernels  33.4 us (34%)
  waiting for transfers between devices  29.1 us (30%)
  local copies, waits for them, and re-layouts  1.04 us (1%)
  between operations  1.02 us (1%)
    ppermute x27, starting transfers between devices, sent(): return lax.ppermute(value, 'fsdp', pairs)  28.8 us
    ppermute x27, waiting for transfers between devices, sent(): return lax.ppermute(value, 'fsdp', pairs)  24.7 us
    pallas_call x20, Pallas kernels, whole(): pl.pallas_call(body, in_specs=(in_specs or [VMEM] * count) + [ANY] * len(...  12.8 us
    pallas_call x4, Pallas kernels, grad_call(): pl.pallas_call(kernel, in_specs=[VMEM] * (ins + 1) + [ANY] * count, out_s...  10.4 us
    pallas_call x4, Pallas kernels, partial_call(): pl.pallas_call(kernel, grid=(2,), in_specs=[VMEM, VMEM] + [ANY] * count,...  8.61 us
    ppermute x2, starting transfers between devices, to_previous(): return lax.ppermute(value, 'section', [(s, s - 1) for s in range(1, 8)])  4.84 us
    ppermute x2, waiting for transfers between devices, to_previous(): return lax.ppermute(value, 'section', [(s, s - 1) for s in range(1, 8)])  4.36 us
  transfers between devices with their start and end apart: 29, of which 13 were waited for; matrix products, arithmetic and copies ran while one was open for 0% of the time, Pallas kernels for 32%

profile of v4, /device:TPU:96, one launch (start us, length us, event | category | flops | bytes accessed | tf_op | source)
XLA Modules:
  0.0 98.2 jit_solution(6082393927776755784)
XLA Ops:
  0.6 0.0 copy-start.3
  0.6 1.0 copy-done.3
  1.7 3.3 %collective-permute-start.2 = (bf16[32,5120]{1,0:T(8,128)(2,1)S(1)}, bf16[32,5120]{1,0:T(8,128)(2,1)S(1)}, u32[]{:S(2)}, u32[]{:S(2)}) collective-permute-start(bf16[32,5120]{1,0:T(8,128)(2,1)S(1)} %copied.1), channel_id=1, source_target_pairs={{0,8},{1,9},{2,10},{3,11},{4,12},{5,13},{6,14},{7,15},{8,0},{9,1},... | collective-permute-start | bytes 983048 | tf_op jit(solution)/shard_map/ppermute | solution.py:395
  4.9 2.8 %collective-permute-start.1 = (bf16[32,5120]{1,0:T(8,128)(2,1)S(1)}, bf16[32,5120]{1,0:T(8,128)(2,1)S(1)}, u32[]{:S(2)}, u32[]{:S(2)}) collective-permute-start(bf16[32,5120]{1,0:T(8,128)(2,1)S(1)} %copied.1), channel_id=1, source_target_pairs={{0,6},{1,3},{2,4},{3,1},{4,2},{5,7},{6,0},{7,5},{8,14},{9,11},{10,... | collective-permute-start | bytes 983048 | tf_op jit(solution)/shard_map/ppermute | solution.py:395
  7.7 0.2 collective-permute-start
  8.0 3.9 %unit_and_raw.1 = (bf16[512,896]{1,0:T(8,128)(2,1)S(1)}, bf16[512,896]{1,0:T(8,128)(2,1)S(1)}, f32[64,512]{1,0:T(8,128)S(1)}) custom-call(bf16[512,896]{1,0:T(8,128)(2,1)S(1)} %bitcast.27, bf16[512,896]{1,0:T(8,128)(2,1)S(1)} %bitcast.28, bf16[5120,896]{1,0:T(8,128)(2,1)S(1)} %bitcast.12, f32[64,5120]{1,0:T(8,128)S(1)} %bitcast.26, ...), custom_call_target="tpu_custom_call" | custom-call | flops 20000000000 | bytes 1000 | tf_op jit(solution)/shard_map/unit_and_raw/pallas_call | solution.py:105
  11.9 0.1 collective-permute-start.3
  12.0 2.2 %input_grad_part.4 = (bf16[256,5120]{1,0:T(8,128)(2,1)S(1)}, f32[256,5120]{1,0:T(8,128)S(1)}, f32[8,128]{1,0:T(8,128)S(1)}) custom-call(bf16[512,896]{1,0:T(8,128)(2,1)S(1)} %get-tuple-element.46.unit.refs_4_, bf16[5120,896]{1,0:T(8,128)(2,1)S(1)} %bitcast.13, f32[64,512]{1,0:T(8,128)S(1)} %get-tuple-element.45.refs_0_), custom_call_target="tpu_custom_call" | custom-call | flops 1000 | bytes 1000 | tf_op jit(solution)/shard_map/input_grad_part/pallas_call | solution.py:143
  14.2 2.4 %collective-permute-done.1.refs_4_.refs_2_ = bf16[32,5120]{1,0:T(8,128)(2,1)S(1)} collective-permute-done((bf16[32,5120]{1,0:T(8,128)(2,1)S(1)}, bf16[32,5120]{1,0:T(8,128)(2,1)S(1)}, u32[]{:S(2)}, u32[]{:S(2)}) %collective-permute-start.1) | collective-permute-done | bytes 327712 | tf_op jit(solution)/shard_map/ppermute | solution.py:395
  16.6 0.0 collective-permute-done.2.refs_0_
  16.6 2.2 %collective-permute-start.4 = (bf16[64,5120]{1,0:T(8,128)(2,1)S(1)}, bf16[64,5120]{1,0:T(8,128)(2,1)S(1)}, u32[]{:S(2)}, u32[]{:S(2)}) collective-permute-start(bf16[64,5120]{1,0:T(8,128)(2,1)S(1)} %stack.5), channel_id=1, source_target_pairs={{0,6},{1,3},{2,4},{3,1},{4,2},{5,7},{6,0},{7,5},{8,14},{9,11},{10,... | collective-permute-start | bytes 1966088 | tf_op jit(solution)/shard_map/ppermute | solution.py:395
  18.8 0.1 collective-permute-start.7
  18.9 0.5 collective-permute-start.5
  19.4 2.1 %input_grad_part.5 = (bf16[256,5120]{1,0:T(8,128)(2,1)S(1)}, f32[256,5120]{1,0:T(8,128)S(1)}, f32[8,128]{1,0:T(8,128)S(1)}) custom-call(bf16[512,896]{1,0:T(8,128)(2,1)S(1)} %get-tuple-element.46.unit.refs_4_, bf16[5120,896]{1,0:T(8,128)(2,1)S(1)} %bitcast.14, ...), custom_call_target="tpu_custom_call", output_to_operand_aliasing={{0}: (2, {}), {1}: (3, {})} | custom-call | flops 1000 | bytes 1000 | tf_op jit(solution)/shard_map/input_grad_part/pallas_call | solution.py:143
  21.5 3.9 %collective-permute-done.5.refs_1_ = f32[64,512]{1,0:T(8,128)S(1)} collective-permute-done((f32[64,512]{1,0:T(8,128)S(1)}, f32[64,512]{1,0:T(8,128)S(1)}, u32[]{:S(2)}, u32[]{:S(2)}) %collective-permute-start.5) | collective-permute-done | bytes 131104 | tf_op jit(solution)/shard_map/ppermute | solution.py:395
  25.5 2.0 %collective-permute-start.6 = (f32[64,512]{1,0:T(8,128)S(1)}, f32[64,512]{1,0:T(8,128)S(1)}, u32[]{:S(2)}, u32[]{:S(2)}) collective-permute-start(f32[64,512]{1,0:T(8,128)S(1)} %raw_sum.4.refs_2_.refs_0_), channel_id=1, source_target_pairs={{0,2},{1,7},{2,0},{3,5},{4,6},{5,3},{6,4},{7,1},{8,10},{9,15},{10,... | collective-permute-start | bytes 393224 | tf_op jit(solution)/shard_map/ppermute | solution.py:395
  27.5 2.1 %input_grad_part.6 = (bf16[256,5120]{1,0:T(8,128)(2,1)S(1)}, f32[256,5120]{1,0:T(8,128)S(1)}, f32[8,128]{1,0:T(8,128)S(1)}) custom-call(bf16[512,896]{1,0:T(8,128)(2,1)S(1)} %get-tuple-element.46.unit.refs_4_, bf16[5120,896]{1,0:T(8,128)(2,1)S(1)} %bitcast.15, ...), custom_call_target="tpu_custom_call", output_to_operand_aliasing={{0}: (2, {}), {1}: (3, {})} | custom-call | flops 1000 | bytes 1000 | tf_op jit(solution)/shard_map/input_grad_part/pallas_call | solution.py:143
  29.7 2.2 %input_grad_part.7 = (bf16[256,5120]{1,0:T(8,128)(2,1)S(1)}, f32[256,5120]{1,0:T(8,128)S(1)}, f32[8,128]{1,0:T(8,128)S(1)}) custom-call(bf16[512,896]{1,0:T(8,128)(2,1)S(1)} %get-tuple-element.46.unit.refs_4_, bf16[5120,896]{1,0:T(8,128)(2,1)S(1)} %bitcast.16, ...), custom_call_target="tpu_custom_call", output_to_operand_aliasing={{0}: (2, {}), {1}: (3, {})} | custom-call | flops 1000 | bytes 1000 | tf_op jit(solution)/shard_map/input_grad_part/pallas_call | solution.py:143
  31.8 0.0 collective-permute-done.6.refs_1_
  31.8 0.0 collective-permute-done.7.refs_3_.refs_1_
  31.8 0.6 collective-permute-done.4.refs_4_
  32.5 0.0 copy-start.4
  32.5 0.2 stack.9
  32.7 0.1 collective-permute-start.12
  32.8 0.1 collective-permute-start.9
  32.9 1.8 %collective-permute-start.10 = (f32[64,512]{1,0:T(8,128)S(1)}, f32[64,512]{1,0:T(8,128)S(1)}, u32[]{:S(2)}, u32[]{:S(2)}) collective-permute-start(f32[64,512]{1,0:T(8,128)S(1)} %raw_sum.5.refs_4_.refs_1_.refs_0_), channel_id=1, source_target_pairs={{0,6},{1,3},{2,4},{3,1},{4,2},{5,7},{6,0},{7,5},{8,14},{9,11},{10,... | collective-permute-start | bytes 393224 | tf_op jit(solution)/shard_map/ppermute | solution.py:395
  34.7 0.1 stack.7.refs_2_
  34.8 0.1 collective-permute-start.8
  34.9 5.6 %collective-permute-done.10.refs_4_.refs_2_.refs_1_ = f32[64,512]{1,0:T(8,128)S(1)} collective-permute-done((f32[64,512]{1,0:T(8,128)S(1)}, f32[64,512]{1,0:T(8,128)S(1)}, u32[]{:S(2)}, u32[]{:S(2)}) %collective-permute-start.10) | collective-permute-done | bytes 131104 | tf_op jit(solution)/shard_map/ppermute | solution.py:395
  40.5 0.9 collective-permute-done.9.refs_3_
  41.4 0.1 stack.8.refs_3_
  41.5 0.7 collective-permute-start.11
  42.1 0.4 input_grad_sum.3
  42.6 0.3 collective-permute-start.14
  42.8 2.6 %left_factor.1 = (bf16[128,896]{1,0:T(8,128)(2,1)S(1)}, f32[32,64]{1,0:T(8,128)S(1)}, f32[64,32]{1,0:T(8,128)S(1)}) custom-call(f32[64,512]{1,0:T(8,128)S(1)} %raw_sum.5.refs_4_.refs_1_.refs_0_, f32[64,512]{1,0:T(8,128)S(1)} %collective-permute-done.10.refs_4_.refs_2_.refs_1_, bf16[512,896]{1,0:T(8,128)(2,1)S(1)} %get-tuple-element.57.refs_2_, ...), custom_call_target="tpu_custom_call" | custom-call | flops 1000 | bytes 1000 | tf_op jit(solution)/shard_map/left_factor/pallas_call | solution.py:105
  45.5 4.7 %right_factor.1 = (f32[4,64,640]{2,1,0:T(8,128)S(1)}, bf16[4,64,640]{2,1,0:T(8,128)(2,1)S(1)}) custom-call(bf16[128,896]{1,0:T(8,128)(2,1)S(1)} %get-tuple-element.61.refs_0_, f32[64,32]{1,0:T(8,128)S(1)} %get-tuple-element.62.refs_1_, bf16[5120,896]{1,0:T(8,128)(2,1)S(1)} %bitcast.17, bf16[32,5120]{1,0:T(8,128)(2,1)S(1)} %bitcast.22, f32[32,5120]{1,0:T(8,128)S(1)} %bitcast.19), custom_call_target="tpu_custom_call" | custom-call | flops 1000 | bytes 1000 | tf_op jit(solution)/shard_map/right_factor/pallas_call | solution.py:105
  50.2 1.3 %collective-permute-start.13 = (bf16[4,64,640]{2,1,0:T(8,128)(2,1)S(1)}, bf16[4,64,640]{2,1,0:T(8,128)(2,1)S(1)}, u32[]{:S(2)}, u32[]{:S(2)}) collective-permute-start(bf16[4,64,640]{2,1,0:T(8,128)(2,1)S(1)} %get-tuple-element.64), channel_id=1, source_target_pairs={{0,1},{1,0},{2,3},{3,2},{4,5},{5,4},{6,7},{7,6},{8,9},{9,8},{10,11... | collective-permute-start | bytes 983048 | tf_op jit(solution)/shard_map/ppermute | solution.py:395
  51.6 1.3 %collective-permute-done.13.refs_1_ = bf16[4,64,640]{2,1,0:T(8,128)(2,1)S(1)} collective-permute-done((bf16[4,64,640]{2,1,0:T(8,128)(2,1)S(1)}, bf16[4,64,640]{2,1,0:T(8,128)(2,1)S(1)}, u32[]{:S(2)}, u32[]{:S(2)}) %collective-permute-start.13) | collective-permute-done | bytes 327712 | tf_op jit(solution)/shard_map/ppermute | solution.py:395
  52.8 0.1 right_sum.4
  52.9 1.2 %collective-permute-start.15 = (bf16[2,64,640]{2,1,0:T(8,128)(2,1)S(1)}, bf16[2,64,640]{2,1,0:T(8,128)(2,1)S(1)}, u32[]{:S(2)}, u32[]{:S(2)}) collective-permute-start(bf16[2,64,640]{2,1,0:T(8,128)(2,1)S(1)} %get-tuple-element.68), channel_id=1, source_target_pairs={{0,2},{1,7},{2,0},{3,5},{4,6},{5,3},{6,4},{7,1},{8,10},{9,15},{10,... | collective-permute-start | bytes 491528 | tf_op jit(solution)/shard_map/ppermute | solution.py:395
  54.1 2.4 %collective-permute-start.16 = (f32[32,64]{1,0:T(8,128)S(1)}, f32[32,64]{1,0:T(8,128)S(1)}, u32[]{:S(2)}, u32[]{:S(2)}) collective-permute-start(f32[32,64]{1,0:T(8,128)S(1)} %get-tuple-element.69.refs_8_), channel_id=1, source_target_pairs={{16,0},{32,16},{48,32},{64,48},{80,64},{96,80},{112,96},{17,1},{33... | collective-permute-start | bytes 24584 | tf_op jit(solution)/shard_map/ppermute | solution.py:419
  56.6 2.6 %weight_grad_part.4 = (bf16[5120,896]{1,0:T(8,128)(2,1)}, f32[8,128]{1,0:T(8,128)S(1)}) custom-call(bf16[128,5120]{1,0:T(8,128)(2,1)S(1)} %collective-permute-done.8.refs_0_, bf16[128,5120]{1,0:T(8,128)(2,1)S(1)} %collective-permute-done.11.refs_1_, bf16[128,5120]{1,0:T(8,128)(2,1)S(1)} %stack.7.refs_2_, bf16[128,5120]{1,0:T(8,128)(2,1)S(1)} %stack.8.refs_3_, ...), custom_call_target="tpu_custom_call" | custom-call | flops 1000 | bytes 1000 | tf_op jit(solution)/shard_map/weight_grad_part/pallas_call | solution.py:345
  59.2 0.6 collective-permute-done.16.refs_2_.refs_9_
  59.7 2.5 %collective-permute-done.15.refs_1_ = bf16[2,64,640]{2,1,0:T(8,128)(2,1)S(1)} collective-permute-done((bf16[2,64,640]{2,1,0:T(8,128)(2,1)S(1)}, bf16[2,64,640]{2,1,0:T(8,128)(2,1)S(1)}, u32[]{:S(2)}, u32[]{:S(2)}) %collective-permute-start.15) | collective-permute-done | bytes 163872 | tf_op jit(solution)/shard_map/ppermute | solution.py:395
  62.2 0.3 input_grad_sum.4
  62.6 1.6 %collective-permute-start.20 = (bf16[64,5120]{1,0:T(8,128)(2,1)S(1)}, bf16[64,5120]{1,0:T(8,128)(2,1)S(1)}, u32[]{:S(2)}, u32[]{:S(2)}) collective-permute-start(bf16[64,5120]{1,0:T(8,128)(2,1)S(1)} %get-tuple-element.72.refs_6_), channel_id=1, source_target_pairs={{0,6},{1,3},{2,4},{3,1},{4,2},{5,7},{6,0},{7,5},{8,14},{9,11},{10,... | collective-permute-start | bytes 1966088 | tf_op jit(solution)/shard_map/ppermute | solution.py:395
  64.2 1.7 %collective-permute-start.17 = (bf16[2,64,640]{2,1,0:T(8,128)(2,1)S(1)}, bf16[2,64,640]{2,1,0:T(8,128)(2,1)S(1)}, u32[]{:S(2)}, u32[]{:S(2)}) collective-permute-start(bf16[2,64,640]{2,1,0:T(8,128)(2,1)S(1)} %get-tuple-element.76), channel_id=1, source_target_pairs={{0,8},{1,9},{2,10},{3,11},{4,12},{5,13},{6,14},{7,15},{8,0},{9,1},... | collective-permute-start | bytes 491528 | tf_op jit(solution)/shard_map/ppermute | solution.py:395
  65.9 2.6 %weight_grad_part.5 = (bf16[5120,896]{1,0:T(8,128)(2,1)}, f32[8,128]{1,0:T(8,128)S(1)}) custom-call(bf16[128,5120]{1,0:T(8,128)(2,1)S(1)} %collective-permute-done.8.refs_0_, bf16[128,5120]{1,0:T(8,128)(2,1)S(1)} %collective-permute-done.11.refs_1_, bf16[128,5120]{1,0:T(8,128)(2,1)S(1)} %stack.7.refs_2_, ...), custom_call_target="tpu_custom_call", output_to_operand_aliasing={{0}: (5, {})} | custom-call | flops 1000 | bytes 1000 | tf_op jit(solution)/shard_map/weight_grad_part/pallas_call | solution.py:345
  68.5 2.6 %weight_grad_part.6 = (bf16[5120,896]{1,0:T(8,128)(2,1)}, f32[8,128]{1,0:T(8,128)S(1)}) custom-call(bf16[128,5120]{1,0:T(8,128)(2,1)S(1)} %collective-permute-done.8.refs_0_, bf16[128,5120]{1,0:T(8,128)(2,1)S(1)} %collective-permute-done.11.refs_1_, bf16[128,5120]{1,0:T(8,128)(2,1)S(1)} %stack.7.refs_2_, ...), custom_call_target="tpu_custom_call", output_to_operand_aliasing={{0}: (5, {})} | custom-call | flops 1000 | bytes 1000 | tf_op jit(solution)/shard_map/weight_grad_part/pallas_call | solution.py:345
  71.1 1.7 %collective-permute-start.18 = (bf16[1,64,640]{2,1,0:T(8,128)(2,1)S(1)}, bf16[1,64,640]{2,1,0:T(8,128)(2,1)S(1)}, u32[]{:S(2)}, u32[]{:S(2)}) collective-permute-start(bf16[1,64,640]{2,1,0:T(8,128)(2,1)S(1)} %get-tuple-element.80), channel_id=1, source_target_pairs={{0,6},{1,3},{2,4},{3,1},{4,2},{5,7},{6,0},{7,5},{8,14},{9,11},{10,... | collective-permute-start | bytes 245768 | tf_op jit(solution)/shard_map/ppermute | solution.py:395
  72.8 2.6 %weight_grad_part.7 = (bf16[5120,896]{1,0:T(8,128)(2,1)}, f32[8,128]{1,0:T(8,128)S(1)}) custom-call(bf16[128,5120]{1,0:T(8,128)(2,1)S(1)} %collective-permute-done.8.refs_0_, bf16[128,5120]{1,0:T(8,128)(2,1)S(1)} %collective-permute-done.11.refs_1_, bf16[128,5120]{1,0:T(8,128)(2,1)S(1)} %stack.7.refs_2_, ...), custom_call_target="tpu_custom_call", output_to_operand_aliasing={{0}: (5, {})} | custom-call | flops 1000 | bytes 1000 | tf_op jit(solution)/shard_map/weight_grad_part/pallas_call | solution.py:345
  75.4 1.4 %collective-permute-done.18.refs_1_ = bf16[1,64,640]{2,1,0:T(8,128)(2,1)S(1)} collective-permute-done((bf16[1,64,640]{2,1,0:T(8,128)(2,1)S(1)}, bf16[1,64,640]{2,1,0:T(8,128)(2,1)S(1)}, u32[]{:S(2)}, u32[]{:S(2)}) %collective-permute-start.18) | collective-permute-done | bytes 81952 | tf_op jit(solution)/shard_map/ppermute | solution.py:395
  76.9 2.4 %collective-permute-start.19 = (bf16[1,64,640]{2,1,0:T(8,128)(2,1)S(1)}, bf16[1,64,640]{2,1,0:T(8,128)(2,1)S(1)}, u32[]{:S(2)}, u32[]{:S(2)}) collective-permute-start(bf16[1,64,640]{2,1,0:T(8,128)(2,1)S(1)} %right_sum.7.refs_2_.refs_0_), channel_id=1, source_target_pairs={{16,0},{32,16},{48,32},{64,48},{80,64},{96,80},{112,96},{17,1},{33... | collective-permute-start | bytes 245768 | tf_op jit(solution)/shard_map/ppermute | solution.py:419
  79.3 0.1 input_grad_sum.5
  79.4 3.8 %collective-permute-done.19.refs_1_ = bf16[1,64,640]{2,1,0:T(8,128)(2,1)S(1)} collective-permute-done((bf16[1,64,640]{2,1,0:T(8,128)(2,1)S(1)}, bf16[1,64,640]{2,1,0:T(8,128)(2,1)S(1)}, u32[]{:S(2)}, u32[]{:S(2)}) %collective-permute-start.19) | collective-permute-done | bytes 81952 | tf_op jit(solution)/shard_map/ppermute | solution.py:419
  83.2 1.7 %collective-permute-start.23 = (bf16[2,64,640]{2,1,0:T(8,128)(2,1)S(1)}, bf16[2,64,640]{2,1,0:T(8,128)(2,1)S(1)}, u32[]{:S(2)}, u32[]{:S(2)}) collective-permute-start(bf16[2,64,640]{2,1,0:T(8,128)(2,1)S(1)} %chunk_pair.1.refs_3_), channel_id=1, source_target_pairs={{0,6},{1,3},{2,4},{3,1},{4,2},{5,7},{6,0},{7,5},{8,14},{9,11},{10,... | collective-permute-start | bytes 491528 | tf_op jit(solution)/shard_map/ppermute | solution.py:395
  85.0 3.1 %collective-permute-start.21 = (bf16[2,64,640]{2,1,0:T(8,128)(2,1)S(1)}, bf16[2,64,640]{2,1,0:T(8,128)(2,1)S(1)}, u32[]{:S(2)}, u32[]{:S(2)}) collective-permute-start(bf16[2,64,640]{2,1,0:T(8,128)(2,1)S(1)} %chunk_pair.1.refs_3_), channel_id=1, source_target_pairs={{0,4},{1,5},{2,6},{3,7},{4,0},{5,1},{6,2},{7,3},{8,12},{9,13},{10,... | collective-permute-start | bytes 491528 | tf_op jit(solution)/shard_map/ppermute | solution.py:395
  88.0 1.9 %collective-permute-start.28 = (bf16[32,5120]{1,0:T(8,128)(2,1)S(1)}, bf16[32,5120]{1,0:T(8,128)(2,1)S(1)}, u32[]{:S(2)}, u32[]{:S(2)}) collective-permute-start(bf16[32,5120]{1,0:T(8,128)(2,1)S(1)} %get-tuple-element.83.refs_2_), channel_id=1, source_target_pairs={{0,8},{1,9},{2,10},{3,11},{4,12},{5,13},{6,14},{7,15},{8,0},{9,1},... | collective-permute-start | bytes 983048 | tf_op jit(solution)/shard_map/ppermute | solution.py:395
  89.9 0.5 collective-permute-start.26
  90.4 0.1 collective-permute-start.25
  90.5 2.6 %collective-permute-done.21.refs_0_ = bf16[2,64,640]{2,1,0:T(8,128)(2,1)S(1)} collective-permute-done((bf16[2,64,640]{2,1,0:T(8,128)(2,1)S(1)}, bf16[2,64,640]{2,1,0:T(8,128)(2,1)S(1)}, u32[]{:S(2)}, u32[]{:S(2)}) %collective-permute-start.21) | collective-permute-done | bytes 163872 | tf_op jit(solution)/shard_map/ppermute | solution.py:395
  93.1 1.4 %collective-permute-done.24.refs_4_ = bf16[2,64,640]{2,1,0:T(8,128)(2,1)S(1)} collective-permute-done((bf16[2,64,640]{2,1,0:T(8,128)(2,1)S(1)}, bf16[2,64,640]{2,1,0:T(8,128)(2,1)S(1)}, u32[]{:S(2)}, u32[]{:S(2)}) %collective-permute-start.24) | collective-permute-done | bytes 163872 | tf_op jit(solution)/shard_map/ppermute | solution.py:395
  94.5 2.1 %collective-permute-done.28.refs_13_ = bf16[32,5120]{1,0:T(8,128)(2,1)S(1)} collective-permute-done((bf16[32,5120]{1,0:T(8,128)(2,1)S(1)}, bf16[32,5120]{1,0:T(8,128)(2,1)S(1)}, u32[]{:S(2)}, u32[]{:S(2)}) %collective-permute-start.28) | collective-permute-done | bytes 327712 | tf_op jit(solution)/shard_map/ppermute | solution.py:395
  96.6 1.6 %feedback_and_received.1 = (f32[32,5120]{1,0:T(8,128)}, f32[32,5120]{1,0:T(8,128)}) custom-call(bf16[2,64,640]{2,1,0:T(8,128)(2,1)S(1)} %collective-permute-done.21.refs_0_, bf16[2,64,640]{2,1,0:T(8,128)(2,1)S(1)} %collective-permute-done.22.refs_1_, bf16[2,64,640]{2,1,0:T(8,128)(2,1)S(1)} %collective-permute-done.23.refs_2_, ...), custom_call_target="tpu_custom_call" | custom-call | flops 1000 | bytes 1000 | tf_op jit(solution)/shard_map/feedback_and_received/pallas_call | solution.py:379
  (40 shorter events, 0.4 us)
Async XLA Ops:
  0.6 1.0 copy-start.3
  1.6 6.3 %copy-start = (bf16[1,5120,896]{2,1,0:T(8,128)(2,1)S(1)}, bf16[1,5120,896]{2,1,0:T(8,128)(2,1)}, u32[]{:S(2)}) copy-start(bf16[1,5120,896]{2,1,0:T(8,128)(2,1)} %param.10) | copy-start | bytes 27525124
  1.6 6.3 %copy-start.1 = (f32[1,32,5120]{2,1,0:T(8,128)S(1)}, f32[1,32,5120]{2,1,0:T(8,128)}, u32[]{:S(2)}) copy-start(f32[1,32,5120]{2,1,0:T(8,128)} %param.12) | copy-start | bytes 1966084
  1.6 6.3 %copy-start.2 = (bf16[1,32,5120]{2,1,0:T(8,128)(2,1)S(1)}, bf16[1,32,5120]{2,1,0:T(8,128)(2,1)}, u32[]{:S(2)}) copy-start(bf16[1,32,5120]{2,1,0:T(8,128)(2,1)} %param.11) | copy-start | bytes 983044
  1.6 6.3 %copy-start.5 = (f32[1,5120,64]{1,2,0:T(8,128)S(1)}, f32[1,5120,64]{1,2,0:T(8,128)}, u32[]{:S(2)}) copy-start(f32[1,5120,64]{1,2,0:T(8,128)} %param.13) | copy-start | bytes 3932164
  1.6 6.3 %copy-start.6 = (bf16[1,512,896]{2,1,0:T(8,128)(2,1)S(1)}, bf16[1,512,896]{2,1,0:T(8,128)(2,1)}, u32[]{:S(2)}) copy-start(bf16[1,512,896]{2,1,0:T(8,128)(2,1)} %param.8) | copy-start | bytes 2752516
  1.6 6.3 %copy-start.7 = (bf16[1,512,896]{2,1,0:T(8,128)(2,1)S(1)}, bf16[1,512,896]{2,1,0:T(8,128)(2,1)}, u32[]{:S(2)}) copy-start(bf16[1,512,896]{2,1,0:T(8,128)(2,1)} %param.9) | copy-start | bytes 2752516
  1.7 14.9 %collective-permute-start.2 = (bf16[32,5120]{1,0:T(8,128)(2,1)S(1)}, bf16[32,5120]{1,0:T(8,128)(2,1)S(1)}, u32[]{:S(2)}, u32[]{:S(2)}) collective-permute-start(bf16[32,5120]{1,0:T(8,128)(2,1)S(1)} %copied.1), channel_id=1, source_target_pairs={{0,8},{1,9},{2,10},{3,11},{4,12},{5,13},{6,14},{7,15},{8,0},{9,1},... | collective-permute-start | bytes 983048 | tf_op jit(solution)/shard_map/ppermute | solution.py:395
  4.9 11.6 %collective-permute-start.1 = (bf16[32,5120]{1,0:T(8,128)(2,1)S(1)}, bf16[32,5120]{1,0:T(8,128)(2,1)S(1)}, u32[]{:S(2)}, u32[]{:S(2)}) collective-permute-start(bf16[32,5120]{1,0:T(8,128)(2,1)S(1)} %copied.1), channel_id=1, source_target_pairs={{0,6},{1,3},{2,4},{3,1},{4,2},{5,7},{6,0},{7,5},{8,14},{9,11},{10,... | collective-permute-start | bytes 983048 | tf_op jit(solution)/shard_map/ppermute | solution.py:395
  7.7 8.8 %collective-permute-start = (bf16[32,5120]{1,0:T(8,128)(2,1)S(1)}, bf16[32,5120]{1,0:T(8,128)(2,1)S(1)}, u32[]{:S(2)}, u32[]{:S(2)}) collective-permute-start(bf16[32,5120]{1,0:T(8,128)(2,1)S(1)} %copied.1), channel_id=1, source_target_pairs={{0,2},{1,7},{2,0},{3,5},{4,6},{5,3},{6,4},{7,1},{8,10},{9,15},{10,... | collective-permute-start | bytes 983048 | tf_op jit(solution)/shard_map/ppermute | solution.py:395
  11.9 2.3 %collective-permute-start.3 = (f32[64,512]{1,0:T(8,128)S(1)}, f32[64,512]{1,0:T(8,128)S(1)}, u32[]{:S(2)}, u32[]{:S(2)}) collective-permute-start(f32[64,512]{1,0:T(8,128)S(1)} %get-tuple-element.45.refs_0_), channel_id=1, source_target_pairs={{0,1},{1,0},{2,3},{3,2},{4,5},{5,4},{6,7},{7,6},{8,9},{9,8},{10,11... | collective-permute-start | bytes 393224 | tf_op jit(solution)/shard_map/ppermute | solution.py:395
  16.6 15.8 %collective-permute-start.4 = (bf16[64,5120]{1,0:T(8,128)(2,1)S(1)}, bf16[64,5120]{1,0:T(8,128)(2,1)S(1)}, u32[]{:S(2)}, u32[]{:S(2)}) collective-permute-start(bf16[64,5120]{1,0:T(8,128)(2,1)S(1)} %stack.5), channel_id=1, source_target_pairs={{0,6},{1,3},{2,4},{3,1},{4,2},{5,7},{6,0},{7,5},{8,14},{9,11},{10,... | collective-permute-start | bytes 1966088 | tf_op jit(solution)/shard_map/ppermute | solution.py:395
  18.8 13.0 %collective-permute-start.7 = (bf16[32,5120]{1,0:T(8,128)(2,1)S(1)}, bf16[32,5120]{1,0:T(8,128)(2,1)S(1)}, u32[]{:S(2)}, u32[]{:S(2)}) collective-permute-start(bf16[32,5120]{1,0:T(8,128)(2,1)S(1)} %stack.6), channel_id=1, source_target_pairs={{0,2},{1,7},{2,0},{3,5},{4,6},{5,3},{6,4},{7,1},{8,10},{9,15},{10,... | collective-permute-start | bytes 983048 | tf_op jit(solution)/shard_map/ppermute | solution.py:395
  18.9 6.6 %collective-permute-start.5 = (f32[64,512]{1,0:T(8,128)S(1)}, f32[64,512]{1,0:T(8,128)S(1)}, u32[]{:S(2)}, u32[]{:S(2)}) collective-permute-start(f32[64,512]{1,0:T(8,128)S(1)} %raw_sum.3.refs_2_.refs_0_.refs_1_), channel_id=1, source_target_pairs={{0,8},{1,9},{2,10},{3,11},{4,12},{5,13},{6,14},{7,15},{8,0},{9,1},... | collective-permute-start | bytes 393224 | tf_op jit(solution)/shard_map/ppermute | solution.py:395
  25.5 6.3 %collective-permute-start.6 = (f32[64,512]{1,0:T(8,128)S(1)}, f32[64,512]{1,0:T(8,128)S(1)}, u32[]{:S(2)}, u32[]{:S(2)}) collective-permute-start(f32[64,512]{1,0:T(8,128)S(1)} %raw_sum.4.refs_2_.refs_0_), channel_id=1, source_target_pairs={{0,2},{1,7},{2,0},{3,5},{4,6},{5,3},{6,4},{7,1},{8,10},{9,15},{10,... | collective-permute-start | bytes 393224 | tf_op jit(solution)/shard_map/ppermute | solution.py:395
  32.5 2.2 %copy-start.4 = (bf16[1,32,5120]{2,1,0:T(8,128)(2,1)S(1)}, bf16[1,32,5120]{2,1,0:T(8,128)(2,1)}, u32[]{:S(2)}) copy-start(bf16[1,32,5120]{2,1,0:T(8,128)(2,1)} %param.7) | copy-start | bytes 983044
  32.7 9.5 %collective-permute-start.12 = (bf16[256,5120]{1,0:T(8,128)(2,1)S(1)}, bf16[256,5120]{1,0:T(8,128)(2,1)S(1)}, u32[]{:S(2)}, u32[]{:S(2)}) collective-permute-start(bf16[256,5120]{1,0:T(8,128)(2,1)S(1)} %stack.9), channel_id=1, source_target_pairs={{0,1},{1,0},{2,3},{3,2},{4,5},{5,4},{6,7},{7,6},{8,9},{9,8},{10,11... | collective-permute-start | bytes 7864328 | tf_op jit(solution)/shard_map/ppermute | solution.py:395
  32.8 8.6 %collective-permute-start.9 = (bf16[32,5120]{1,0:T(8,128)(2,1)S(1)}, bf16[32,5120]{1,0:T(8,128)(2,1)S(1)}, u32[]{:S(2)}, u32[]{:S(2)}) collective-permute-start(bf16[32,5120]{1,0:T(8,128)(2,1)S(1)} %get-tuple-element.87.refs_2_), channel_id=1, source_target_pairs={{0,2},{1,7},{2,0},{3,5},{4,6},{5,3},{6,4},{7,1},{8,10},{9,15},{10,... | collective-permute-start | bytes 983048 | tf_op jit(solution)/shard_map/ppermute | solution.py:395
  32.9 7.6 %collective-permute-start.10 = (f32[64,512]{1,0:T(8,128)S(1)}, f32[64,512]{1,0:T(8,128)S(1)}, u32[]{:S(2)}, u32[]{:S(2)}) collective-permute-start(f32[64,512]{1,0:T(8,128)S(1)} %raw_sum.5.refs_4_.refs_1_.refs_0_), channel_id=1, source_target_pairs={{0,6},{1,3},{2,4},{3,1},{4,2},{5,7},{6,0},{7,5},{8,14},{9,11},{10,... | collective-permute-start | bytes 393224 | tf_op jit(solution)/shard_map/ppermute | solution.py:395
  34.8 21.7 %collective-permute-start.8 = (bf16[128,5120]{1,0:T(8,128)(2,1)S(1)}, bf16[128,5120]{1,0:T(8,128)(2,1)S(1)}, u32[]{:S(2)}, u32[]{:S(2)}) collective-permute-start(bf16[128,5120]{1,0:T(8,128)(2,1)S(1)} %stack.7.refs_2_), channel_id=1, source_target_pairs={{0,1},{1,0},{2,3},{3,2},{4,5},{5,4},{6,7},{7,6},{8,9},{9,8},{10,11... | collective-permute-start | bytes 3932168 | tf_op jit(solution)/shard_map/ppermute | solution.py:395
  41.5 15.1 %collective-permute-start.11 = (bf16[128,5120]{1,0:T(8,128)(2,1)S(1)}, bf16[128,5120]{1,0:T(8,128)(2,1)S(1)}, u32[]{:S(2)}, u32[]{:S(2)}) collective-permute-start(bf16[128,5120]{1,0:T(8,128)(2,1)S(1)} %stack.8.refs_3_), channel_id=1, source_target_pairs={{0,1},{1,0},{2,3},{3,2},{4,5},{5,4},{6,7},{7,6},{8,9},{9,8},{10,11... | collective-permute-start | bytes 3932168 | tf_op jit(solution)/shard_map/ppermute | solution.py:395
  42.6 19.7 %collective-permute-start.14 = (bf16[128,5120]{1,0:T(8,128)(2,1)S(1)}, bf16[128,5120]{1,0:T(8,128)(2,1)S(1)}, u32[]{:S(2)}, u32[]{:S(2)}) collective-permute-start(bf16[128,5120]{1,0:T(8,128)(2,1)S(1)} %get-tuple-element.60.refs_3_), channel_id=1, source_target_pairs={{0,2},{1,7},{2,0},{3,5},{4,6},{5,3},{6,4},{7,1},{8,10},{9,15},{10,... | collective-permute-start | bytes 3932168 | tf_op jit(solution)/shard_map/ppermute | solution.py:395
  50.2 2.6 %collective-permute-start.13 = (bf16[4,64,640]{2,1,0:T(8,128)(2,1)S(1)}, bf16[4,64,640]{2,1,0:T(8,128)(2,1)S(1)}, u32[]{:S(2)}, u32[]{:S(2)}) collective-permute-start(bf16[4,64,640]{2,1,0:T(8,128)(2,1)S(1)} %get-tuple-element.64), channel_id=1, source_target_pairs={{0,1},{1,0},{2,3},{3,2},{4,5},{5,4},{6,7},{7,6},{8,9},{9,8},{10,11... | collective-permute-start | bytes 983048 | tf_op jit(solution)/shard_map/ppermute | solution.py:395
  52.9 9.3 %collective-permute-start.15 = (bf16[2,64,640]{2,1,0:T(8,128)(2,1)S(1)}, bf16[2,64,640]{2,1,0:T(8,128)(2,1)S(1)}, u32[]{:S(2)}, u32[]{:S(2)}) collective-permute-start(bf16[2,64,640]{2,1,0:T(8,128)(2,1)S(1)} %get-tuple-element.68), channel_id=1, source_target_pairs={{0,2},{1,7},{2,0},{3,5},{4,6},{5,3},{6,4},{7,1},{8,10},{9,15},{10,... | collective-permute-start | bytes 491528 | tf_op jit(solution)/shard_map/ppermute | solution.py:395
  54.1 5.6 %collective-permute-start.16 = (f32[32,64]{1,0:T(8,128)S(1)}, f32[32,64]{1,0:T(8,128)S(1)}, u32[]{:S(2)}, u32[]{:S(2)}) collective-permute-start(f32[32,64]{1,0:T(8,128)S(1)} %get-tuple-element.69.refs_8_), channel_id=1, source_target_pairs={{16,0},{32,16},{48,32},{64,48},{80,64},{96,80},{112,96},{17,1},{33... | collective-permute-start | bytes 24584 | tf_op jit(solution)/shard_map/ppermute | solution.py:419
  62.6 16.7 %collective-permute-start.20 = (bf16[64,5120]{1,0:T(8,128)(2,1)S(1)}, bf16[64,5120]{1,0:T(8,128)(2,1)S(1)}, u32[]{:S(2)}, u32[]{:S(2)}) collective-permute-start(bf16[64,5120]{1,0:T(8,128)(2,1)S(1)} %get-tuple-element.72.refs_6_), channel_id=1, source_target_pairs={{0,6},{1,3},{2,4},{3,1},{4,2},{5,7},{6,0},{7,5},{8,14},{9,11},{10,... | collective-permute-start | bytes 1966088 | tf_op jit(solution)/shard_map/ppermute | solution.py:395
  64.2 6.9 %collective-permute-start.17 = (bf16[2,64,640]{2,1,0:T(8,128)(2,1)S(1)}, bf16[2,64,640]{2,1,0:T(8,128)(2,1)S(1)}, u32[]{:S(2)}, u32[]{:S(2)}) collective-permute-start(bf16[2,64,640]{2,1,0:T(8,128)(2,1)S(1)} %get-tuple-element.76), channel_id=1, source_target_pairs={{0,8},{1,9},{2,10},{3,11},{4,12},{5,13},{6,14},{7,15},{8,0},{9,1},... | collective-permute-start | bytes 491528 | tf_op jit(solution)/shard_map/ppermute | solution.py:395
  71.1 5.7 %collective-permute-start.18 = (bf16[1,64,640]{2,1,0:T(8,128)(2,1)S(1)}, bf16[1,64,640]{2,1,0:T(8,128)(2,1)S(1)}, u32[]{:S(2)}, u32[]{:S(2)}) collective-permute-start(bf16[1,64,640]{2,1,0:T(8,128)(2,1)S(1)} %get-tuple-element.80), channel_id=1, source_target_pairs={{0,6},{1,3},{2,4},{3,1},{4,2},{5,7},{6,0},{7,5},{8,14},{9,11},{10,... | collective-permute-start | bytes 245768 | tf_op jit(solution)/shard_map/ppermute | solution.py:395
  76.9 6.3 %collective-permute-start.19 = (bf16[1,64,640]{2,1,0:T(8,128)(2,1)S(1)}, bf16[1,64,640]{2,1,0:T(8,128)(2,1)S(1)}, u32[]{:S(2)}, u32[]{:S(2)}) collective-permute-start(bf16[1,64,640]{2,1,0:T(8,128)(2,1)S(1)} %right_sum.7.refs_2_.refs_0_), channel_id=1, source_target_pairs={{16,0},{32,16},{48,32},{64,48},{80,64},{96,80},{112,96},{17,1},{33... | collective-permute-start | bytes 245768 | tf_op jit(solution)/shard_map/ppermute | solution.py:419
  83.2 6.6 %collective-permute-start.23 = (bf16[2,64,640]{2,1,0:T(8,128)(2,1)S(1)}, bf16[2,64,640]{2,1,0:T(8,128)(2,1)S(1)}, u32[]{:S(2)}, u32[]{:S(2)}) collective-permute-start(bf16[2,64,640]{2,1,0:T(8,128)(2,1)S(1)} %chunk_pair.1.refs_3_), channel_id=1, source_target_pairs={{0,6},{1,3},{2,4},{3,1},{4,2},{5,7},{6,0},{7,5},{8,14},{9,11},{10,... | collective-permute-start | bytes 491528 | tf_op jit(solution)/shard_map/ppermute | solution.py:395
  85.0 5.4 %collective-permute-start.22 = (bf16[2,64,640]{2,1,0:T(8,128)(2,1)S(1)}, bf16[2,64,640]{2,1,0:T(8,128)(2,1)S(1)}, u32[]{:S(2)}, u32[]{:S(2)}) collective-permute-start(bf16[2,64,640]{2,1,0:T(8,128)(2,1)S(1)} %chunk_pair.1.refs_3_), channel_id=1, source_target_pairs={{0,2},{1,7},{2,0},{3,5},{4,6},{5,3},{6,4},{7,1},{8,10},{9,15},{10,... | collective-permute-start | bytes 491528 | tf_op jit(solution)/shard_map/ppermute | solution.py:395
  85.0 8.1 %collective-permute-start.21 = (bf16[2,64,640]{2,1,0:T(8,128)(2,1)S(1)}, bf16[2,64,640]{2,1,0:T(8,128)(2,1)S(1)}, u32[]{:S(2)}, u32[]{:S(2)}) collective-permute-start(bf16[2,64,640]{2,1,0:T(8,128)(2,1)S(1)} %chunk_pair.1.refs_3_), channel_id=1, source_target_pairs={{0,4},{1,5},{2,6},{3,7},{4,0},{5,1},{6,2},{7,3},{8,12},{9,13},{10,... | collective-permute-start | bytes 491528 | tf_op jit(solution)/shard_map/ppermute | solution.py:395
  88.0 8.6 %collective-permute-start.28 = (bf16[32,5120]{1,0:T(8,128)(2,1)S(1)}, bf16[32,5120]{1,0:T(8,128)(2,1)S(1)}, u32[]{:S(2)}, u32[]{:S(2)}) collective-permute-start(bf16[32,5120]{1,0:T(8,128)(2,1)S(1)} %get-tuple-element.83.refs_2_), channel_id=1, source_target_pairs={{0,8},{1,9},{2,10},{3,11},{4,12},{5,13},{6,14},{7,15},{8,0},{9,1},... | collective-permute-start | bytes 983048 | tf_op jit(solution)/shard_map/ppermute | solution.py:395
  89.9 3.2 %collective-permute-start.27 = (bf16[2,64,640]{2,1,0:T(8,128)(2,1)S(1)}, bf16[2,64,640]{2,1,0:T(8,128)(2,1)S(1)}, u32[]{:S(2)}, u32[]{:S(2)}) collective-permute-start(bf16[2,64,640]{2,1,0:T(8,128)(2,1)S(1)} %chunk_pair.1.refs_3_), channel_id=1, source_target_pairs={{0,1},{1,0},{2,3},{3,2},{4,5},{5,4},{6,7},{7,6},{8,9},{9,8},{10,11... | collective-permute-start | bytes 491528 | tf_op jit(solution)/shard_map/ppermute | solution.py:395
  89.9 3.2 %collective-permute-start.26 = (bf16[2,64,640]{2,1,0:T(8,128)(2,1)S(1)}, bf16[2,64,640]{2,1,0:T(8,128)(2,1)S(1)}, u32[]{:S(2)}, u32[]{:S(2)}) collective-permute-start(bf16[2,64,640]{2,1,0:T(8,128)(2,1)S(1)} %collective-permute-done.23.refs_2_), channel_id=1, source_target_pairs={{0,1},{1,0},{2,3},{3,2},{4,5},{5,4},{6,7},{7,6},{8,9},{9,8},{10,11... | collective-permute-start | bytes 491528 | tf_op jit(solution)/shard_map/ppermute | solution.py:395
  90.4 2.7 %collective-permute-start.25 = (bf16[2,64,640]{2,1,0:T(8,128)(2,1)S(1)}, bf16[2,64,640]{2,1,0:T(8,128)(2,1)S(1)}, u32[]{:S(2)}, u32[]{:S(2)}) collective-permute-start(bf16[2,64,640]{2,1,0:T(8,128)(2,1)S(1)} %collective-permute-done.22.refs_1_), channel_id=1, source_target_pairs={{0,1},{1,0},{2,3},{3,2},{4,5},{5,4},{6,7},{7,6},{8,9},{9,8},{10,11... | collective-permute-start | bytes 491528 | tf_op jit(solution)/shard_map/ppermute | solution.py:395
  93.1 1.4 %collective-permute-start.24 = (bf16[2,64,640]{2,1,0:T(8,128)(2,1)S(1)}, bf16[2,64,640]{2,1,0:T(8,128)(2,1)S(1)}, u32[]{:S(2)}, u32[]{:S(2)}) collective-permute-start(bf16[2,64,640]{2,1,0:T(8,128)(2,1)S(1)} %collective-permute-done.21.refs_0_), channel_id=1, source_target_pairs={{0,1},{1,0},{2,3},{3,2},{4,5},{5,4},{6,7},{7,6},{8,9},{9,8},{10,11... | collective-permute-start | bytes 491528 | tf_op jit(solution)/shard_map/ppermute | solution.py:395

commit v5 on v4

--- a/solution.py
+++ b/solution.py
@@ -266,15 +266,16 @@
     )
 
 
-def factor_kernel(z, left_t, weight, resid, feedback, own_out, other_out):
+def factor_kernel(z, left, weight, resid, feedback, own_out, other_out):
     _, _, x, core = place()
-    l1, l2 = pieces(left_t[...], 2)
+    l1, l2 = pieces(left[...], 2)
+    own_left = jnp.concatenate([l1, l1, l2], axis=0)
     for step in range(STEPS):
         columns = slice(step * TILE, (step + 1) * TILE)
         both = nt(z[...], weight[columns, :])
         value = both[0:R] + both[R : 2 * R]
         r1, r2 = pieces(resid[:, columns].astype(F32) + feedback[:, columns], 2)
-        value = value + (nn(l1, r1) + (nn(l1, r2) + nn(l2, r1)))
+        value = value + tn(own_left, jnp.concatenate([r1, r2, r1], axis=0))
         c = step // 4
         apart = xor_x(step % 4, x)
         spot = jnp.where(apart == 0, 3, jnp.where(apart == 2, 0, jnp.where(apart == 1 + 2 * c, 1, 2)))
@@ -288,12 +289,12 @@
             other_out[spot] = value.astype(BF)
 
 
-def factor_call(z, left_t, weight, resid, feedback, deps):
+def factor_call(z, left, weight, resid, feedback, deps):
     return whole(
         factor_kernel,
         [shape(4, R, TILE), shape(4, R, TILE, dtype=BF)],
         "right_factor",
-        (z, left_t, weight, resid, feedback),
+        (z, left, weight, resid, feedback),
         deps,
     )
 
@@ -451,7 +452,7 @@
     grad_first = to_first(send)
     z, left, left_t = basis_call(raw, come, unit, (send,))
     left_next = to_previous(left)
-    own, other = factor_call(z, left_t, weight, resid, fb, ())
+    own, other = factor_call(z, left, weight, resid, fb, ())
 
     come = to_core(other)
     send, kept = right_step(own, come, ())

time: 98.4 us -> 98.4 us (level)
  no operation moved by 1% of the time
where the time goes in v5:
time: 98.4 us; the launch traced here: 98.2 us
  Pallas kernels  33.7 us (34%)
  starting transfers between devices  33.7 us (34%)
  waiting for transfers between devices  28.7 us (29%)
  local copies, waits for them, and re-layouts  1.04 us (1%)
  between operations  1.02 us (1%)
    ppermute x27, starting transfers between devices, sent(): return lax.ppermute(value, 'fsdp', pairs)  28.8 us
    ppermute x27, waiting for transfers between devices, sent(): return lax.ppermute(value, 'fsdp', pairs)  24.4 us
    pallas_call x20, Pallas kernels, whole(): pl.pallas_call(body, in_specs=(in_specs or [VMEM] * count) + [ANY] * len(...  13.1 us
    pallas_call x4, Pallas kernels, grad_call(): pl.pallas_call(kernel, in_specs=[VMEM] * (ins + 1) + [ANY] * count, out_s...  10.4 us
    pallas_call x4, Pallas kernels, partial_call(): pl.pallas_call(kernel, grid=(2,), in_specs=[VMEM, VMEM] + [ANY] * count,...  8.61 us
    ppermute x2, starting transfers between devices, to_previous(): return lax.ppermute(value, 'section', [(s, s - 1) for s in range(1, 8)])  4.84 us
    ppermute x2, waiting for transfers between devices, to_previous(): return lax.ppermute(value, 'section', [(s, s - 1) for s in range(1, 8)])  4.36 us
  transfers between devices with their start and end apart: 29, of which 13 were waited for; matrix products, arithmetic and copies ran while one was open for 0% of the time, Pallas kernels for 32%

profile of v5, /device:TPU:96, one launch (start us, length us, event | category | flops | bytes accessed | tf_op | source)
XLA Modules:
  0.0 98.2 jit_solution(457344496213310544)
XLA Ops:
  0.6 0.0 copy-start.3
  0.6 1.0 copy-done.3
  1.7 3.3 %collective-permute-start.2 = (bf16[32,5120]{1,0:T(8,128)(2,1)S(1)}, bf16[32,5120]{1,0:T(8,128)(2,1)S(1)}, u32[]{:S(2)}, u32[]{:S(2)}) collective-permute-start(bf16[32,5120]{1,0:T(8,128)(2,1)S(1)} %copied.1), channel_id=1, source_target_pairs={{0,8},{1,9},{2,10},{3,11},{4,12},{5,13},{6,14},{7,15},{8,0},{9,1},... | collective-permute-start | bytes 983048 | tf_op jit(solution)/shard_map/ppermute | solution.py:396
  4.9 2.8 %collective-permute-start.1 = (bf16[32,5120]{1,0:T(8,128)(2,1)S(1)}, bf16[32,5120]{1,0:T(8,128)(2,1)S(1)}, u32[]{:S(2)}, u32[]{:S(2)}) collective-permute-start(bf16[32,5120]{1,0:T(8,128)(2,1)S(1)} %copied.1), channel_id=1, source_target_pairs={{0,6},{1,3},{2,4},{3,1},{4,2},{5,7},{6,0},{7,5},{8,14},{9,11},{10,... | collective-permute-start | bytes 983048 | tf_op jit(solution)/shard_map/ppermute | solution.py:396
  7.7 0.2 collective-permute-start
  8.0 3.9 %unit_and_raw.1 = (bf16[512,896]{1,0:T(8,128)(2,1)S(1)}, bf16[512,896]{1,0:T(8,128)(2,1)S(1)}, f32[64,512]{1,0:T(8,128)S(1)}) custom-call(bf16[512,896]{1,0:T(8,128)(2,1)S(1)} %bitcast.27, bf16[512,896]{1,0:T(8,128)(2,1)S(1)} %bitcast.28, bf16[5120,896]{1,0:T(8,128)(2,1)S(1)} %bitcast.12, f32[64,5120]{1,0:T(8,128)S(1)} %bitcast.26, ...), custom_call_target="tpu_custom_call" | custom-call | flops 20000000000 | bytes 1000 | tf_op jit(solution)/shard_map/unit_and_raw/pallas_call | solution.py:105
  11.9 0.1 collective-permute-start.3
  12.0 2.2 %input_grad_part.4 = (bf16[256,5120]{1,0:T(8,128)(2,1)S(1)}, f32[256,5120]{1,0:T(8,128)S(1)}, f32[8,128]{1,0:T(8,128)S(1)}) custom-call(bf16[512,896]{1,0:T(8,128)(2,1)S(1)} %get-tuple-element.45.unit.refs_4_, bf16[5120,896]{1,0:T(8,128)(2,1)S(1)} %bitcast.13, f32[64,512]{1,0:T(8,128)S(1)} %get-tuple-element.44.refs_0_), custom_call_target="tpu_custom_call" | custom-call | flops 1000 | bytes 1000 | tf_op jit(solution)/shard_map/input_grad_part/pallas_call | solution.py:143
  14.2 2.4 %collective-permute-done.1.refs_4_.refs_2_ = bf16[32,5120]{1,0:T(8,128)(2,1)S(1)} collective-permute-done((bf16[32,5120]{1,0:T(8,128)(2,1)S(1)}, bf16[32,5120]{1,0:T(8,128)(2,1)S(1)}, u32[]{:S(2)}, u32[]{:S(2)}) %collective-permute-start.1) | collective-permute-done | bytes 327712 | tf_op jit(solution)/shard_map/ppermute | solution.py:396
  16.6 0.0 collective-permute-done.2.refs_0_
  16.6 2.2 %collective-permute-start.4 = (bf16[64,5120]{1,0:T(8,128)(2,1)S(1)}, bf16[64,5120]{1,0:T(8,128)(2,1)S(1)}, u32[]{:S(2)}, u32[]{:S(2)}) collective-permute-start(bf16[64,5120]{1,0:T(8,128)(2,1)S(1)} %stack.5), channel_id=1, source_target_pairs={{0,6},{1,3},{2,4},{3,1},{4,2},{5,7},{6,0},{7,5},{8,14},{9,11},{10,... | collective-permute-start | bytes 1966088 | tf_op jit(solution)/shard_map/ppermute | solution.py:396
  18.8 0.1 collective-permute-start.7
  18.9 0.5 collective-permute-start.5
  19.4 2.1 %input_grad_part.5 = (bf16[256,5120]{1,0:T(8,128)(2,1)S(1)}, f32[256,5120]{1,0:T(8,128)S(1)}, f32[8,128]{1,0:T(8,128)S(1)}) custom-call(bf16[512,896]{1,0:T(8,128)(2,1)S(1)} %get-tuple-element.45.unit.refs_4_, bf16[5120,896]{1,0:T(8,128)(2,1)S(1)} %bitcast.14, ...), custom_call_target="tpu_custom_call", output_to_operand_aliasing={{0}: (2, {}), {1}: (3, {})} | custom-call | flops 1000 | bytes 1000 | tf_op jit(solution)/shard_map/input_grad_part/pallas_call | solution.py:143
  21.5 3.9 %collective-permute-done.5.refs_1_ = f32[64,512]{1,0:T(8,128)S(1)} collective-permute-done((f32[64,512]{1,0:T(8,128)S(1)}, f32[64,512]{1,0:T(8,128)S(1)}, u32[]{:S(2)}, u32[]{:S(2)}) %collective-permute-start.5) | collective-permute-done | bytes 131104 | tf_op jit(solution)/shard_map/ppermute | solution.py:396
  25.5 2.0 %collective-permute-start.6 = (f32[64,512]{1,0:T(8,128)S(1)}, f32[64,512]{1,0:T(8,128)S(1)}, u32[]{:S(2)}, u32[]{:S(2)}) collective-permute-start(f32[64,512]{1,0:T(8,128)S(1)} %raw_sum.4.refs_2_.refs_0_), channel_id=1, source_target_pairs={{0,2},{1,7},{2,0},{3,5},{4,6},{5,3},{6,4},{7,1},{8,10},{9,15},{10,... | collective-permute-start | bytes 393224 | tf_op jit(solution)/shard_map/ppermute | solution.py:396
  27.5 2.1 %input_grad_part.6 = (bf16[256,5120]{1,0:T(8,128)(2,1)S(1)}, f32[256,5120]{1,0:T(8,128)S(1)}, f32[8,128]{1,0:T(8,128)S(1)}) custom-call(bf16[512,896]{1,0:T(8,128)(2,1)S(1)} %get-tuple-element.45.unit.refs_4_, bf16[5120,896]{1,0:T(8,128)(2,1)S(1)} %bitcast.15, ...), custom_call_target="tpu_custom_call", output_to_operand_aliasing={{0}: (2, {}), {1}: (3, {})} | custom-call | flops 1000 | bytes 1000 | tf_op jit(solution)/shard_map/input_grad_part/pallas_call | solution.py:143
  29.7 2.2 %input_grad_part.7 = (bf16[256,5120]{1,0:T(8,128)(2,1)S(1)}, f32[256,5120]{1,0:T(8,128)S(1)}, f32[8,128]{1,0:T(8,128)S(1)}) custom-call(bf16[512,896]{1,0:T(8,128)(2,1)S(1)} %get-tuple-element.45.unit.refs_4_, bf16[5120,896]{1,0:T(8,128)(2,1)S(1)} %bitcast.16, ...), custom_call_target="tpu_custom_call", output_to_operand_aliasing={{0}: (2, {}), {1}: (3, {})} | custom-call | flops 1000 | bytes 1000 | tf_op jit(solution)/shard_map/input_grad_part/pallas_call | solution.py:143
  31.8 0.0 collective-permute-done.6.refs_1_
  31.8 0.0 collective-permute-done.7.refs_3_.refs_1_
  31.8 0.6 collective-permute-done.4.refs_4_
  32.5 0.0 copy-start.4
  32.5 0.2 stack.9
  32.7 0.1 collective-permute-start.12
  32.8 0.1 collective-permute-start.9
  32.9 1.8 %collective-permute-start.10 = (f32[64,512]{1,0:T(8,128)S(1)}, f32[64,512]{1,0:T(8,128)S(1)}, u32[]{:S(2)}, u32[]{:S(2)}) collective-permute-start(f32[64,512]{1,0:T(8,128)S(1)} %raw_sum.5.refs_4_.refs_1_.refs_0_), channel_id=1, source_target_pairs={{0,6},{1,3},{2,4},{3,1},{4,2},{5,7},{6,0},{7,5},{8,14},{9,11},{10,... | collective-permute-start | bytes 393224 | tf_op jit(solution)/shard_map/ppermute | solution.py:396
  34.7 0.1 stack.7.refs_2_
  34.8 0.1 collective-permute-start.8
  34.9 5.6 %collective-permute-done.10.refs_4_.refs_2_.refs_1_ = f32[64,512]{1,0:T(8,128)S(1)} collective-permute-done((f32[64,512]{1,0:T(8,128)S(1)}, f32[64,512]{1,0:T(8,128)S(1)}, u32[]{:S(2)}, u32[]{:S(2)}) %collective-permute-start.10) | collective-permute-done | bytes 131104 | tf_op jit(solution)/shard_map/ppermute | solution.py:396
  40.5 0.9 collective-permute-done.9.refs_3_
  41.4 0.1 stack.8.refs_3_
  41.5 0.7 collective-permute-start.11
  42.1 0.4 input_grad_sum.3
  42.6 0.3 collective-permute-start.14
  42.8 3.2 %left_factor.1 = (bf16[128,896]{1,0:T(8,128)(2,1)S(1)}, f32[32,64]{1,0:T(8,128)S(1)}, f32[64,32]{1,0:T(8,128)}) custom-call(f32[64,512]{1,0:T(8,128)S(1)} %raw_sum.5.refs_4_.refs_1_.refs_0_, f32[64,512]{1,0:T(8,128)S(1)} %collective-permute-done.10.refs_4_.refs_2_.refs_1_, bf16[512,896]{1,0:T(8,128)(2,1)S(1)} %get-tuple-element.56.refs_2_, ...), custom_call_target="tpu_custom_call" | custom-call | flops 1000 | bytes 1000 | tf_op jit(solution)/shard_map/left_factor/pallas_call | solution.py:105
  46.1 4.5 %right_factor.1 = (f32[4,64,640]{2,1,0:T(8,128)S(1)}, bf16[4,64,640]{2,1,0:T(8,128)(2,1)S(1)}) custom-call(bf16[128,896]{1,0:T(8,128)(2,1)S(1)} %get-tuple-element.60.refs_0_, f32[32,64]{1,0:T(8,128)S(1)} %get-tuple-element.61.refs_1_.refs_8_, bf16[5120,896]{1,0:T(8,128)(2,1)S(1)} %bitcast.17, bf16[32,5120]{1,0:T(8,128)(2,1)S(1)} %bitcast.22, ...), custom_call_target="tpu_custom_call" | custom-call | flops 1000 | bytes 1000 | tf_op jit(solution)/shard_map/right_factor/pallas_call | solution.py:105
  50.6 1.3 %collective-permute-start.13 = (bf16[4,64,640]{2,1,0:T(8,128)(2,1)S(1)}, bf16[4,64,640]{2,1,0:T(8,128)(2,1)S(1)}, u32[]{:S(2)}, u32[]{:S(2)}) collective-permute-start(bf16[4,64,640]{2,1,0:T(8,128)(2,1)S(1)} %get-tuple-element.63), channel_id=1, source_target_pairs={{0,1},{1,0},{2,3},{3,2},{4,5},{5,4},{6,7},{7,6},{8,9},{9,8},{10,11... | collective-permute-start | bytes 983048 | tf_op jit(solution)/shard_map/ppermute | solution.py:396
  51.9 1.3 %collective-permute-done.13.refs_1_ = bf16[4,64,640]{2,1,0:T(8,128)(2,1)S(1)} collective-permute-done((bf16[4,64,640]{2,1,0:T(8,128)(2,1)S(1)}, bf16[4,64,640]{2,1,0:T(8,128)(2,1)S(1)}, u32[]{:S(2)}, u32[]{:S(2)}) %collective-permute-start.13) | collective-permute-done | bytes 327712 | tf_op jit(solution)/shard_map/ppermute | solution.py:396
  53.2 0.1 right_sum.4
  53.2 1.2 %collective-permute-start.15 = (bf16[2,64,640]{2,1,0:T(8,128)(2,1)S(1)}, bf16[2,64,640]{2,1,0:T(8,128)(2,1)S(1)}, u32[]{:S(2)}, u32[]{:S(2)}) collective-permute-start(bf16[2,64,640]{2,1,0:T(8,128)(2,1)S(1)} %get-tuple-element.67), channel_id=1, source_target_pairs={{0,2},{1,7},{2,0},{3,5},{4,6},{5,3},{6,4},{7,1},{8,10},{9,15},{10,... | collective-permute-start | bytes 491528 | tf_op jit(solution)/shard_map/ppermute | solution.py:396
  54.4 2.4 %collective-permute-start.16 = (f32[32,64]{1,0:T(8,128)S(1)}, f32[32,64]{1,0:T(8,128)S(1)}, u32[]{:S(2)}, u32[]{:S(2)}) collective-permute-start(f32[32,64]{1,0:T(8,128)S(1)} %get-tuple-element.61.refs_1_.refs_8_), channel_id=1, source_target_pairs={{16,0},{32,16},{48,32},{64,48},{80,64},{96,80},{112,96},{17,1},{33... | collective-permute-start | bytes 24584 | tf_op jit(solution)/shard_map/ppermute | solution.py:420
  56.9 2.6 %weight_grad_part.4 = (bf16[5120,896]{1,0:T(8,128)(2,1)}, f32[8,128]{1,0:T(8,128)S(1)}) custom-call(bf16[128,5120]{1,0:T(8,128)(2,1)S(1)} %collective-permute-done.8.refs_0_, bf16[128,5120]{1,0:T(8,128)(2,1)S(1)} %collective-permute-done.11.refs_1_, bf16[128,5120]{1,0:T(8,128)(2,1)S(1)} %stack.7.refs_2_, bf16[128,5120]{1,0:T(8,128)(2,1)S(1)} %stack.8.refs_3_, ...), custom_call_target="tpu_custom_call" | custom-call | flops 1000 | bytes 1000 | tf_op jit(solution)/shard_map/weight_grad_part/pallas_call | solution.py:346
  59.5 0.6 collective-permute-done.16.refs_2_.refs_9_
  60.1 2.1 %collective-permute-done.15.refs_1_ = bf16[2,64,640]{2,1,0:T(8,128)(2,1)S(1)} collective-permute-done((bf16[2,64,640]{2,1,0:T(8,128)(2,1)S(1)}, bf16[2,64,640]{2,1,0:T(8,128)(2,1)S(1)}, u32[]{:S(2)}, u32[]{:S(2)}) %collective-permute-start.15) | collective-permute-done | bytes 163872 | tf_op jit(solution)/shard_map/ppermute | solution.py:396
  62.2 0.3 input_grad_sum.4
  62.6 1.6 %collective-permute-start.20 = (bf16[64,5120]{1,0:T(8,128)(2,1)S(1)}, bf16[64,5120]{1,0:T(8,128)(2,1)S(1)}, u32[]{:S(2)}, u32[]{:S(2)}) collective-permute-start(bf16[64,5120]{1,0:T(8,128)(2,1)S(1)} %get-tuple-element.70.refs_6_), channel_id=1, source_target_pairs={{0,6},{1,3},{2,4},{3,1},{4,2},{5,7},{6,0},{7,5},{8,14},{9,11},{10,... | collective-permute-start | bytes 1966088 | tf_op jit(solution)/shard_map/ppermute | solution.py:396
  64.2 1.7 %collective-permute-start.17 = (bf16[2,64,640]{2,1,0:T(8,128)(2,1)S(1)}, bf16[2,64,640]{2,1,0:T(8,128)(2,1)S(1)}, u32[]{:S(2)}, u32[]{:S(2)}) collective-permute-start(bf16[2,64,640]{2,1,0:T(8,128)(2,1)S(1)} %get-tuple-element.74), channel_id=1, source_target_pairs={{0,8},{1,9},{2,10},{3,11},{4,12},{5,13},{6,14},{7,15},{8,0},{9,1},... | collective-permute-start | bytes 491528 | tf_op jit(solution)/shard_map/ppermute | solution.py:396
  65.9 2.6 %weight_grad_part.5 = (bf16[5120,896]{1,0:T(8,128)(2,1)}, f32[8,128]{1,0:T(8,128)S(1)}) custom-call(bf16[128,5120]{1,0:T(8,128)(2,1)S(1)} %collective-permute-done.8.refs_0_, bf16[128,5120]{1,0:T(8,128)(2,1)S(1)} %collective-permute-done.11.refs_1_, bf16[128,5120]{1,0:T(8,128)(2,1)S(1)} %stack.7.refs_2_, ...), custom_call_target="tpu_custom_call", output_to_operand_aliasing={{0}: (5, {})} | custom-call | flops 1000 | bytes 1000 | tf_op jit(solution)/shard_map/weight_grad_part/pallas_call | solution.py:346
  68.5 2.6 %weight_grad_part.6 = (bf16[5120,896]{1,0:T(8,128)(2,1)}, f32[8,128]{1,0:T(8,128)S(1)}) custom-call(bf16[128,5120]{1,0:T(8,128)(2,1)S(1)} %collective-permute-done.8.refs_0_, bf16[128,5120]{1,0:T(8,128)(2,1)S(1)} %collective-permute-done.11.refs_1_, bf16[128,5120]{1,0:T(8,128)(2,1)S(1)} %stack.7.refs_2_, ...), custom_call_target="tpu_custom_call", output_to_operand_aliasing={{0}: (5, {})} | custom-call | flops 1000 | bytes 1000 | tf_op jit(solution)/shard_map/weight_grad_part/pallas_call | solution.py:346
  71.1 1.7 %collective-permute-start.18 = (bf16[1,64,640]{2,1,0:T(8,128)(2,1)S(1)}, bf16[1,64,640]{2,1,0:T(8,128)(2,1)S(1)}, u32[]{:S(2)}, u32[]{:S(2)}) collective-permute-start(bf16[1,64,640]{2,1,0:T(8,128)(2,1)S(1)} %get-tuple-element.78), channel_id=1, source_target_pairs={{0,6},{1,3},{2,4},{3,1},{4,2},{5,7},{6,0},{7,5},{8,14},{9,11},{10,... | collective-permute-start | bytes 245768 | tf_op jit(solution)/shard_map/ppermute | solution.py:396
  72.8 2.6 %weight_grad_part.7 = (bf16[5120,896]{1,0:T(8,128)(2,1)}, f32[8,128]{1,0:T(8,128)S(1)}) custom-call(bf16[128,5120]{1,0:T(8,128)(2,1)S(1)} %collective-permute-done.8.refs_0_, bf16[128,5120]{1,0:T(8,128)(2,1)S(1)} %collective-permute-done.11.refs_1_, bf16[128,5120]{1,0:T(8,128)(2,1)S(1)} %stack.7.refs_2_, ...), custom_call_target="tpu_custom_call", output_to_operand_aliasing={{0}: (5, {})} | custom-call | flops 1000 | bytes 1000 | tf_op jit(solution)/shard_map/weight_grad_part/pallas_call | solution.py:346
  75.4 1.4 %collective-permute-done.18.refs_1_ = bf16[1,64,640]{2,1,0:T(8,128)(2,1)S(1)} collective-permute-done((bf16[1,64,640]{2,1,0:T(8,128)(2,1)S(1)}, bf16[1,64,640]{2,1,0:T(8,128)(2,1)S(1)}, u32[]{:S(2)}, u32[]{:S(2)}) %collective-permute-start.18) | collective-permute-done | bytes 81952 | tf_op jit(solution)/shard_map/ppermute | solution.py:396
  76.9 2.4 %collective-permute-start.19 = (bf16[1,64,640]{2,1,0:T(8,128)(2,1)S(1)}, bf16[1,64,640]{2,1,0:T(8,128)(2,1)S(1)}, u32[]{:S(2)}, u32[]{:S(2)}) collective-permute-start(bf16[1,64,640]{2,1,0:T(8,128)(2,1)S(1)} %right_sum.7.refs_2_.refs_0_), channel_id=1, source_target_pairs={{16,0},{32,16},{48,32},{64,48},{80,64},{96,80},{112,96},{17,1},{33... | collective-permute-start | bytes 245768 | tf_op jit(solution)/shard_map/ppermute | solution.py:420
  79.3 0.1 input_grad_sum.5
  79.4 3.8 %collective-permute-done.19.refs_1_ = bf16[1,64,640]{2,1,0:T(8,128)(2,1)S(1)} collective-permute-done((bf16[1,64,640]{2,1,0:T(8,128)(2,1)S(1)}, bf16[1,64,640]{2,1,0:T(8,128)(2,1)S(1)}, u32[]{:S(2)}, u32[]{:S(2)}) %collective-permute-start.19) | collective-permute-done | bytes 81952 | tf_op jit(solution)/shard_map/ppermute | solution.py:420
  83.2 1.7 %collective-permute-start.23 = (bf16[2,64,640]{2,1,0:T(8,128)(2,1)S(1)}, bf16[2,64,640]{2,1,0:T(8,128)(2,1)S(1)}, u32[]{:S(2)}, u32[]{:S(2)}) collective-permute-start(bf16[2,64,640]{2,1,0:T(8,128)(2,1)S(1)} %chunk_pair.1.refs_3_), channel_id=1, source_target_pairs={{0,6},{1,3},{2,4},{3,1},{4,2},{5,7},{6,0},{7,5},{8,14},{9,11},{10,... | collective-permute-start | bytes 491528 | tf_op jit(solution)/shard_map/ppermute | solution.py:396
  85.0 3.1 %collective-permute-start.21 = (bf16[2,64,640]{2,1,0:T(8,128)(2,1)S(1)}, bf16[2,64,640]{2,1,0:T(8,128)(2,1)S(1)}, u32[]{:S(2)}, u32[]{:S(2)}) collective-permute-start(bf16[2,64,640]{2,1,0:T(8,128)(2,1)S(1)} %chunk_pair.1.refs_3_), channel_id=1, source_target_pairs={{0,4},{1,5},{2,6},{3,7},{4,0},{5,1},{6,2},{7,3},{8,12},{9,13},{10,... | collective-permute-start | bytes 491528 | tf_op jit(solution)/shard_map/ppermute | solution.py:396
  88.0 1.9 %collective-permute-start.28 = (bf16[32,5120]{1,0:T(8,128)(2,1)S(1)}, bf16[32,5120]{1,0:T(8,128)(2,1)S(1)}, u32[]{:S(2)}, u32[]{:S(2)}) collective-permute-start(bf16[32,5120]{1,0:T(8,128)(2,1)S(1)} %get-tuple-element.81.refs_2_), channel_id=1, source_target_pairs={{0,8},{1,9},{2,10},{3,11},{4,12},{5,13},{6,14},{7,15},{8,0},{9,1},... | collective-permute-start | bytes 983048 | tf_op jit(solution)/shard_map/ppermute | solution.py:396
  89.9 0.5 collective-permute-start.26
  90.4 0.1 collective-permute-start.25
  90.5 2.6 %collective-permute-done.21.refs_0_ = bf16[2,64,640]{2,1,0:T(8,128)(2,1)S(1)} collective-permute-done((bf16[2,64,640]{2,1,0:T(8,128)(2,1)S(1)}, bf16[2,64,640]{2,1,0:T(8,128)(2,1)S(1)}, u32[]{:S(2)}, u32[]{:S(2)}) %collective-permute-start.21) | collective-permute-done | bytes 163872 | tf_op jit(solution)/shard_map/ppermute | solution.py:396
  93.1 1.4 %collective-permute-done.24.refs_4_ = bf16[2,64,640]{2,1,0:T(8,128)(2,1)S(1)} collective-permute-done((bf16[2,64,640]{2,1,0:T(8,128)(2,1)S(1)}, bf16[2,64,640]{2,1,0:T(8,128)(2,1)S(1)}, u32[]{:S(2)}, u32[]{:S(2)}) %collective-permute-start.24) | collective-permute-done | bytes 163872 | tf_op jit(solution)/shard_map/ppermute | solution.py:396
  94.5 2.1 %collective-permute-done.28.refs_13_ = bf16[32,5120]{1,0:T(8,128)(2,1)S(1)} collective-permute-done((bf16[32,5120]{1,0:T(8,128)(2,1)S(1)}, bf16[32,5120]{1,0:T(8,128)(2,1)S(1)}, u32[]{:S(2)}, u32[]{:S(2)}) %collective-permute-start.28) | collective-permute-done | bytes 327712 | tf_op jit(solution)/shard_map/ppermute | solution.py:396
  96.6 1.6 %feedback_and_received.1 = (f32[32,5120]{1,0:T(8,128)}, f32[32,5120]{1,0:T(8,128)}) custom-call(bf16[2,64,640]{2,1,0:T(8,128)(2,1)S(1)} %collective-permute-done.21.refs_0_, bf16[2,64,640]{2,1,0:T(8,128)(2,1)S(1)} %collective-permute-done.22.refs_1_, bf16[2,64,640]{2,1,0:T(8,128)(2,1)S(1)} %collective-permute-done.23.refs_2_, ...), custom_call_target="tpu_custom_call" | custom-call | flops 1000 | bytes 1000 | tf_op jit(solution)/shard_map/feedback_and_received/pallas_call | solution.py:380
  (40 shorter events, 0.4 us)
Async XLA Ops:
  0.6 1.0 copy-start.3
  1.6 6.3 %copy-start = (bf16[1,5120,896]{2,1,0:T(8,128)(2,1)S(1)}, bf16[1,5120,896]{2,1,0:T(8,128)(2,1)}, u32[]{:S(2)}) copy-start(bf16[1,5120,896]{2,1,0:T(8,128)(2,1)} %param.10) | copy-start | bytes 27525124
  1.6 6.3 %copy-start.1 = (f32[1,32,5120]{2,1,0:T(8,128)S(1)}, f32[1,32,5120]{2,1,0:T(8,128)}, u32[]{:S(2)}) copy-start(f32[1,32,5120]{2,1,0:T(8,128)} %param.12) | copy-start | bytes 1966084
  1.6 6.3 %copy-start.2 = (bf16[1,32,5120]{2,1,0:T(8,128)(2,1)S(1)}, bf16[1,32,5120]{2,1,0:T(8,128)(2,1)}, u32[]{:S(2)}) copy-start(bf16[1,32,5120]{2,1,0:T(8,128)(2,1)} %param.11) | copy-start | bytes 983044
  1.6 6.3 %copy-start.5 = (f32[1,5120,64]{1,2,0:T(8,128)S(1)}, f32[1,5120,64]{1,2,0:T(8,128)}, u32[]{:S(2)}) copy-start(f32[1,5120,64]{1,2,0:T(8,128)} %param.13) | copy-start | bytes 3932164
  1.6 6.3 %copy-start.6 = (bf16[1,512,896]{2,1,0:T(8,128)(2,1)S(1)}, bf16[1,512,896]{2,1,0:T(8,128)(2,1)}, u32[]{:S(2)}) copy-start(bf16[1,512,896]{2,1,0:T(8,128)(2,1)} %param.8) | copy-start | bytes 2752516
  1.6 6.3 %copy-start.7 = (bf16[1,512,896]{2,1,0:T(8,128)(2,1)S(1)}, bf16[1,512,896]{2,1,0:T(8,128)(2,1)}, u32[]{:S(2)}) copy-start(bf16[1,512,896]{2,1,0:T(8,128)(2,1)} %param.9) | copy-start | bytes 2752516
  1.7 14.9 %collective-permute-start.2 = (bf16[32,5120]{1,0:T(8,128)(2,1)S(1)}, bf16[32,5120]{1,0:T(8,128)(2,1)S(1)}, u32[]{:S(2)}, u32[]{:S(2)}) collective-permute-start(bf16[32,5120]{1,0:T(8,128)(2,1)S(1)} %copied.1), channel_id=1, source_target_pairs={{0,8},{1,9},{2,10},{3,11},{4,12},{5,13},{6,14},{7,15},{8,0},{9,1},... | collective-permute-start | bytes 983048 | tf_op jit(solution)/shard_map/ppermute | solution.py:396
  4.9 11.6 %collective-permute-start.1 = (bf16[32,5120]{1,0:T(8,128)(2,1)S(1)}, bf16[32,5120]{1,0:T(8,128)(2,1)S(1)}, u32[]{:S(2)}, u32[]{:S(2)}) collective-permute-start(bf16[32,5120]{1,0:T(8,128)(2,1)S(1)} %copied.1), channel_id=1, source_target_pairs={{0,6},{1,3},{2,4},{3,1},{4,2},{5,7},{6,0},{7,5},{8,14},{9,11},{10,... | collective-permute-start | bytes 983048 | tf_op jit(solution)/shard_map/ppermute | solution.py:396
  7.7 8.8 %collective-permute-start = (bf16[32,5120]{1,0:T(8,128)(2,1)S(1)}, bf16[32,5120]{1,0:T(8,128)(2,1)S(1)}, u32[]{:S(2)}, u32[]{:S(2)}) collective-permute-start(bf16[32,5120]{1,0:T(8,128)(2,1)S(1)} %copied.1), channel_id=1, source_target_pairs={{0,2},{1,7},{2,0},{3,5},{4,6},{5,3},{6,4},{7,1},{8,10},{9,15},{10,... | collective-permute-start | bytes 983048 | tf_op jit(solution)/shard_map/ppermute | solution.py:396
  11.9 2.3 %collective-permute-start.3 = (f32[64,512]{1,0:T(8,128)S(1)}, f32[64,512]{1,0:T(8,128)S(1)}, u32[]{:S(2)}, u32[]{:S(2)}) collective-permute-start(f32[64,512]{1,0:T(8,128)S(1)} %get-tuple-element.44.refs_0_), channel_id=1, source_target_pairs={{0,1},{1,0},{2,3},{3,2},{4,5},{5,4},{6,7},{7,6},{8,9},{9,8},{10,11... | collective-permute-start | bytes 393224 | tf_op jit(solution)/shard_map/ppermute | solution.py:396
  16.6 15.8 %collective-permute-start.4 = (bf16[64,5120]{1,0:T(8,128)(2,1)S(1)}, bf16[64,5120]{1,0:T(8,128)(2,1)S(1)}, u32[]{:S(2)}, u32[]{:S(2)}) collective-permute-start(bf16[64,5120]{1,0:T(8,128)(2,1)S(1)} %stack.5), channel_id=1, source_target_pairs={{0,6},{1,3},{2,4},{3,1},{4,2},{5,7},{6,0},{7,5},{8,14},{9,11},{10,... | collective-permute-start | bytes 1966088 | tf_op jit(solution)/shard_map/ppermute | solution.py:396
  18.8 13.0 %collective-permute-start.7 = (bf16[32,5120]{1,0:T(8,128)(2,1)S(1)}, bf16[32,5120]{1,0:T(8,128)(2,1)S(1)}, u32[]{:S(2)}, u32[]{:S(2)}) collective-permute-start(bf16[32,5120]{1,0:T(8,128)(2,1)S(1)} %stack.6), channel_id=1, source_target_pairs={{0,2},{1,7},{2,0},{3,5},{4,6},{5,3},{6,4},{7,1},{8,10},{9,15},{10,... | collective-permute-start | bytes 983048 | tf_op jit(solution)/shard_map/ppermute | solution.py:396
  18.9 6.6 %collective-permute-start.5 = (f32[64,512]{1,0:T(8,128)S(1)}, f32[64,512]{1,0:T(8,128)S(1)}, u32[]{:S(2)}, u32[]{:S(2)}) collective-permute-start(f32[64,512]{1,0:T(8,128)S(1)} %raw_sum.3.refs_2_.refs_0_.refs_1_), channel_id=1, source_target_pairs={{0,8},{1,9},{2,10},{3,11},{4,12},{5,13},{6,14},{7,15},{8,0},{9,1},... | collective-permute-start | bytes 393224 | tf_op jit(solution)/shard_map/ppermute | solution.py:396
  25.5 6.3 %collective-permute-start.6 = (f32[64,512]{1,0:T(8,128)S(1)}, f32[64,512]{1,0:T(8,128)S(1)}, u32[]{:S(2)}, u32[]{:S(2)}) collective-permute-start(f32[64,512]{1,0:T(8,128)S(1)} %raw_sum.4.refs_2_.refs_0_), channel_id=1, source_target_pairs={{0,2},{1,7},{2,0},{3,5},{4,6},{5,3},{6,4},{7,1},{8,10},{9,15},{10,... | collective-permute-start | bytes 393224 | tf_op jit(solution)/shard_map/ppermute | solution.py:396
  32.5 2.2 %copy-start.4 = (bf16[1,32,5120]{2,1,0:T(8,128)(2,1)S(1)}, bf16[1,32,5120]{2,1,0:T(8,128)(2,1)}, u32[]{:S(2)}) copy-start(bf16[1,32,5120]{2,1,0:T(8,128)(2,1)} %param.7) | copy-start | bytes 983044
  32.7 9.5 %collective-permute-start.12 = (bf16[256,5120]{1,0:T(8,128)(2,1)S(1)}, bf16[256,5120]{1,0:T(8,128)(2,1)S(1)}, u32[]{:S(2)}, u32[]{:S(2)}) collective-permute-start(bf16[256,5120]{1,0:T(8,128)(2,1)S(1)} %stack.9), channel_id=1, source_target_pairs={{0,1},{1,0},{2,3},{3,2},{4,5},{5,4},{6,7},{7,6},{8,9},{9,8},{10,11... | collective-permute-start | bytes 7864328 | tf_op jit(solution)/shard_map/ppermute | solution.py:396
  32.8 8.6 %collective-permute-start.9 = (bf16[32,5120]{1,0:T(8,128)(2,1)S(1)}, bf16[32,5120]{1,0:T(8,128)(2,1)S(1)}, u32[]{:S(2)}, u32[]{:S(2)}) collective-permute-start(bf16[32,5120]{1,0:T(8,128)(2,1)S(1)} %get-tuple-element.85.refs_2_), channel_id=1, source_target_pairs={{0,2},{1,7},{2,0},{3,5},{4,6},{5,3},{6,4},{7,1},{8,10},{9,15},{10,... | collective-permute-start | bytes 983048 | tf_op jit(solution)/shard_map/ppermute | solution.py:396
  32.9 7.6 %collective-permute-start.10 = (f32[64,512]{1,0:T(8,128)S(1)}, f32[64,512]{1,0:T(8,128)S(1)}, u32[]{:S(2)}, u32[]{:S(2)}) collective-permute-start(f32[64,512]{1,0:T(8,128)S(1)} %raw_sum.5.refs_4_.refs_1_.refs_0_), channel_id=1, source_target_pairs={{0,6},{1,3},{2,4},{3,1},{4,2},{5,7},{6,0},{7,5},{8,14},{9,11},{10,... | collective-permute-start | bytes 393224 | tf_op jit(solution)/shard_map/ppermute | solution.py:396
  34.8 22.0 %collective-permute-start.8 = (bf16[128,5120]{1,0:T(8,128)(2,1)S(1)}, bf16[128,5120]{1,0:T(8,128)(2,1)S(1)}, u32[]{:S(2)}, u32[]{:S(2)}) collective-permute-start(bf16[128,5120]{1,0:T(8,128)(2,1)S(1)} %stack.7.refs_2_), channel_id=1, source_target_pairs={{0,1},{1,0},{2,3},{3,2},{4,5},{5,4},{6,7},{7,6},{8,9},{9,8},{10,11... | collective-permute-start | bytes 3932168 | tf_op jit(solution)/shard_map/ppermute | solution.py:396
  41.5 15.4 %collective-permute-start.11 = (bf16[128,5120]{1,0:T(8,128)(2,1)S(1)}, bf16[128,5120]{1,0:T(8,128)(2,1)S(1)}, u32[]{:S(2)}, u32[]{:S(2)}) collective-permute-start(bf16[128,5120]{1,0:T(8,128)(2,1)S(1)} %stack.8.refs_3_), channel_id=1, source_target_pairs={{0,1},{1,0},{2,3},{3,2},{4,5},{5,4},{6,7},{7,6},{8,9},{9,8},{10,11... | collective-permute-start | bytes 3932168 | tf_op jit(solution)/shard_map/ppermute | solution.py:396
  42.6 19.7 %collective-permute-start.14 = (bf16[128,5120]{1,0:T(8,128)(2,1)S(1)}, bf16[128,5120]{1,0:T(8,128)(2,1)S(1)}, u32[]{:S(2)}, u32[]{:S(2)}) collective-permute-start(bf16[128,5120]{1,0:T(8,128)(2,1)S(1)} %get-tuple-element.59.refs_3_), channel_id=1, source_target_pairs={{0,2},{1,7},{2,0},{3,5},{4,6},{5,3},{6,4},{7,1},{8,10},{9,15},{10,... | collective-permute-start | bytes 3932168 | tf_op jit(solution)/shard_map/ppermute | solution.py:396
  50.6 2.6 %collective-permute-start.13 = (bf16[4,64,640]{2,1,0:T(8,128)(2,1)S(1)}, bf16[4,64,640]{2,1,0:T(8,128)(2,1)S(1)}, u32[]{:S(2)}, u32[]{:S(2)}) collective-permute-start(bf16[4,64,640]{2,1,0:T(8,128)(2,1)S(1)} %get-tuple-element.63), channel_id=1, source_target_pairs={{0,1},{1,0},{2,3},{3,2},{4,5},{5,4},{6,7},{7,6},{8,9},{9,8},{10,11... | collective-permute-start | bytes 983048 | tf_op jit(solution)/shard_map/ppermute | solution.py:396
  53.2 9.0 %collective-permute-start.15 = (bf16[2,64,640]{2,1,0:T(8,128)(2,1)S(1)}, bf16[2,64,640]{2,1,0:T(8,128)(2,1)S(1)}, u32[]{:S(2)}, u32[]{:S(2)}) collective-permute-start(bf16[2,64,640]{2,1,0:T(8,128)(2,1)S(1)} %get-tuple-element.67), channel_id=1, source_target_pairs={{0,2},{1,7},{2,0},{3,5},{4,6},{5,3},{6,4},{7,1},{8,10},{9,15},{10,... | collective-permute-start | bytes 491528 | tf_op jit(solution)/shard_map/ppermute | solution.py:396
  54.4 5.6 %collective-permute-start.16 = (f32[32,64]{1,0:T(8,128)S(1)}, f32[32,64]{1,0:T(8,128)S(1)}, u32[]{:S(2)}, u32[]{:S(2)}) collective-permute-start(f32[32,64]{1,0:T(8,128)S(1)} %get-tuple-element.61.refs_1_.refs_8_), channel_id=1, source_target_pairs={{16,0},{32,16},{48,32},{64,48},{80,64},{96,80},{112,96},{17,1},{33... | collective-permute-start | bytes 24584 | tf_op jit(solution)/shard_map/ppermute | solution.py:420
  62.6 16.7 %collective-permute-start.20 = (bf16[64,5120]{1,0:T(8,128)(2,1)S(1)}, bf16[64,5120]{1,0:T(8,128)(2,1)S(1)}, u32[]{:S(2)}, u32[]{:S(2)}) collective-permute-start(bf16[64,5120]{1,0:T(8,128)(2,1)S(1)} %get-tuple-element.70.refs_6_), channel_id=1, source_target_pairs={{0,6},{1,3},{2,4},{3,1},{4,2},{5,7},{6,0},{7,5},{8,14},{9,11},{10,... | collective-permute-start | bytes 1966088 | tf_op jit(solution)/shard_map/ppermute | solution.py:396
  64.2 6.9 %collective-permute-start.17 = (bf16[2,64,640]{2,1,0:T(8,128)(2,1)S(1)}, bf16[2,64,640]{2,1,0:T(8,128)(2,1)S(1)}, u32[]{:S(2)}, u32[]{:S(2)}) collective-permute-start(bf16[2,64,640]{2,1,0:T(8,128)(2,1)S(1)} %get-tuple-element.74), channel_id=1, source_target_pairs={{0,8},{1,9},{2,10},{3,11},{4,12},{5,13},{6,14},{7,15},{8,0},{9,1},... | collective-permute-start | bytes 491528 | tf_op jit(solution)/shard_map/ppermute | solution.py:396
  71.1 5.7 %collective-permute-start.18 = (bf16[1,64,640]{2,1,0:T(8,128)(2,1)S(1)}, bf16[1,64,640]{2,1,0:T(8,128)(2,1)S(1)}, u32[]{:S(2)}, u32[]{:S(2)}) collective-permute-start(bf16[1,64,640]{2,1,0:T(8,128)(2,1)S(1)} %get-tuple-element.78), channel_id=1, source_target_pairs={{0,6},{1,3},{2,4},{3,1},{4,2},{5,7},{6,0},{7,5},{8,14},{9,11},{10,... | collective-permute-start | bytes 245768 | tf_op jit(solution)/shard_map/ppermute | solution.py:396
  76.9 6.3 %collective-permute-start.19 = (bf16[1,64,640]{2,1,0:T(8,128)(2,1)S(1)}, bf16[1,64,640]{2,1,0:T(8,128)(2,1)S(1)}, u32[]{:S(2)}, u32[]{:S(2)}) collective-permute-start(bf16[1,64,640]{2,1,0:T(8,128)(2,1)S(1)} %right_sum.7.refs_2_.refs_0_), channel_id=1, source_target_pairs={{16,0},{32,16},{48,32},{64,48},{80,64},{96,80},{112,96},{17,1},{33... | collective-permute-start | bytes 245768 | tf_op jit(solution)/shard_map/ppermute | solution.py:420
  83.2 6.6 %collective-permute-start.23 = (bf16[2,64,640]{2,1,0:T(8,128)(2,1)S(1)}, bf16[2,64,640]{2,1,0:T(8,128)(2,1)S(1)}, u32[]{:S(2)}, u32[]{:S(2)}) collective-permute-start(bf16[2,64,640]{2,1,0:T(8,128)(2,1)S(1)} %chunk_pair.1.refs_3_), channel_id=1, source_target_pairs={{0,6},{1,3},{2,4},{3,1},{4,2},{5,7},{6,0},{7,5},{8,14},{9,11},{10,... | collective-permute-start | bytes 491528 | tf_op jit(solution)/shard_map/ppermute | solution.py:396
  85.0 5.4 %collective-permute-start.22 = (bf16[2,64,640]{2,1,0:T(8,128)(2,1)S(1)}, bf16[2,64,640]{2,1,0:T(8,128)(2,1)S(1)}, u32[]{:S(2)}, u32[]{:S(2)}) collective-permute-start(bf16[2,64,640]{2,1,0:T(8,128)(2,1)S(1)} %chunk_pair.1.refs_3_), channel_id=1, source_target_pairs={{0,2},{1,7},{2,0},{3,5},{4,6},{5,3},{6,4},{7,1},{8,10},{9,15},{10,... | collective-permute-start | bytes 491528 | tf_op jit(solution)/shard_map/ppermute | solution.py:396
  85.0 8.1 %collective-permute-start.21 = (bf16[2,64,640]{2,1,0:T(8,128)(2,1)S(1)}, bf16[2,64,640]{2,1,0:T(8,128)(2,1)S(1)}, u32[]{:S(2)}, u32[]{:S(2)}) collective-permute-start(bf16[2,64,640]{2,1,0:T(8,128)(2,1)S(1)} %chunk_pair.1.refs_3_), channel_id=1, source_target_pairs={{0,4},{1,5},{2,6},{3,7},{4,0},{5,1},{6,2},{7,3},{8,12},{9,13},{10,... | collective-permute-start | bytes 491528 | tf_op jit(solution)/shard_map/ppermute | solution.py:396
  88.0 8.6 %collective-permute-start.28 = (bf16[32,5120]{1,0:T(8,128)(2,1)S(1)}, bf16[32,5120]{1,0:T(8,128)(2,1)S(1)}, u32[]{:S(2)}, u32[]{:S(2)}) collective-permute-start(bf16[32,5120]{1,0:T(8,128)(2,1)S(1)} %get-tuple-element.81.refs_2_), channel_id=1, source_target_pairs={{0,8},{1,9},{2,10},{3,11},{4,12},{5,13},{6,14},{7,15},{8,0},{9,1},... | collective-permute-start | bytes 983048 | tf_op jit(solution)/shard_map/ppermute | solution.py:396
  89.9 3.2 %collective-permute-start.27 = (bf16[2,64,640]{2,1,0:T(8,128)(2,1)S(1)}, bf16[2,64,640]{2,1,0:T(8,128)(2,1)S(1)}, u32[]{:S(2)}, u32[]{:S(2)}) collective-permute-start(bf16[2,64,640]{2,1,0:T(8,128)(2,1)S(1)} %chunk_pair.1.refs_3_), channel_id=1, source_target_pairs={{0,1},{1,0},{2,3},{3,2},{4,5},{5,4},{6,7},{7,6},{8,9},{9,8},{10,11... | collective-permute-start | bytes 491528 | tf_op jit(solution)/shard_map/ppermute | solution.py:396
  89.9 3.2 %collective-permute-start.26 = (bf16[2,64,640]{2,1,0:T(8,128)(2,1)S(1)}, bf16[2,64,640]{2,1,0:T(8,128)(2,1)S(1)}, u32[]{:S(2)}, u32[]{:S(2)}) collective-permute-start(bf16[2,64,640]{2,1,0:T(8,128)(2,1)S(1)} %collective-permute-done.23.refs_2_), channel_id=1, source_target_pairs={{0,1},{1,0},{2,3},{3,2},{4,5},{5,4},{6,7},{7,6},{8,9},{9,8},{10,11... | collective-permute-start | bytes 491528 | tf_op jit(solution)/shard_map/ppermute | solution.py:396
  90.4 2.7 %collective-permute-start.25 = (bf16[2,64,640]{2,1,0:T(8,128)(2,1)S(1)}, bf16[2,64,640]{2,1,0:T(8,128)(2,1)S(1)}, u32[]{:S(2)}, u32[]{:S(2)}) collective-permute-start(bf16[2,64,640]{2,1,0:T(8,128)(2,1)S(1)} %collective-permute-done.22.refs_1_), channel_id=1, source_target_pairs={{0,1},{1,0},{2,3},{3,2},{4,5},{5,4},{6,7},{7,6},{8,9},{9,8},{10,11... | collective-permute-start | bytes 491528 | tf_op jit(solution)/shard_map/ppermute | solution.py:396
  93.1 1.4 %collective-permute-start.24 = (bf16[2,64,640]{2,1,0:T(8,128)(2,1)S(1)}, bf16[2,64,640]{2,1,0:T(8,128)(2,1)S(1)}, u32[]{:S(2)}, u32[]{:S(2)}) collective-permute-start(bf16[2,64,640]{2,1,0:T(8,128)(2,1)S(1)} %collective-permute-done.21.refs_0_), channel_id=1, source_target_pairs={{0,1},{1,0},{2,3},{3,2},{4,5},{5,4},{6,7},{7,6},{8,9},{9,8},{10,11... | collective-permute-start | bytes 491528 | tf_op jit(solution)/shard_map/ppermute | solution.py:396
